TPU v7x, 128 devices: a whole 4x4x4 slice. The times are simulated.
128 devices in a mesh: blocks: 32 (over x, y, core), slab: 4 (over z).
Axes of the slice: x: 4, y: 4, z: 4, core: 2. Of those that a mesh axis runs over, the one named last changes fastest.
Arguments:
- populations: float32 [19, 4, 32, 4096], P(None, 'slab', 'blocks'), may hold values from -6 to 6
- w_in: bfloat16 [512, 19], replicated, may hold values from -1.25 to 1.25
- w_mid: bfloat16 [1, 512, 512], replicated, may hold values from -0.25 to 0.25
- w_out: bfloat16 [19, 512], replicated, may hold values from -0.25 to 0.25
- cotangent: float32 [19, 4, 32, 4096], P(None, 'slab', 'blocks'), may hold values from -6 to 6
- face_source: int32 [32, 4], replicated, may hold values from 0 to 31, as said below
- face_level: int32 [4, 32, 6], P('slab', 'blocks'), may hold values 0 or 1
- face_quadrant: int32 [4, 32, 6], P('slab', 'blocks'), may hold values from 0 to 3
Outputs:
- final: float32 [19, 4, 32, 4096], P(None, 'slab', 'blocks')
- grad_pops: float32 [19, 4, 32, 4096], P(None, 'slab', 'blocks')
- grad_in: float32 [512, 19], replicated
- grad_mid: float32 [1, 512, 512], replicated
- grad_out: float32 [19, 512], replicated
Inputs may be any that keep to these rules, and one draw needn't show every extreme that they name: face_source is symmetric: face_source[face_source[b, f], f xor 1] = b. The +y and -y neighbours of block b are the same block, b xor 1. Every neighbour's index differs from the block's by at most 3 modulo 32, never by 0, and that distance is reached.
All inputs are finite; a program needn't handle non-finite values. No bound on the sum of `face_level` on one device may be relied on, other than what follows from the above.
Results may differ from a plain program's by a relative error of at most 0.0088.
Values sent between devices are 32-bit elements; how exact they have to be, the bound alone decides.
No kernel may reach another device: no remote copies, remote signals or barrier semaphores. Data moves between devices by JAX's collectives and lax.ppermute only.
A program may use at most 128 MiB of HBM per device.

v0:
```python
from functools import partial

import jax
import jax.numpy as jnp
from jax import lax
from jax.experimental import pallas as pl
from jax.experimental.pallas import tpu as pltpu
from jax.sharding import PartitionSpec as P

Q = 19
HID = 512
CELLS = 4096
ROWS = 32
CHUNK = 1024
TILES = CHUNK // 128
STEPS_GRID = CELLS // CHUNK
NB = 32
NZ = 4
AXES = ("blocks", "slab")
F32 = jnp.float32
BF16 = jnp.bfloat16
PIECE = 72
GROWS = 32 * PIECE
OUT_AT = 4 * HID
IN_AT = OUT_AT + 4 * 24

VELOCITIES = [
    (0, 0, 0),
    (1, 0, 0),
    (-1, 0, 0),
    (0, 1, 0),
    (0, -1, 0),
    (0, 0, 1),
    (0, 0, -1),
    (1, 1, 0),
    (-1, -1, 0),
    (1, -1, 0),
    (-1, 1, 0),
    (1, 0, 1),
    (-1, 0, -1),
    (1, 0, -1),
    (-1, 0, 1),
    (0, 1, 1),
    (0, -1, -1),
    (0, 1, -1),
    (0, -1, 1),
]
OPPOSITE = [0, 2, 1, 4, 3, 6, 5, 8, 7, 10, 9, 12, 11, 14, 13, 16, 15, 18, 17]


def members(face):
    sign = 1 if face % 2 == 0 else -1
    return [q for q in range(Q) if VELOCITIES[q][face // 2] == sign]


def iota(rows, dim):
    return lax.broadcasted_iota(jnp.int32, (rows, 128), dim)


def roll(value, shift, axis):
    shift %= value.shape[axis]
    return value if shift == 0 else pltpu.roll(value, shift, axis)


def shifted(v, velocity):
    cx, cy, cz = velocity
    lane = iota(ROWS, 1)
    if cz:
        v = jnp.where(lane & 15 == (0 if cz == 1 else 15), roll(v, -15 * cz, 1), roll(v, cz, 1))
    if cy:
        t = roll(v, 16 * cy, 1)
        swapped = jnp.where(iota(ROWS, 0) & 1 == 1, roll(t, 1, 0), roll(t, -1, 0))
        v = jnp.where(lane >> 4 == (0 if cy == 1 else 7), swapped, t)
    if cx:
        v = roll(v, 2 * cx, 0)
    return v


def corner(q):
    row, lane = iota(ROWS, 0), iota(ROWS, 1)
    coords = [row >> 1, (row & 1) * 8 + (lane >> 4), lane & 15]
    mask = None
    for axis in range(3):
        c = VELOCITIES[q][axis]
        if c:
            here = coords[axis] == (0 if c == 1 else 15)
            mask = here if mask is None else mask & here
    return mask


def is_edge(q):
    return sum(abs(c) for c in VELOCITIES[q]) == 2


def pack_faces(src, put_x, put_y, put_z):
    lane16, lane32 = iota(16, 1), iota(ROWS, 1)
    for f in (0, 1):
        for i, q in enumerate(members(f)):
            for r in (0, 1):
                put_x(f, r, i, src[q, pl.ds((30 if f == 0 else 0) + r, 1), :])
    for f in (2, 3):
        acc = jnp.zeros((16, 128), F32)
        for i, q in enumerate(members(f)):
            v = src[q, pl.ds(1 if f == 2 else 0, 16, stride=2), :]
            v = roll(v, 16 * i - (112 if f == 2 else 0), 1)
            acc = jnp.where(lane16 >> 4 == i, v, acc)
        put_y(f - 2, acc)
    acc = jnp.zeros((ROWS, 128), F32)
    for f in (4, 5):
        for i, q in enumerate(members(f)):
            slot = i if f == 4 else 8 + i
            v = roll(src[q], slot - (15 if f == 4 else 0), 1)
            acc = jnp.where(lane32 & 15 == slot, v, acc)
    put_z(acc)


def unpack_faces(dst, get_x, y_ref, z, add):
    lane16, lane32 = iota(16, 1), iota(ROWS, 1)
    for f in (0, 1):
        for i, q in enumerate(members(f)):
            for r in (0, 1):
                at = pl.ds((30 if f == 0 else 0) + r, 1)
                v = get_x(f, r, i)
                dst[q, at, :] = dst[q, at, :] + v if add else v
    for f in (2, 3):
        packed = y_ref[f - 2]
        for i, q in enumerate(members(f)):
            at = pl.ds(1 if f == 2 else 0, 16, stride=2)
            v = roll(packed, (112 if f == 2 else 0) - 16 * i, 1)
            old = dst[q, at, :]
            new = old + v if add else v
            dst[q, at, :] = jnp.where(lane16 >> 4 == (7 if f == 2 else 0), new, old)
    for f in (4, 5):
        for i, q in enumerate(members(f)):
            v = roll(z, 15 - i if f == 4 else -(8 + i), 1)
            old = dst[q]
            new = old + v if add else v
            dst[q] = jnp.where(lane32 & 15 == (15 if f == 4 else 0), new, old)


def picked(value, index):
    return jnp.take_along_axis(value, index, axis=1)


def level_of(info, f):
    return info[0, 2 + (f ^ 1)] == 1


def quadrant_of(info, f):
    r = info[0, 8 + (f ^ 1)]
    return r >> 1, r & 1


def refine_x(info, x):
    lane = iota(8, 1)
    for f in (0, 1):
        fine = level_of(info, f)
        qr, qc = quadrant_of(info, f)
        rows = [x[f, 0], x[f, 1]]
        source = jnp.where(qr == 0, rows[0], rows[1])
        for r in (0, 1):
            index = (r * 4 + (lane >> 5)) * 16 + qc * 8 + ((lane & 15) >> 1)
            x[f, r] = jnp.where(fine, picked(source, index), rows[r])


def refine_y(info, y):
    lane = iota(8, 1)
    for f in (2, 3):
        fine = level_of(info, f)
        qr, qc = quadrant_of(info, f)
        whole = y[f - 2]
        source = jnp.where(qr == 0, whole[:8], whole[8:])
        v = picked(source, (lane >> 4) * 16 + qc * 8 + ((lane & 15) >> 1))
        for d in (0, 1):
            at = pl.ds(d, 8, stride=2)
            y[f - 2, at, :] = jnp.where(fine, v, y[f - 2, at, :])


def refine_z(info, z_two):
    lane = iota(8, 1)
    for f in (4, 5):
        z = z_two.at[f - 4]
        fine = level_of(info, f)
        qr, qc = quadrant_of(info, f)
        parts = {(h, p): z[pl.ds(16 * h + p, 8, stride=2), :] for h in (0, 1) for p in (0, 1)}
        halves = [jnp.where(qc == 0, parts[h, 0], parts[h, 1]) for h in (0, 1)]
        source = jnp.where(qr == 0, halves[0], halves[1])
        for p in (0, 1):
            v = picked(source, (p * 4 + (lane >> 5)) * 16 + (lane & 15))
            for d in (0, 1):
                at = pl.ds(2 * d + p, 8, stride=4)
                z[at, :] = jnp.where(fine, v, z[at, :])
    return jnp.where(iota(ROWS, 1) & 15 < 8, z_two[0], z_two[1])


def gather_x(info, x):
    lane = iota(8, 1)
    index = (2 * ((lane >> 4) & 3)) * 16 + 2 * (lane & 7)
    for f in (0, 1):
        fine = level_of(info, f)
        qr, qc = quadrant_of(info, f)
        rows = [x[f, 0], x[f, 1]]
        sums = []
        for v in rows:
            v = v + roll(v, -1, 1)
            v = v + roll(v, -16, 1)
            sums.append(picked(v, index))
        v = jnp.where(lane < 64, sums[0], sums[1])
        v = jnp.where((lane & 15) >> 3 == qc, v, 0.0)
        for r in (0, 1):
            x[f, r] = jnp.where(fine, jnp.where(qr == r, v, 0.0), rows[r])


def gather_y(info, y):
    lane = iota(8, 1)
    index = (lane >> 4) * 16 + 2 * (lane & 7)
    for f in (2, 3):
        fine = level_of(info, f)
        qr, qc = quadrant_of(info, f)
        v = y[f - 2, pl.ds(0, 8, stride=2), :] + y[f - 2, pl.ds(1, 8, stride=2), :]
        v = picked(v + roll(v, -1, 1), index)
        v = jnp.where((lane & 15) >> 3 == qc, v, 0.0)
        for h in (0, 1):
            at = pl.ds(8 * h, 8)
            y[f - 2, at, :] = jnp.where(fine, jnp.where(qr == h, v, 0.0), y[f - 2, at, :])


def gather_z(info, z_two):
    lane = iota(8, 1)
    index = (2 * ((lane >> 4) & 3)) * 16 + (lane & 15)
    for f in (4, 5):
        z = z_two.at[f - 4]
        fine = level_of(info, f)
        qr, qc = quadrant_of(info, f)
        sums = []
        for p in (0, 1):
            v = z[pl.ds(p, 8, stride=4), :] + z[pl.ds(2 + p, 8, stride=4), :]
            sums.append(picked(v + roll(v, -16, 1), index))
        v = jnp.where(lane < 64, sums[0], sums[1])
        for h in (0, 1):
            for p in (0, 1):
                at = pl.ds(16 * h + p, 8, stride=2)
                here = (qr == h) & (qc == p)
                z[at, :] = jnp.where(fine, jnp.where(here, v, 0.0), z[at, :])
    return jnp.where(iota(ROWS, 1) & 15 < 8, z_two[0], z_two[1])


def choose_x(info, face, pieces, kind):
    d = info[0, face]
    even = info[0, 14] == 0
    outer1, outer3 = jnp.where(even, NB - 1, 1), jnp.where(even, NB - 3, 3)
    inner1, inner3 = jnp.where(even, 1, NB - 1), jnp.where(even, 3, NB - 3)
    spots = [inner1, outer1, NB - 2, 2, inner3, outer3]
    return lambda f, r: sum_where(
        [(d == spot, piece[kind * 4 + f * 2 + r]) for spot, piece in zip(spots, pieces)]
    )


def sum_where(cases):
    total = jnp.zeros((8, 128), F32)
    for condition, value in cases:
        total = jnp.where(condition, value, total)
    return total


def stream_back(info, bar, local, xs, xys, zs, work, y_two, z_two):
    for q in range(Q):
        v = bar[q]
        if is_edge(q):
            v = jnp.where(corner(q), 0.0, v)
        work[q] = shifted(v, tuple(-c for c in VELOCITIES[q]))
    x_four = xs.at[1]
    x_four[...] = jnp.zeros(x_four.shape, F32)

    def put_x(f, r, i, v):
        x_four[f, r, pl.ds(i, 1), :] = v

    def put_y(f, v):
        y_two[f] = v

    def put_z(v):
        z_two[0] = v
        z_two[1] = v

    pack_faces(work, put_x, put_y, put_z)
    gather_x(info, x_four)
    gather_y(info, y_two)
    zs[1] = gather_z(info, z_two)
    xys[pl.ds(32, 32), :] = xs[1].reshape(32, 128)
    xys[pl.ds(96, 32), :] = y_two[...].reshape(32, 128)
    row, lane = iota(ROWS, 0), iota(ROWS, 1)
    coords = [row >> 1, (row & 1) * 8 + (lane >> 4), lane & 15]
    for q in range(Q):
        v = work[q]
        leaving = None
        for axis in range(3):
            c = VELOCITIES[q][axis]
            if c:
                here = coords[axis] == (15 if c == 1 else 0)
                leaving = here if leaving is None else leaving | here
        if leaving is not None:
            v = jnp.where(leaving, 0.0, v)
        if is_edge(q):
            v = v + jnp.where(corner(OPPOSITE[q]), bar[OPPOSITE[q]], 0.0)
        local[q] = v


def send_post(post, xs, xys, zs):
    x_four = xs.at[0]
    x_four[...] = jnp.zeros(x_four.shape, F32)

    def put_x(f, r, i, v):
        x_four[f, r, pl.ds(i, 1), :] = v

    def put_y(f, v):
        xys[pl.ds(64 + 16 * f, 16), :] = v

    def put_z(v):
        zs[0] = v

    pack_faces(post, put_x, put_y, put_z)
    xys[pl.ds(0, 32), :] = xs[0].reshape(32, 128)


def stream(info, post, pieces, both, below, above, out, work, x_four, y_two, z_two):
    heads = [both.at[pl.ds(0, 64)]] + list(pieces)
    for f in (0, 1):
        pick = choose_x(info, f ^ 1, [Rows(h) for h in heads], 0)
        for r in (0, 1):
            x_four[f, r] = pick(f, r)
    refine_x(info, x_four)
    y_two[0] = both[pl.ds(64, 16), :]
    y_two[1] = both[pl.ds(80, 16), :]
    refine_y(info, y_two)
    z_two[0] = below[0]
    z_two[1] = above[0]
    z = refine_z(info, z_two)
    work[...] = post[...]
    unpack_faces(work, lambda f, r, i: x_four[f, r, pl.ds(i, 1), :], y_two, z, False)
    for q in range(Q):
        v = shifted(work[q], VELOCITIES[q])
        if is_edge(q):
            v = jnp.where(corner(q), post[OPPOSITE[q]], v)
        out[q] = v


class Rows:
    def __init__(self, ref):
        self.ref = ref

    def __getitem__(self, i):
        return self.ref[pl.ds(8 * i, 8), :]


def take_back(info, bar, pieces, both, below, above, x_four, y_two):
    heads = [both.at[pl.ds(0, 64)]] + list(pieces)
    for f in (0, 1):
        pick = choose_x(info, f, [Rows(h) for h in heads], 1)
        for r in (0, 1):
            x_four[f, r] = pick(f, r)
    y_two[0] = both[pl.ds(96, 16), :]
    y_two[1] = both[pl.ds(112, 16), :]
    z = jnp.where(iota(ROWS, 1) & 15 < 8, above[1], below[1])
    unpack_faces(bar, lambda f, r, i: x_four[f, r, pl.ds(i, 1), :], y_two, z, True)


def dot(a, b, ca=1, cb=0):
    return lax.dot_general(a, b, (((ca,), (cb,)), ((), ())), preferred_element_type=F32)


def cells_of(ref, step):
    parts = [
        ref[:, pl.ds(step * TILES + j, 1), :].reshape(Q, 128) for j in range(TILES)
    ]
    return jnp.concatenate(parts, axis=1)


def put_cells(ref, step, value):
    for j in range(TILES):
        ref[:, pl.ds(step * TILES + j, 1), :] = value[:, j * 128 : (j + 1) * 128].reshape(Q, 1, 128)


def forward(x, w_in_t, w_mid, w_out):
    xb = x.astype(BF16)
    h0 = jnp.tanh(dot(w_in_t, xb, 0, 0)).astype(BF16)
    h1 = jnp.tanh(dot(w_mid, h0)).astype(BF16)
    return xb, h0, h1, x + dot(w_out, h1)


def slope(h):
    h = h.astype(F32)
    return 1.0 - h * h


def backward(pbar, xb, h0, h1, w_in_t, w_mid_t, w_out):
    e = pbar.astype(BF16)
    g_out = dot(e, h1, 1, 1)
    a1 = (dot(w_out, e, 0, 0) * slope(h1)).astype(BF16)
    g_mid = dot(a1, h0, 1, 1)
    a0 = (dot(w_mid_t, a1) * slope(h0)).astype(BF16)
    g_in = dot(xb, a0, 1, 1)
    return pbar + dot(w_in_t, a0), g_in, g_mid, g_out


def add_grads(grads, g_in, g_mid, g_out, first):
    def put(at, rows, value):
        for j in range(4):
            spot = pl.ds(at + j * (HID if rows == HID else 24), rows)
            v = value[:, j * 128 : (j + 1) * 128]
            grads[spot, :] = v if first is None else grads[spot, :] + v

    put(0, HID, g_mid)
    put(OUT_AT, Q, g_out)
    put(IN_AT, Q, g_in)


def first_kernel(info, f0, cot, w_in_t, w_mid, w_out, post, local, xs, xys, zs, h0_out, h1_out,
                 work, y_two, z_two):
    step = pl.program_id(0)

    @pl.when(step == 0)
    def _():
        stream_back(info, cot, local, xs, xys, zs, work, y_two, z_two)

    xb, h0, h1, out = forward(cells_of(f0, step), w_in_t[...], w_mid[...], w_out[...])
    h0_out[...] = h0
    h1_out[...] = h1
    put_cells(post, step, out)

    @pl.when(step == STEPS_GRID - 1)
    def _():
        send_post(post, xs, xys, zs)


def second_kernel(info, post1, local2, p1, p2, p3, p4, p5, both, below, above, w_in_t, w_mid,
                  w_mid_t, w_out, post, local, xs, xys, zs, grads,
                  f1, pbar, fbar, work, x_four, y_two, z_two):
    step = pl.program_id(0)
    pieces = [p1, p2, p3, p4, p5]

    @pl.when(step == 0)
    def _():
        stream(info, post1, pieces, both, below, above, f1, work, x_four, y_two, z_two)
        pbar[...] = local2[...]
        take_back(info, pbar, pieces, both, below, above, x_four, y_two)
        grads[...] = jnp.zeros(grads.shape, F32)

    xb, h0, h1, out = forward(cells_of(f1, step), w_in_t[...], w_mid[...], w_out[...])
    put_cells(post, step, out)
    bar, g_in, g_mid, g_out = backward(
        cells_of(pbar, step), xb, h0, h1, w_in_t[...], w_mid_t[...], w_out[...]
    )
    put_cells(fbar, step, bar)
    add_grads(grads, g_in, g_mid, g_out, False)

    @pl.when(step == STEPS_GRID - 1)
    def _():
        send_post(post, xs, xys, zs)
        stream_back(info, fbar, local, xs, xys, zs, work, y_two, z_two)


def third_kernel(info, f0, local1, p1, p2, p3, p4, p5, both, below, above, w_in_t, w_mid_t, w_out,
                 grads2, h0_in, h1_in, fbar, grads, pbar, x_four, y_two):
    step = pl.program_id(0)

    @pl.when(step == 0)
    def _():
        pbar[...] = local1[...]
        take_back(info, pbar, [p1, p2, p3, p4, p5], both, below, above, x_four, y_two)
        grads[...] = grads2[...]

    bar, g_in, g_mid, g_out = backward(
        cells_of(pbar, step), cells_of(f0, step).astype(BF16), h0_in[...], h1_in[...],
        w_in_t[...], w_mid_t[...], w_out[...],
    )
    put_cells(fbar, step, bar)
    add_grads(grads, g_in, g_mid, g_out, False)


def final_kernel(info, post2, p1, p2, p3, p4, p5, both, below, above, out, work, x_four, y_two,
                 z_two):
    stream(info, post2, [p1, p2, p3, p4, p5], both, below, above, out, work, x_four, y_two, z_two)


def unpack_kernel(whole, g_in, g_mid, g_out):
    scale = float(NB * NZ * CELLS) ** -0.5
    for j in range(4):
        cols = pl.ds(j * 128, 128)
        g_mid[:, cols] = whole[pl.ds(j * HID, HID), :] * scale
        g_out[:, cols] = whole[pl.ds(OUT_AT + 24 * j, Q), :] * scale
        g_in[:, cols] = whole[pl.ds(IN_AT + 24 * j, Q), :] * scale


def vmem(shape, dtype=F32):
    return pltpu.VMEM(shape, dtype)


BLOCK = (Q, ROWS, 128)
SENDS = [
    jax.ShapeDtypeStruct((2, 2, 2, 8, 128), F32),
    jax.ShapeDtypeStruct((128, 128), F32),
    jax.ShapeDtypeStruct((2, ROWS, 128), F32),
]


def run(kernel, args, outs, scratch, grid=None, windows=(), flops=0, out_windows=()):
    spec_kw = dict(memory_space=pltpu.VMEM)

    def spec(shape, windowed):
        if grid is None:
            return pl.BlockSpec(memory_space=pltpu.VMEM)
        if windowed:
            return pl.BlockSpec((shape[0], CHUNK), lambda c: (0, c))
        zeros = (0,) * len(shape)
        return pl.BlockSpec(shape, lambda c: zeros)

    in_specs = [pl.BlockSpec(memory_space=pltpu.SMEM)] if args[0].dtype == jnp.int32 else [
        spec(args[0].shape, False)
    ]
    in_specs += [spec(a.shape, i + 1 in windows) for i, a in enumerate(args[1:])]
    out_specs = [spec(o.shape, i in out_windows) for i, o in enumerate(outs)]
    kw = {} if grid is None else {"grid": grid}
    return pl.pallas_call(
        kernel,
        out_shape=outs,
        in_specs=in_specs,
        out_specs=out_specs,
        scratch_shapes=scratch,
        compiler_params=pltpu.CompilerParams(vmem_limit_bytes=48 * 1024 * 1024),
        cost_estimate=pl.CostEstimate(flops=flops, bytes_accessed=1 << 20, transcendentals=0),
        **kw,
    )(*args)


def send(value, target):
    pairs = [
        (b * NZ + z, nb * NZ + nz)
        for b in range(NB)
        for z in range(NZ)
        for nb, nz in [target(b, z)]
    ]
    return lax.ppermute(value, AXES, pairs)


def exchange(xs, xys, zs):
    x = xs.reshape(64, 128)

    def to(even, odd):
        return lambda b, z: ((b + (even if b % 2 == 0 else odd)) % NB, z)

    both = send(xys, to(1, -1))
    pieces = [
        send(x, to(-1, 1)),
        send(x, to(2, 2)),
        send(x, to(-2, -2)),
        send(x, to(3, -3)),
        send(x, to(-3, 3)),
    ]
    below = send(zs, lambda b, z: (b, (z + 1) % NZ))
    above = send(zs, lambda b, z: (b, (z - 1) % NZ))
    return (*pieces, both, below, above)


def along(axes, d):
    def target(b, z):
        coords = {"x": b // 8, "y": b // 2 % 4, "c": b % 2, "z": z}
        axis = axes[coords["c"]]
        coords[axis] = (coords[axis] + d) % 4
        return coords["x"] * 8 + coords["y"] * 2 + coords["c"], coords["z"]

    return target


ORDER = [("z", "x"), ("y", "y"), ("x", "z")]


def total_over_devices(grads):
    b, z = lax.axis_index("blocks"), lax.axis_index("slab")
    core = b % 2
    coords = {"x": b // 8, "y": b // 2 % 4, "z": z}
    places = [jnp.where(core == 0, coords[a0], coords[a1]) for a0, a1 in ORDER]

    def take(parts, i):
        return lax.dynamic_index_in_dim(parts, i, 0, keepdims=False)

    swap = lambda b, z: (b ^ 1, z)
    halves = grads.reshape(2, GROWS // 2, 128)
    part = take(halves, core) + send(take(halves, 1 - core), swap)
    for level in (0, 1):
        i = places[level]
        quarters = part.reshape(4, -1, 128)
        got = [
            send(take(quarters, (i + d) % 4), along(ORDER[level], d)) for d in (1, 2, 3)
        ]
        part = take(quarters, i) + got[0] + got[1] + got[2]
    got = [send(part, along(ORDER[2], d)) for d in (1, 2, 3)]
    part = part + got[0] + got[1] + got[2]
    for level in (1, 0):
        i = places[level]
        got = [part] + [send(part, along(ORDER[level], d)) for d in (1, 2, 3)]
        stacked = jnp.stack(got)
        order = (i - jnp.arange(4)) % 4
        part = jnp.concatenate([take(stacked, order[k]) for k in range(4)])
    other = send(part, swap)
    first = jnp.where(core == 0, part, other)
    last = jnp.where(core == 0, other, part)
    return jnp.concatenate([first, last])


def shards(populations, w_in, w_mid, w_out, cotangent, face_source, face_level, face_quadrant):
    f0 = populations.reshape(BLOCK)
    cot = cotangent.reshape(BLOCK)
    w_in_t = w_in.T
    w_mid = w_mid[0]
    w_mid_t = w_mid.T
    position = lax.axis_index("blocks")
    near = lax.dynamic_index_in_dim(face_source, position, 0, keepdims=False)[:2]
    distance = (near - position + NB) % NB
    info = jnp.concatenate(
        [distance, face_level[0, 0], face_quadrant[0, 0], jnp.stack([position % 2, position])]
    )[None]
    block = jax.ShapeDtypeStruct(BLOCK, F32)
    hidden = jax.ShapeDtypeStruct((HID, CELLS), BF16)
    grad = jax.ShapeDtypeStruct((GROWS, 128), F32)
    big = 2 * HID * HID * CELLS
    faces = [vmem((2, 2, 8, 128)), vmem((2, 16, 128)), vmem((2, ROWS, 128))]
    grid = (STEPS_GRID,)

    post1, local2, *sends, h0, h1 = run(
        first_kernel, [info, f0, cot, w_in_t, w_mid, w_out], [block, block, *SENDS, hidden, hidden],
        [vmem(BLOCK), *faces[1:]], grid, (), big, (5, 6),
    )
    got = exchange(*sends)
    post2, local1, *sends, grads2 = run(
        second_kernel, [info, post1, local2, *got, w_in_t, w_mid, w_mid_t, w_out],
        [block, block, *SENDS, grad], [vmem(BLOCK)] * 4 + faces, grid, (), 3 * big,
    )
    got = exchange(*sends)
    fbar0, grads = run(
        third_kernel,
        [info, f0, local1, *got, w_in_t, w_mid_t, w_out, grads2, h0, h1],
        [block, grad], [vmem(BLOCK), *faces[:2]], grid, (15, 16), 2 * big,
    )
    post2, grads = lax.optimization_barrier((post2, grads))
    (final,) = run(final_kernel, [info, post2, *got], [block], [vmem(BLOCK), *faces], None, (), 1 << 20)
    whole = total_over_devices(grads)
    g_in, g_mid, g_out = run(
        unpack_kernel, [whole],
        [jax.ShapeDtypeStruct(s, F32) for s in ((Q, HID), (HID, HID), (Q, HID))], [],
    )
    place = (Q, 1, 1, CELLS)
    return final.reshape(place), fbar0.reshape(place), g_in.T, g_mid[None], g_out


def solution(mesh):
    cells = P(None, "slab", "blocks", None)
    local = P("slab", "blocks", None)
    return jax.shard_map(
        shards,
        mesh=mesh,
        in_specs=(cells, P(), P(), P(), cells, P(), local, local),
        out_specs=(cells, cells, P(), P(), P()),
        check_vma=False,
    )
```

profile of v0, /device:TPU:1, one launch (start us, length us, event | category | flops | bytes accessed | tf_op | source)
XLA Modules:
  0.0 134.8 jit_solution(11061112761000522020)
XLA Ops:
  2.3 1.0 copy-done.1
  6.7 7.4 %shard_map.119 = (f32[19,32,128]{2,1,0:T(8,128)S(1)}, f32[19,32,128]{2,1,0:T(8,128)S(1)}, f32[2,2,2,8,128]{4,3,2,1,0:T(8,128)S(1)}, f32[128,128]{1,0:T(8,128)S(1...) custom-call(s32[1,16]{1,0:T(1,128)S(1)} %bitcast.88, ...), custom_call_target="tpu_custom_call" | custom-call | flops 2147483648 | bytes 1048576 | tf_op jit(solution)/shard_map/pallas_call | solution.py:523
  14.2 2.0 %copy-done.10 = bf16[512,4096]{1,0:T(8,128)(2,1)} copy-done((bf16[512,4096]{1,0:T(8,128)(2,1)}, bf16[512,4096]{1,0:T(8,128)(2,1)S(1)}, u32[]{:S(2)}) %copy-start.10) | copy-done | bytes 4194328
  16.2 2.7 %collective-permute-start = (f32[64,128]{1,0:T(8,128)S(1)}, f32[64,128]{1,0:T(8,128)S(1)}, u32[]{:S(2)}, u32[]{:S(2)}) collective-permute-start(f32[64,128]{1,0:T(8,128)S(1)} %bitcast.100), channel_id=1, source_target_pairs={{0,124},{1,125},{2,126},{3,127},{4,8},{5,9},{6,10},{7,11},{8,4},{9... | collective-permute-start | bytes 98312 | tf_op jit(solution)/shard_map/ppermute | solution.py:542
  18.8 1.3 collective-permute-start.1
  20.1 3.5 %collective-permute-start.2 = (f32[64,128]{1,0:T(8,128)S(1)}, f32[64,128]{1,0:T(8,128)S(1)}, u32[]{:S(2)}, u32[]{:S(2)}) collective-permute-start(f32[64,128]{1,0:T(8,128)S(1)} %bitcast.102), channel_id=1, source_target_pairs={{0,120},{1,121},{2,122},{3,123},{4,124},{5,125},{6,126},{7,127},{8... | collective-permute-start | bytes 98312 | tf_op jit(solution)/shard_map/ppermute | solution.py:542
  23.6 4.0 %collective-permute-start.5 = (f32[128,128]{1,0:T(8,128)S(1)}, f32[128,128]{1,0:T(8,128)S(1)}, u32[]{:S(2)}, u32[]{:S(2)}) collective-permute-start(f32[128,128]{1,0:T(8,128)S(1)} %get-tuple-element.28), channel_id=1, source_target_pairs={{0,4},{1,5},{2,6},{3,7},{4,0},{5,1},{6,2},{7,3},{8,12},{9,13},{10,... | collective-permute-start | bytes 196616 | tf_op jit(solution)/shard_map/ppermute | solution.py:542
  27.7 1.7 %collective-permute-start.6 = (f32[2,32,128]{2,1,0:T(8,128)S(1)}, f32[2,32,128]{2,1,0:T(8,128)S(1)}, u32[]{:S(2)}, u32[]{:S(2)}) collective-permute-start(f32[2,32,128]{2,1,0:T(8,128)S(1)} %get-tuple-element.29), channel_id=1, source_target_pairs={{0,1},{1,2},{2,3},{3,0},{4,5},{5,6},{6,7},{7,4},{8,9},{9,10},{10,1... | collective-permute-start | bytes 98312 | tf_op jit(solution)/shard_map/ppermute | solution.py:542
  29.4 2.2 %collective-permute-start.7 = (f32[2,32,128]{2,1,0:T(8,128)S(1)}, f32[2,32,128]{2,1,0:T(8,128)S(1)}, u32[]{:S(2)}, u32[]{:S(2)}) collective-permute-start(f32[2,32,128]{2,1,0:T(8,128)S(1)} %get-tuple-element.29), channel_id=1, source_target_pairs={{0,3},{1,0},{2,1},{3,2},{4,7},{5,4},{6,5},{7,6},{8,11},{9,8},{10,9... | collective-permute-start | bytes 98312 | tf_op jit(solution)/shard_map/ppermute | solution.py:542
  31.8 2.5 %collective-permute-done.3.p4 = f32[64,128]{1,0:T(8,128)S(1)} collective-permute-done((f32[64,128]{1,0:T(8,128)S(1)}, f32[64,128]{1,0:T(8,128)S(1)}, u32[]{:S(2)}, u32[]{:S(2)}) %collective-permute-start.3) | collective-permute-done | bytes 32800 | tf_op jit(solution)/shard_map/ppermute | solution.py:542
  34.4 15.1 %shard_map.120 = (f32[19,32,128]{2,1,0:T(8,128)S(1)}, f32[19,32,128]{2,1,0:T(8,128)S(1)}, f32[2,2,2,8,128]{4,3,2,1,0:T(8,128)S(1)}, f32[128,128]{1,0:T(8,128)S(1...) custom-call(s32[1,16]{1,0:T(1,128)S(1)} %bitcast.89, f32[19,32,128]{2,1,0:T(8,128)S(1)} %get-tuple-element.25.post1, ...), custom_call_target="tpu_custom_call" | custom-call | flops 6442450944 | bytes 1048576 | tf_op jit(solution)/shard_map/pallas_call | solution.py:523
  51.6 1.1 collective-permute-start.9
  52.7 3.7 %collective-permute-start.10 = (f32[64,128]{1,0:T(8,128)S(1)}, f32[64,128]{1,0:T(8,128)S(1)}, u32[]{:S(2)}, u32[]{:S(2)}) collective-permute-start(f32[64,128]{1,0:T(8,128)S(1)} %bitcast.97), channel_id=1, source_target_pairs={{0,120},{1,121},{2,122},{3,123},{4,124},{5,125},{6,126},{7,127},{8... | collective-permute-start | bytes 98312 | tf_op jit(solution)/shard_map/ppermute | solution.py:542
  56.4 1.1 collective-permute-start.13
  57.5 1.1 collective-permute-start.11
  58.6 1.3 collective-permute-start.14
  59.8 2.3 %collective-permute-start.15 = (f32[2,32,128]{2,1,0:T(8,128)S(1)}, f32[2,32,128]{2,1,0:T(8,128)S(1)}, u32[]{:S(2)}, u32[]{:S(2)}) collective-permute-start(f32[2,32,128]{2,1,0:T(8,128)S(1)} %get-tuple-element.34), channel_id=1, source_target_pairs={{0,3},{1,0},{2,1},{3,2},{4,7},{5,4},{6,5},{7,6},{8,11},{9,8},{10,9... | collective-permute-start | bytes 98312 | tf_op jit(solution)/shard_map/ppermute | solution.py:542
  62.1 2.0 %collective-permute-done.11.p4 = f32[64,128]{1,0:T(8,128)S(1)} collective-permute-done((f32[64,128]{1,0:T(8,128)S(1)}, f32[64,128]{1,0:T(8,128)S(1)}, u32[]{:S(2)}, u32[]{:S(2)}) %collective-permute-start.11) | collective-permute-done | bytes 32800 | tf_op jit(solution)/shard_map/ppermute | solution.py:542
  64.2 1.3 copy-done.12
  65.4 11.7 %shard_map.121 = (f32[19,32,128]{2,1,0:T(8,128)}, f32[2304,128]{1,0:T(8,128)S(1)}) custom-call(s32[1,16]{1,0:T(1,128)S(1)} %bitcast.90, f32[19,32,128]{2,1,0:T(8,128)S(1)} %bitcast.94, f32[19,32,128]{2,1,0:T(8,128)S(1)} %get-tuple-element.31.local1, f32[64,128]{1,0:T(8,128)S(1)} %collective-permute-done.8.p1, f32[64,128]{1,0:T(8,128)S(1)} %collective-permute-done.9.p2, ...), custom_call_target="tpu_custom_call" | custom-call | flops 4294967296 | bytes 1048576 | tf_op jit(solution)/shard_map/pallas_call | solution.py:523
  77.2 1.3 collective-permute-start.16
  78.5 1.6 %collective-permute-done.16 = f32[1152,128]{1,0:T(8,128)S(1)} collective-permute-done((f32[1152,128]{1,0:T(8,128)S(1)}, f32[1152,128]{1,0:T(8,128)S(1)}, u32[]{:S(2)}, u32[]{:S(2)}) %collective-permute-start.16) | collective-permute-done | bytes 589856 | tf_op jit(solution)/shard_map/ppermute | solution.py:542
  81.8 2.8 %collective-permute-done.19 = f32[288,128]{1,0:T(8,128)S(1)} collective-permute-done((f32[288,128]{1,0:T(8,128)S(1)}, f32[288,128]{1,0:T(8,128)S(1)}, u32[]{:S(2)}, u32[]{:S(2)}) %collective-permute-start.19) | collective-permute-done | bytes 147488 | tf_op jit(solution)/shard_map/ppermute | solution.py:542
  84.6 1.4 %collective-permute-done.18 = f32[288,128]{1,0:T(8,128)S(1)} collective-permute-done((f32[288,128]{1,0:T(8,128)S(1)}, f32[288,128]{1,0:T(8,128)S(1)}, u32[]{:S(2)}, u32[]{:S(2)}) %collective-permute-start.18) | collective-permute-done | bytes 147488 | tf_op jit(solution)/shard_map/ppermute | solution.py:542
  86.0 1.5 %collective-permute-done.17 = f32[288,128]{1,0:T(8,128)S(1)} collective-permute-done((f32[288,128]{1,0:T(8,128)S(1)}, f32[288,128]{1,0:T(8,128)S(1)}, u32[]{:S(2)}, u32[]{:S(2)}) %collective-permute-start.17) | collective-permute-done | bytes 147488 | tf_op jit(solution)/shard_map/ppermute | solution.py:542
  87.6 4.9 %collective-permute-start.22 = (f32[72,128]{1,0:T(8,128)S(1)}, f32[72,128]{1,0:T(8,128)S(1)}, u32[]{:S(2)}, u32[]{:S(2)}) collective-permute-start(f32[72,128]{1,0:T(8,128)S(1)} %get-tuple-element.71), channel_id=1, source_target_pairs={{0,24},{1,25},{2,26},{3,27},{4,28},{5,29},{6,30},{7,31},{8,0},{9,1... | collective-permute-start | bytes 110600 | tf_op jit(solution)/shard_map/ppermute | solution.py:542
  93.6 3.3 %collective-permute-done.21 = f32[72,128]{1,0:T(8,128)S(1)} collective-permute-done((f32[72,128]{1,0:T(8,128)S(1)}, f32[72,128]{1,0:T(8,128)S(1)}, u32[]{:S(2)}, u32[]{:S(2)}) %collective-permute-start.21) | collective-permute-done | bytes 36896 | tf_op jit(solution)/shard_map/ppermute | solution.py:542
  97.2 3.2 %collective-permute-start.25 = (f32[72,128]{1,0:T(8,128)S(1)}, f32[72,128]{1,0:T(8,128)S(1)}, u32[]{:S(2)}, u32[]{:S(2)}) collective-permute-start(f32[72,128]{1,0:T(8,128)S(1)} %fusion.3), channel_id=1, source_target_pairs={{0,96},{1,97},{2,98},{3,99},{4,7},{5,4},{6,5},{7,6},{8,104},{9,105... | collective-permute-start | bytes 110600 | tf_op jit(solution)/shard_map/ppermute | solution.py:542
  101.5 3.4 %collective-permute-done.24 = f32[72,128]{1,0:T(8,128)S(1)} collective-permute-done((f32[72,128]{1,0:T(8,128)S(1)}, f32[72,128]{1,0:T(8,128)S(1)}, u32[]{:S(2)}, u32[]{:S(2)}) %collective-permute-start.24) | collective-permute-done | bytes 36896 | tf_op jit(solution)/shard_map/ppermute | solution.py:542
  125.4 6.4 %collective-permute-start.32 = (f32[1152,128]{1,0:T(8,128)S(1)}, f32[1152,128]{1,0:T(8,128)S(1)}, u32[]{:S(2)}, u32[]{:S(2)}) collective-permute-start(f32[1152,128]{1,0:T(8,128)S(1)} %pad_maximum_fusion.2), channel_id=1, source_target_pairs={{0,4},{1,5},{2,6},{3,7},{4,0},{5,1},{6,2},{7,3},{8,12},{9,13},{10,... | collective-permute-start | bytes 1769480 | tf_op jit(solution)/shard_map/ppermute | solution.py:542
  131.8 1.7 %shard_map.122 = f32[19,32,128]{2,1,0:T(8,128)} custom-call(s32[1,16]{1,0:T(1,128)S(1)} %bitcast.91, f32[19,32,128]{2,1,0:T(8,128)S(1)} %get-tuple-element.39.post2, f32[64,128]{1,0:T(8,128)S(1)} %collective-permute-done.8.p1, f32[64,128]{1,0:T(8,128)S(1)} %collective-permute-done.9.p2, f32[64,128]{1,0:T(8,128)S(1)} %collective-permute-done.10.p3, ...), custom_call_target="tpu_custom_call" | custom-call | flops 1048576 | bytes 1048576 | tf_op jit(solution)/shard_map/pallas_call | solution.py:523
  133.7 1.2 shard_map.123
  (89 shorter events, 16.6 us)
Async XLA Ops:
  16.2 11.5 %collective-permute-start = (f32[64,128]{1,0:T(8,128)S(1)}, f32[64,128]{1,0:T(8,128)S(1)}, u32[]{:S(2)}, u32[]{:S(2)}) collective-permute-start(f32[64,128]{1,0:T(8,128)S(1)} %bitcast.100), channel_id=1, source_target_pairs={{0,124},{1,125},{2,126},{3,127},{4,8},{5,9},{6,10},{7,11},{8,4},{9... | collective-permute-start | bytes 98312 | tf_op jit(solution)/shard_map/ppermute | solution.py:542
  18.8 8.8 %collective-permute-start.1 = (f32[64,128]{1,0:T(8,128)S(1)}, f32[64,128]{1,0:T(8,128)S(1)}, u32[]{:S(2)}, u32[]{:S(2)}) collective-permute-start(f32[64,128]{1,0:T(8,128)S(1)} %bitcast.101), channel_id=1, source_target_pairs={{0,8},{1,9},{2,10},{3,11},{4,12},{5,13},{6,14},{7,15},{8,16},{9,17... | collective-permute-start | bytes 98312 | tf_op jit(solution)/shard_map/ppermute | solution.py:542
  20.1 9.3 %collective-permute-start.2 = (f32[64,128]{1,0:T(8,128)S(1)}, f32[64,128]{1,0:T(8,128)S(1)}, u32[]{:S(2)}, u32[]{:S(2)}) collective-permute-start(f32[64,128]{1,0:T(8,128)S(1)} %bitcast.102), channel_id=1, source_target_pairs={{0,120},{1,121},{2,122},{3,123},{4,124},{5,125},{6,126},{7,127},{8... | collective-permute-start | bytes 98312 | tf_op jit(solution)/shard_map/ppermute | solution.py:542
  23.6 10.7 %collective-permute-start.5 = (f32[128,128]{1,0:T(8,128)S(1)}, f32[128,128]{1,0:T(8,128)S(1)}, u32[]{:S(2)}, u32[]{:S(2)}) collective-permute-start(f32[128,128]{1,0:T(8,128)S(1)} %get-tuple-element.28), channel_id=1, source_target_pairs={{0,4},{1,5},{2,6},{3,7},{4,0},{5,1},{6,2},{7,3},{8,12},{9,13},{10,... | collective-permute-start | bytes 196616 | tf_op jit(solution)/shard_map/ppermute | solution.py:542
  27.7 6.7 %collective-permute-start.3 = (f32[64,128]{1,0:T(8,128)S(1)}, f32[64,128]{1,0:T(8,128)S(1)}, u32[]{:S(2)}, u32[]{:S(2)}) collective-permute-start(f32[64,128]{1,0:T(8,128)S(1)} %bitcast.103), channel_id=1, source_target_pairs={{0,12},{1,13},{2,14},{3,15},{4,120},{5,121},{6,122},{7,123},{8,20}... | collective-permute-start | bytes 98312 | tf_op jit(solution)/shard_map/ppermute | solution.py:542
  27.7 6.7 %collective-permute-start.4 = (f32[64,128]{1,0:T(8,128)S(1)}, f32[64,128]{1,0:T(8,128)S(1)}, u32[]{:S(2)}, u32[]{:S(2)}) collective-permute-start(f32[64,128]{1,0:T(8,128)S(1)} %bitcast.104), channel_id=1, source_target_pairs={{0,116},{1,117},{2,118},{3,119},{4,16},{5,17},{6,18},{7,19},{8,124... | collective-permute-start | bytes 98312 | tf_op jit(solution)/shard_map/ppermute | solution.py:542
  27.7 6.7 %collective-permute-start.6 = (f32[2,32,128]{2,1,0:T(8,128)S(1)}, f32[2,32,128]{2,1,0:T(8,128)S(1)}, u32[]{:S(2)}, u32[]{:S(2)}) collective-permute-start(f32[2,32,128]{2,1,0:T(8,128)S(1)} %get-tuple-element.29), channel_id=1, source_target_pairs={{0,1},{1,2},{2,3},{3,0},{4,5},{5,6},{6,7},{7,4},{8,9},{9,10},{10,1... | collective-permute-start | bytes 98312 | tf_op jit(solution)/shard_map/ppermute | solution.py:542
  29.4 5.0 %collective-permute-start.7 = (f32[2,32,128]{2,1,0:T(8,128)S(1)}, f32[2,32,128]{2,1,0:T(8,128)S(1)}, u32[]{:S(2)}, u32[]{:S(2)}) collective-permute-start(f32[2,32,128]{2,1,0:T(8,128)S(1)} %get-tuple-element.29), channel_id=1, source_target_pairs={{0,3},{1,0},{2,1},{3,2},{4,7},{5,4},{6,5},{7,6},{8,11},{9,8},{10,9... | collective-permute-start | bytes 98312 | tf_op jit(solution)/shard_map/ppermute | solution.py:542
  50.6 8.0 %collective-permute-start.8 = (f32[64,128]{1,0:T(8,128)S(1)}, f32[64,128]{1,0:T(8,128)S(1)}, u32[]{:S(2)}, u32[]{:S(2)}) collective-permute-start(f32[64,128]{1,0:T(8,128)S(1)} %bitcast.95), channel_id=1, source_target_pairs={{0,124},{1,125},{2,126},{3,127},{4,8},{5,9},{6,10},{7,11},{8,4},{9... | collective-permute-start | bytes 98312 | tf_op jit(solution)/shard_map/ppermute | solution.py:542
  51.6 7.0 %collective-permute-start.9 = (f32[64,128]{1,0:T(8,128)S(1)}, f32[64,128]{1,0:T(8,128)S(1)}, u32[]{:S(2)}, u32[]{:S(2)}) collective-permute-start(f32[64,128]{1,0:T(8,128)S(1)} %bitcast.96), channel_id=1, source_target_pairs={{0,8},{1,9},{2,10},{3,11},{4,12},{5,13},{6,14},{7,15},{8,16},{9,17... | collective-permute-start | bytes 98312 | tf_op jit(solution)/shard_map/ppermute | solution.py:542
  52.7 7.1 %collective-permute-start.10 = (f32[64,128]{1,0:T(8,128)S(1)}, f32[64,128]{1,0:T(8,128)S(1)}, u32[]{:S(2)}, u32[]{:S(2)}) collective-permute-start(f32[64,128]{1,0:T(8,128)S(1)} %bitcast.97), channel_id=1, source_target_pairs={{0,120},{1,121},{2,122},{3,123},{4,124},{5,125},{6,126},{7,127},{8... | collective-permute-start | bytes 98312 | tf_op jit(solution)/shard_map/ppermute | solution.py:542
  56.4 7.8 %collective-permute-start.13 = (f32[128,128]{1,0:T(8,128)S(1)}, f32[128,128]{1,0:T(8,128)S(1)}, u32[]{:S(2)}, u32[]{:S(2)}) collective-permute-start(f32[128,128]{1,0:T(8,128)S(1)} %get-tuple-element.33), channel_id=1, source_target_pairs={{0,4},{1,5},{2,6},{3,7},{4,0},{5,1},{6,2},{7,3},{8,12},{9,13},{10,... | collective-permute-start | bytes 196616 | tf_op jit(solution)/shard_map/ppermute | solution.py:542
  57.5 6.7 %collective-permute-start.11 = (f32[64,128]{1,0:T(8,128)S(1)}, f32[64,128]{1,0:T(8,128)S(1)}, u32[]{:S(2)}, u32[]{:S(2)}) collective-permute-start(f32[64,128]{1,0:T(8,128)S(1)} %bitcast.98), channel_id=1, source_target_pairs={{0,12},{1,13},{2,14},{3,15},{4,120},{5,121},{6,122},{7,123},{8,20}... | collective-permute-start | bytes 98312 | tf_op jit(solution)/shard_map/ppermute | solution.py:542
  58.5 5.6 %collective-permute-start.12 = (f32[64,128]{1,0:T(8,128)S(1)}, f32[64,128]{1,0:T(8,128)S(1)}, u32[]{:S(2)}, u32[]{:S(2)}) collective-permute-start(f32[64,128]{1,0:T(8,128)S(1)} %bitcast.99), channel_id=1, source_target_pairs={{0,116},{1,117},{2,118},{3,119},{4,16},{5,17},{6,18},{7,19},{8,124... | collective-permute-start | bytes 98312 | tf_op jit(solution)/shard_map/ppermute | solution.py:542
  58.6 5.6 %collective-permute-start.14 = (f32[2,32,128]{2,1,0:T(8,128)S(1)}, f32[2,32,128]{2,1,0:T(8,128)S(1)}, u32[]{:S(2)}, u32[]{:S(2)}) collective-permute-start(f32[2,32,128]{2,1,0:T(8,128)S(1)} %get-tuple-element.34), channel_id=1, source_target_pairs={{0,1},{1,2},{2,3},{3,0},{4,5},{5,6},{6,7},{7,4},{8,9},{9,10},{10,1... | collective-permute-start | bytes 98312 | tf_op jit(solution)/shard_map/ppermute | solution.py:542
  59.8 4.3 %collective-permute-start.15 = (f32[2,32,128]{2,1,0:T(8,128)S(1)}, f32[2,32,128]{2,1,0:T(8,128)S(1)}, u32[]{:S(2)}, u32[]{:S(2)}) collective-permute-start(f32[2,32,128]{2,1,0:T(8,128)S(1)} %get-tuple-element.34), channel_id=1, source_target_pairs={{0,3},{1,0},{2,1},{3,2},{4,7},{5,4},{6,5},{7,6},{8,11},{9,8},{10,9... | collective-permute-start | bytes 98312 | tf_op jit(solution)/shard_map/ppermute | solution.py:542
  80.3 4.4 %collective-permute-start.19 = (f32[288,128]{1,0:T(8,128)S(1)}, f32[288,128]{1,0:T(8,128)S(1)}, u32[]{:S(2)}, u32[]{:S(2)}) collective-permute-start(f32[288,128]{1,0:T(8,128)S(1)} %get-tuple-element.62), channel_id=1, source_target_pairs={{0,3},{1,0},{2,1},{3,2},{4,100},{5,101},{6,102},{7,103},{8,11},{9,... | collective-permute-start | bytes 442376 | tf_op jit(solution)/shard_map/ppermute | solution.py:542
  80.4 5.7 %collective-permute-start.18 = (f32[288,128]{1,0:T(8,128)S(1)}, f32[288,128]{1,0:T(8,128)S(1)}, u32[]{:S(2)}, u32[]{:S(2)}) collective-permute-start(f32[288,128]{1,0:T(8,128)S(1)} %get-tuple-element.63), channel_id=1, source_target_pairs={{0,2},{1,3},{2,0},{3,1},{4,68},{5,69},{6,70},{7,71},{8,10},{9,11},... | collective-permute-start | bytes 442376 | tf_op jit(solution)/shard_map/ppermute | solution.py:542
  80.9 6.6 %collective-permute-start.17 = (f32[288,128]{1,0:T(8,128)S(1)}, f32[288,128]{1,0:T(8,128)S(1)}, u32[]{:S(2)}, u32[]{:S(2)}) collective-permute-start(f32[288,128]{1,0:T(8,128)S(1)} %get-tuple-element.61), channel_id=1, source_target_pairs={{0,1},{1,2},{2,3},{3,0},{4,36},{5,37},{6,38},{7,39},{8,9},{9,10},{... | collective-permute-start | bytes 442376 | tf_op jit(solution)/shard_map/ppermute | solution.py:542
  87.6 6.0 %collective-permute-start.22 = (f32[72,128]{1,0:T(8,128)S(1)}, f32[72,128]{1,0:T(8,128)S(1)}, u32[]{:S(2)}, u32[]{:S(2)}) collective-permute-start(f32[72,128]{1,0:T(8,128)S(1)} %get-tuple-element.71), channel_id=1, source_target_pairs={{0,24},{1,25},{2,26},{3,27},{4,28},{5,29},{6,30},{7,31},{8,0},{9,1... | collective-permute-start | bytes 110600 | tf_op jit(solution)/shard_map/ppermute | solution.py:542
  92.5 4.4 %collective-permute-start.21 = (f32[72,128]{1,0:T(8,128)S(1)}, f32[72,128]{1,0:T(8,128)S(1)}, u32[]{:S(2)}, u32[]{:S(2)}) collective-permute-start(f32[72,128]{1,0:T(8,128)S(1)} %get-tuple-element.72), channel_id=1, source_target_pairs={{0,16},{1,17},{2,18},{3,19},{4,20},{5,21},{6,22},{7,23},{8,24},{9,... | collective-permute-start | bytes 110600 | tf_op jit(solution)/shard_map/ppermute | solution.py:542
  92.8 4.4 %collective-permute-start.20 = (f32[72,128]{1,0:T(8,128)S(1)}, f32[72,128]{1,0:T(8,128)S(1)}, u32[]{:S(2)}, u32[]{:S(2)}) collective-permute-start(f32[72,128]{1,0:T(8,128)S(1)} %get-tuple-element.70), channel_id=1, source_target_pairs={{0,8},{1,9},{2,10},{3,11},{4,12},{5,13},{6,14},{7,15},{8,16},{9,17... | collective-permute-start | bytes 110600 | tf_op jit(solution)/shard_map/ppermute | solution.py:542
  97.2 4.2 %collective-permute-start.25 = (f32[72,128]{1,0:T(8,128)S(1)}, f32[72,128]{1,0:T(8,128)S(1)}, u32[]{:S(2)}, u32[]{:S(2)}) collective-permute-start(f32[72,128]{1,0:T(8,128)S(1)} %fusion.3), channel_id=1, source_target_pairs={{0,96},{1,97},{2,98},{3,99},{4,7},{5,4},{6,5},{7,6},{8,104},{9,105... | collective-permute-start | bytes 110600 | tf_op jit(solution)/shard_map/ppermute | solution.py:542
  100.4 4.4 %collective-permute-start.24 = (f32[72,128]{1,0:T(8,128)S(1)}, f32[72,128]{1,0:T(8,128)S(1)}, u32[]{:S(2)}, u32[]{:S(2)}) collective-permute-start(f32[72,128]{1,0:T(8,128)S(1)} %fusion.3), channel_id=1, source_target_pairs={{0,64},{1,65},{2,66},{3,67},{4,6},{5,7},{6,4},{7,5},{8,72},{9,73},... | collective-permute-start | bytes 110600 | tf_op jit(solution)/shard_map/ppermute | solution.py:542
  100.4 4.4 %collective-permute-start.23 = (f32[72,128]{1,0:T(8,128)S(1)}, f32[72,128]{1,0:T(8,128)S(1)}, u32[]{:S(2)}, u32[]{:S(2)}) collective-permute-start(f32[72,128]{1,0:T(8,128)S(1)} %fusion.3), channel_id=1, source_target_pairs={{0,32},{1,33},{2,34},{3,35},{4,5},{5,6},{6,7},{7,4},{8,40},{9,41},... | collective-permute-start | bytes 110600 | tf_op jit(solution)/shard_map/ppermute | solution.py:542
  104.8 10.2 %collective-permute-start.28 = (f32[72,128]{1,0:T(8,128)S(1)}, f32[72,128]{1,0:T(8,128)S(1)}, u32[]{:S(2)}, u32[]{:S(2)}) collective-permute-start(f32[72,128]{1,0:T(8,128)S(1)} %add_add_fusion), channel_id=1, source_target_pairs={{0,24},{1,25},{2,26},{3,27},{4,28},{5,29},{6,30},{7,31},{8,0},{9,1... | collective-permute-start | bytes 110600 | tf_op jit(solution)/shard_map/ppermute | solution.py:542
  105.8 9.3 %collective-permute-start.27 = (f32[72,128]{1,0:T(8,128)S(1)}, f32[72,128]{1,0:T(8,128)S(1)}, u32[]{:S(2)}, u32[]{:S(2)}) collective-permute-start(f32[72,128]{1,0:T(8,128)S(1)} %add_add_fusion), channel_id=1, source_target_pairs={{0,16},{1,17},{2,18},{3,19},{4,20},{5,21},{6,22},{7,23},{8,24},{9,... | collective-permute-start | bytes 110600 | tf_op jit(solution)/shard_map/ppermute | solution.py:542
  106.0 9.1 %collective-permute-start.26 = (f32[72,128]{1,0:T(8,128)S(1)}, f32[72,128]{1,0:T(8,128)S(1)}, u32[]{:S(2)}, u32[]{:S(2)}) collective-permute-start(f32[72,128]{1,0:T(8,128)S(1)} %add_add_fusion), channel_id=1, source_target_pairs={{0,8},{1,9},{2,10},{3,11},{4,12},{5,13},{6,14},{7,15},{8,16},{9,17... | collective-permute-start | bytes 110600 | tf_op jit(solution)/shard_map/ppermute | solution.py:542
  115.2 10.0 %collective-permute-start.31 = (f32[288,128]{1,0:T(8,128)S(1)}, f32[288,128]{1,0:T(8,128)S(1)}, u32[]{:S(2)}, u32[]{:S(2)}) collective-permute-start(f32[288,128]{1,0:T(8,128)S(1)} %get-tuple-element.65), channel_id=1, source_target_pairs={{0,3},{1,0},{2,1},{3,2},{4,100},{5,101},{6,102},{7,103},{8,11},{9,... | collective-permute-start | bytes 442376 | tf_op jit(solution)/shard_map/ppermute | solution.py:542
  116.1 9.1 %collective-permute-start.30 = (f32[288,128]{1,0:T(8,128)S(1)}, f32[288,128]{1,0:T(8,128)S(1)}, u32[]{:S(2)}, u32[]{:S(2)}) collective-permute-start(f32[288,128]{1,0:T(8,128)S(1)} %get-tuple-element.65), channel_id=1, source_target_pairs={{0,2},{1,3},{2,0},{3,1},{4,68},{5,69},{6,70},{7,71},{8,10},{9,11},... | collective-permute-start | bytes 442376 | tf_op jit(solution)/shard_map/ppermute | solution.py:542
  116.2 9.1 %collective-permute-start.29 = (f32[288,128]{1,0:T(8,128)S(1)}, f32[288,128]{1,0:T(8,128)S(1)}, u32[]{:S(2)}, u32[]{:S(2)}) collective-permute-start(f32[288,128]{1,0:T(8,128)S(1)} %get-tuple-element.65), channel_id=1, source_target_pairs={{0,1},{1,2},{2,3},{3,0},{4,36},{5,37},{6,38},{7,39},{8,9},{9,10},{... | collective-permute-start | bytes 442376 | tf_op jit(solution)/shard_map/ppermute | solution.py:542
  125.4 8.1 %collective-permute-start.32 = (f32[1152,128]{1,0:T(8,128)S(1)}, f32[1152,128]{1,0:T(8,128)S(1)}, u32[]{:S(2)}, u32[]{:S(2)}) collective-permute-start(f32[1152,128]{1,0:T(8,128)S(1)} %pad_maximum_fusion.2), channel_id=1, source_target_pairs={{0,4},{1,5},{2,6},{3,7},{4,0},{5,1},{6,2},{7,3},{8,12},{9,13},{10,... | collective-permute-start | bytes 1769480 | tf_op jit(solution)/shard_map/ppermute | solution.py:542
  (14 other events, 122.3 us)
where the time goes:
time: 135 us
  starting transfers between devices  49.2 us (36%)
  Pallas kernels  37.1 us (27%)
  waiting for transfers between devices  19.7 us (15%)
  between operations  16.5 us (12%)
  local copies, waits for them, and re-layouts  11.8 us (9%)
    ppermute x33, starting transfers between devices, send(): return lax.ppermute(value, AXES, pairs)  49.2 us
    pallas_call x5, Pallas kernels, run(): pl.pallas_call(kernel, out_shape=outs, in_specs=in_specs, out_specs=out_s...  37.1 us
    ppermute x33, waiting for transfers between devices, send(): return lax.ppermute(value, AXES, pairs)  19.7 us
    unnamed x27, local copies, waits for them, and re-layouts  9.63 us
  transfers between devices with their start and end apart: 33, of which 11 were waited for; matrix products, arithmetic and copies ran while one was open for 1% of the time, Pallas kernels for 1%

commit v1 on v0

v1 whole, which is shorter than its diff:
```python
import jax
import jax.numpy as jnp
from jax import lax
from jax.experimental import pallas as pl
from jax.experimental.pallas import tpu as pltpu
from jax.sharding import Mesh
from jax.sharding import PartitionSpec as P

Q = 19
HID = 512
CELLS = 4096
ROWS = 32
CHUNK = 1024
TILES = CHUNK // 128
CHUNKS = CELLS // CHUNK
NB = 32
NZ = 4
NX = 4
BLOCKS = ("bx", "by", "core")
AXES = ("bx", "by", "core", "slab")
CHIPS = ("bx", "by", "slab")
F32 = jnp.float32
BF16 = jnp.bfloat16
VMEM_LIMIT = 32 * 1024 * 1024
GROWS = 2304
HALF = GROWS // 2
OUT_AT = 4 * HID
IN_AT = OUT_AT + 4 * 24

VELOCITIES = [
    (0, 0, 0),
    (1, 0, 0),
    (-1, 0, 0),
    (0, 1, 0),
    (0, -1, 0),
    (0, 0, 1),
    (0, 0, -1),
    (1, 1, 0),
    (-1, -1, 0),
    (1, -1, 0),
    (-1, 1, 0),
    (1, 0, 1),
    (-1, 0, -1),
    (1, 0, -1),
    (-1, 0, 1),
    (0, 1, 1),
    (0, -1, -1),
    (0, 1, -1),
    (0, -1, 1),
]
OPPOSITE = [0, 2, 1, 4, 3, 6, 5, 8, 7, 10, 9, 12, 11, 14, 13, 16, 15, 18, 17]


def members(face):
    sign = 1 if face % 2 == 0 else -1
    return [q for q in range(Q) if VELOCITIES[q][face // 2] == sign]


def iota(rows, dim):
    return lax.broadcasted_iota(jnp.int32, (rows, 128), dim)


def roll(value, shift, axis):
    shift %= value.shape[axis]
    return value if shift == 0 else pltpu.roll(value, shift, axis)


def shifted(v, velocity):
    cx, cy, cz = velocity
    lane = iota(ROWS, 1)
    if cz:
        v = jnp.where(lane & 15 == (0 if cz == 1 else 15), roll(v, -15 * cz, 1), roll(v, cz, 1))
    if cy:
        t = roll(v, 16 * cy, 1)
        swapped = jnp.where(iota(ROWS, 0) & 1 == 1, roll(t, 1, 0), roll(t, -1, 0))
        v = jnp.where(lane >> 4 == (0 if cy == 1 else 7), swapped, t)
    if cx:
        v = roll(v, 2 * cx, 0)
    return v


def corner(q):
    row, lane = iota(ROWS, 0), iota(ROWS, 1)
    coords = [row >> 1, (row & 1) * 8 + (lane >> 4), lane & 15]
    mask = None
    for axis in range(3):
        c = VELOCITIES[q][axis]
        if c:
            here = coords[axis] == (0 if c == 1 else 15)
            mask = here if mask is None else mask & here
    return mask


def is_edge(q):
    return sum(abs(c) for c in VELOCITIES[q]) == 2


def pack_faces(src, put_x, put_y, put_z):
    lane16, lane32 = iota(16, 1), iota(ROWS, 1)
    for f in (0, 1):
        for i, q in enumerate(members(f)):
            for r in (0, 1):
                put_x(f, r, i, src[q, pl.ds((30 if f == 0 else 0) + r, 1), :])
    for f in (2, 3):
        acc = jnp.zeros((16, 128), F32)
        for i, q in enumerate(members(f)):
            v = src[q, pl.ds(1 if f == 2 else 0, 16, stride=2), :]
            v = roll(v, 16 * i - (112 if f == 2 else 0), 1)
            acc = jnp.where(lane16 >> 4 == i, v, acc)
        put_y(f - 2, acc)
    acc = jnp.zeros((ROWS, 128), F32)
    for f in (4, 5):
        for i, q in enumerate(members(f)):
            slot = i if f == 4 else 8 + i
            v = roll(src[q], slot - (15 if f == 4 else 0), 1)
            acc = jnp.where(lane32 & 15 == slot, v, acc)
    put_z(acc)


def unpack_faces(dst, get_x, y_ref, z, add):
    lane16, lane32 = iota(16, 1), iota(ROWS, 1)
    for f in (0, 1):
        for i, q in enumerate(members(f)):
            for r in (0, 1):
                at = pl.ds((30 if f == 0 else 0) + r, 1)
                v = get_x(f, r, i)
                dst[q, at, :] = dst[q, at, :] + v if add else v
    for f in (2, 3):
        packed = y_ref[f - 2]
        for i, q in enumerate(members(f)):
            at = pl.ds(1 if f == 2 else 0, 16, stride=2)
            v = roll(packed, (112 if f == 2 else 0) - 16 * i, 1)
            old = dst[q, at, :]
            new = old + v if add else v
            dst[q, at, :] = jnp.where(lane16 >> 4 == (7 if f == 2 else 0), new, old)
    for f in (4, 5):
        for i, q in enumerate(members(f)):
            v = roll(z, 15 - i if f == 4 else -(8 + i), 1)
            old = dst[q]
            new = old + v if add else v
            dst[q] = jnp.where(lane32 & 15 == (15 if f == 4 else 0), new, old)


def picked(value, index):
    return jnp.take_along_axis(value, index, axis=1)


class Tables:
    def __init__(self, place, source, level, quadrant):
        self.place, self.source, self.level, self.quadrant = place, source, level, quadrant

    def block(self):
        return self.place[0]

    def distance(self, face):
        d = self.source[face, self.block()] - self.block()
        return jnp.where(d < 0, d + NB, d)


def level_of(info, f):
    return info.level[0, f ^ 1] == 1


def quadrant_of(info, f):
    r = info.quadrant[0, f ^ 1]
    return r >> 1, r & 1


def refine_x(info, x):
    lane = iota(8, 1)
    for f in (0, 1):
        fine = level_of(info, f)
        qr, qc = quadrant_of(info, f)
        rows = [x[f, 0], x[f, 1]]
        source = jnp.where(qr == 0, rows[0], rows[1])
        for r in (0, 1):
            index = (r * 4 + (lane >> 5)) * 16 + qc * 8 + ((lane & 15) >> 1)
            x[f, r] = jnp.where(fine, picked(source, index), rows[r])


def refine_y(info, y):
    lane = iota(8, 1)
    for f in (2, 3):
        fine = level_of(info, f)
        qr, qc = quadrant_of(info, f)
        whole = y[f - 2]
        source = jnp.where(qr == 0, whole[:8], whole[8:])
        v = picked(source, (lane >> 4) * 16 + qc * 8 + ((lane & 15) >> 1))
        for d in (0, 1):
            at = pl.ds(d, 8, stride=2)
            y[f - 2, at, :] = jnp.where(fine, v, y[f - 2, at, :])


def refine_z(info, z_two):
    lane = iota(8, 1)
    for f in (4, 5):
        z = z_two.at[f - 4]
        fine = level_of(info, f)
        qr, qc = quadrant_of(info, f)
        parts = {(h, p): z[pl.ds(16 * h + p, 8, stride=2), :] for h in (0, 1) for p in (0, 1)}
        halves = [jnp.where(qc == 0, parts[h, 0], parts[h, 1]) for h in (0, 1)]
        source = jnp.where(qr == 0, halves[0], halves[1])
        for p in (0, 1):
            v = picked(source, (p * 4 + (lane >> 5)) * 16 + (lane & 15))
            for d in (0, 1):
                at = pl.ds(2 * d + p, 8, stride=4)
                z[at, :] = jnp.where(fine, v, z[at, :])
    return jnp.where(iota(ROWS, 1) & 15 < 8, z_two[0], z_two[1])


def gather_x(info, x):
    lane = iota(8, 1)
    index = (2 * ((lane >> 4) & 3)) * 16 + 2 * (lane & 7)
    for f in (0, 1):
        fine = level_of(info, f)
        qr, qc = quadrant_of(info, f)
        rows = [x[f, 0], x[f, 1]]
        sums = []
        for v in rows:
            v = v + roll(v, -1, 1)
            v = v + roll(v, -16, 1)
            sums.append(picked(v, index))
        v = jnp.where(lane < 64, sums[0], sums[1])
        v = jnp.where((lane & 15) >> 3 == qc, v, 0.0)
        for r in (0, 1):
            x[f, r] = jnp.where(fine, jnp.where(qr == r, v, 0.0), rows[r])


def gather_y(info, y):
    lane = iota(8, 1)
    index = (lane >> 4) * 16 + 2 * (lane & 7)
    for f in (2, 3):
        fine = level_of(info, f)
        qr, qc = quadrant_of(info, f)
        v = y[f - 2, pl.ds(0, 8, stride=2), :] + y[f - 2, pl.ds(1, 8, stride=2), :]
        v = picked(v + roll(v, -1, 1), index)
        v = jnp.where((lane & 15) >> 3 == qc, v, 0.0)
        for h in (0, 1):
            at = pl.ds(8 * h, 8)
            y[f - 2, at, :] = jnp.where(fine, jnp.where(qr == h, v, 0.0), y[f - 2, at, :])


def gather_z(info, z_two):
    lane = iota(8, 1)
    index = (2 * ((lane >> 4) & 3)) * 16 + (lane & 15)
    for f in (4, 5):
        z = z_two.at[f - 4]
        fine = level_of(info, f)
        qr, qc = quadrant_of(info, f)
        sums = []
        for p in (0, 1):
            v = z[pl.ds(p, 8, stride=4), :] + z[pl.ds(2 + p, 8, stride=4), :]
            sums.append(picked(v + roll(v, -16, 1), index))
        v = jnp.where(lane < 64, sums[0], sums[1])
        for h in (0, 1):
            for p in (0, 1):
                at = pl.ds(16 * h + p, 8, stride=2)
                here = (qr == h) & (qc == p)
                z[at, :] = jnp.where(fine, jnp.where(here, v, 0.0), z[at, :])
    return jnp.where(iota(ROWS, 1) & 15 < 8, z_two[0], z_two[1])


def choose_x(info, face, both, low, high, far, kind):
    d = info.distance(face)
    even = info.block() & 1 == 0
    cases = [
        (jnp.where(even, 1, NB - 1), both, 0),
        (NB - 2, low, 0),
        (jnp.where(even, NB - 1, NB - 3), low, 64),
        (2, high, 0),
        (jnp.where(even, 3, 1), high, 64),
        (jnp.where(even, NB - 3, 3), far, 0),
    ]
    return lambda f, r: sum_where(
        [
            (d == spot, ref[pl.ds(at + 8 * (kind * 4 + f * 2 + r), 8), :])
            for spot, ref, at in cases
        ]
    )


def sum_where(cases):
    total = jnp.zeros((8, 128), F32)
    for condition, value in cases:
        total = jnp.where(condition, value, total)
    return total


def stream_back(info, bar, local, xs, xys, zs, work, y_two, z_two):
    for q in range(Q):
        v = bar[q]
        if is_edge(q):
            v = jnp.where(corner(q), 0.0, v)
        work[q] = shifted(v, tuple(-c for c in VELOCITIES[q]))
    x_four = xs.at[1]
    x_four[...] = jnp.zeros(x_four.shape, F32)

    def put_x(f, r, i, v):
        x_four[f, r, pl.ds(i, 1), :] = v

    def put_y(f, v):
        y_two[f] = v

    def put_z(v):
        z_two[0] = v
        z_two[1] = v

    pack_faces(work, put_x, put_y, put_z)
    gather_x(info, x_four)
    gather_y(info, y_two)
    zs[1] = gather_z(info, z_two)
    xys[pl.ds(32, 32), :] = xs[1].reshape(32, 128)
    xys[pl.ds(96, 32), :] = y_two[...].reshape(32, 128)
    row, lane = iota(ROWS, 0), iota(ROWS, 1)
    coords = [row >> 1, (row & 1) * 8 + (lane >> 4), lane & 15]
    for q in range(Q):
        v = work[q]
        leaving = None
        for axis in range(3):
            c = VELOCITIES[q][axis]
            if c:
                here = coords[axis] == (15 if c == 1 else 0)
                leaving = here if leaving is None else leaving | here
        if leaving is not None:
            v = jnp.where(leaving, 0.0, v)
        if is_edge(q):
            v = v + jnp.where(corner(OPPOSITE[q]), bar[OPPOSITE[q]], 0.0)
        local[q] = v


def send_post(post, xs, xys, zs):
    x_four = xs.at[0]
    x_four[...] = jnp.zeros(x_four.shape, F32)

    def put_x(f, r, i, v):
        x_four[f, r, pl.ds(i, 1), :] = v

    def put_y(f, v):
        xys[pl.ds(64 + 16 * f, 16), :] = v

    def put_z(v):
        zs[0] = v

    pack_faces(post, put_x, put_y, put_z)
    xys[pl.ds(0, 32), :] = xs[0].reshape(32, 128)


def stream(info, post, got, out, work, x_four, y_two, z_two):
    both, low, high, far, below, above = got
    for f in (0, 1):
        pick = choose_x(info, f ^ 1, both, low, high, far, 0)
        for r in (0, 1):
            x_four[f, r] = pick(f, r)
    refine_x(info, x_four)
    y_two[0] = both[pl.ds(64, 16), :]
    y_two[1] = both[pl.ds(80, 16), :]
    refine_y(info, y_two)
    z_two[0] = below[0]
    z_two[1] = above[0]
    z = refine_z(info, z_two)
    work[...] = post[...]
    unpack_faces(work, lambda f, r, i: x_four[f, r, pl.ds(i, 1), :], y_two, z, False)
    for q in range(Q):
        v = shifted(work[q], VELOCITIES[q])
        if is_edge(q):
            v = jnp.where(corner(q), post[OPPOSITE[q]], v)
        out[q] = v


def take_back(info, bar, got, x_four, y_two):
    both, low, high, far, below, above = got
    for f in (0, 1):
        pick = choose_x(info, f, both, low, high, far, 1)
        for r in (0, 1):
            x_four[f, r] = pick(f, r)
    y_two[0] = both[pl.ds(96, 16), :]
    y_two[1] = both[pl.ds(112, 16), :]
    z = jnp.where(iota(ROWS, 1) & 15 < 8, above[1], below[1])
    unpack_faces(bar, lambda f, r, i: x_four[f, r, pl.ds(i, 1), :], y_two, z, True)


def dot(a, b, ca=1, cb=0):
    return lax.dot_general(a, b, (((ca,), (cb,)), ((), ())), preferred_element_type=F32)


def cells_of(ref, step):
    parts = [
        ref[:, pl.ds(step * TILES + j, 1), :].reshape(Q, 128) for j in range(TILES)
    ]
    return jnp.concatenate(parts, axis=1)


def put_cells(ref, step, value):
    for j in range(TILES):
        ref[:, pl.ds(step * TILES + j, 1), :] = value[:, j * 128 : (j + 1) * 128].reshape(Q, 1, 128)


def span(step):
    return pl.ds(step * CHUNK, CHUNK)


def forward(x, w_in_t, w_mid, w_out):
    xb = x.astype(BF16)
    h0 = jnp.tanh(dot(w_in_t, xb, 0, 0)).astype(BF16)
    h1 = jnp.tanh(dot(w_mid, h0)).astype(BF16)
    return h0, h1, x + dot(w_out, h1)


def slope(h):
    h = h.astype(F32)
    return 1.0 - h * h


def signals(pbar, h0, h1, w_mid_t, w_out):
    e = pbar.astype(BF16)
    a1 = (dot(w_out, e, 0, 0) * slope(h1)).astype(BF16)
    a0 = (dot(w_mid_t, a1) * slope(h0)).astype(BF16)
    return e, a1, a0


class Copies:
    def __init__(self, sems):
        self.sems, self.made = sems, []

    def start(self, source, target):
        copy = pltpu.make_async_copy(source, target, self.sems.at[len(self.made)])
        copy.start()
        self.made.append(copy)
        return copy

    def wait(self):
        for copy in self.made:
            copy.wait()


def put_grads(grads, x, e, h0, h1, a0, a1, more):
    def put(at, rows, value):
        for j in range(4):
            spot = pl.ds(at + j * (HID if rows == HID else 24), rows)
            v = value[:, j * 128 : (j + 1) * 128]
            grads[spot, :] = v if more is None else more[spot, :] + v

    put(0, HID, dot(a1[...], h0[...], 1, 1))
    put(OUT_AT, Q, dot(e[...], h1[...], 1, 1))
    put(IN_AT, Q, dot(x[...], a0[...], 1, 1))
    if more is None:
        rest = GROWS - IN_AT - 96
        grads[pl.ds(IN_AT + 96, rest), :] = jnp.zeros((rest, 128), F32)


def first_kernel(place, source_far, level_far, quadrant_far, f0_far, cot_far, w_in_far, w_mid_far,
                 w_out_far, post, local, xs, xys, zs, h0_far, h1_far,
                 source, level, quadrant, f0, cot, w_in_t, w_mid, w_out, h0, h1, work, y_two, z_two,
                 sems, out_sems):
    info = Tables(place, source, level, quadrant)
    copies = Copies(sems)
    for far, near in ((cot_far, cot), (source_far, source), (level_far, level),
                      (quadrant_far, quadrant), (f0_far, f0), (w_in_far, w_in_t),
                      (w_mid_far, w_mid), (w_out_far, w_out)):
        copies.start(far, near)
    for copy in copies.made[:4]:
        copy.wait()
    stream_back(info, cot, local, xs, xys, zs, work, y_two, z_two)
    for copy in copies.made[4:]:
        copy.wait()
    copies = Copies(out_sems)
    for step in range(CHUNKS):
        a, b, out = forward(cells_of(f0, step), w_in_t[...], w_mid[...], w_out[...])
        h0[:, span(step)] = a
        copies.start(h0.at[:, span(step)], h0_far.at[:, span(step)])
        h1[:, span(step)] = b
        copies.start(h1.at[:, span(step)], h1_far.at[:, span(step)])
        put_cells(post, step, out)
    send_post(post, xs, xys, zs)
    copies.wait()


def second_kernel(place, source, level, quadrant, post1, local2, both, low, high, far, below, above,
                  w_in_t, w_mid, w_mid_t, w_out,
                  post, local, xs, xys, zs, x, e, h0_far, h1_far, a0_far, a1_far,
                  h0, h1, a0, a1, f1, pbar, fbar, work, x_four, y_two, z_two, sems):
    info = Tables(place, source, level, quadrant)
    got = (both, low, high, far, below, above)
    stream(info, post1, got, f1, work, x_four, y_two, z_two)
    pbar[...] = local2[...]
    take_back(info, pbar, got, x_four, y_two)
    copies = Copies(sems)
    for step in range(CHUNKS):
        at = span(step)
        f = cells_of(f1, step)
        h0_now, h1_now, out = forward(f, w_in_t[...], w_mid[...], w_out[...])
        put_cells(post, step, out)
        x[:, at] = f.astype(BF16)
        h0[:, at] = h0_now
        copies.start(h0.at[:, at], h0_far.at[:, at])
        h1[:, at] = h1_now
        copies.start(h1.at[:, at], h1_far.at[:, at])
        bar = cells_of(pbar, step)
        e_now, a1_now, a0_now = signals(bar, h0_now, h1_now, w_mid_t[...], w_out[...])
        put_cells(fbar, step, bar + dot(w_in_t[...], a0_now))
        e[:, at] = e_now
        a1[:, at] = a1_now
        copies.start(a1.at[:, at], a1_far.at[:, at])
        a0[:, at] = a0_now
        copies.start(a0.at[:, at], a0_far.at[:, at])
    send_post(post, xs, xys, zs)
    stream_back(info, fbar, local, xs, xys, zs, work, y_two, z_two)
    copies.wait()


def grads_kernel(x, e, h0_far, h1_far, a0_far, a1_far, grads, h0, h1, a0, a1, sems):
    copies = Copies(sems)
    pairs = ((h0_far, h0), (a1_far, a1), (h1_far, h1), (a0_far, a0))
    for step in range(CHUNKS):
        for far, near in pairs:
            copies.start(far.at[:, span(step)], near.at[:, span(step)])
    for step in range(CHUNKS):
        for copy in copies.made[4 * step : 4 * step + 4]:
            copy.wait()
        at = span(step)
        put_grads(grads, x.at[:, at], e.at[:, at], h0.at[:, at], h1.at[:, at], a0.at[:, at],
                  a1.at[:, at], grads if step else None)


def third_kernel(place, source, level, quadrant, f0, local1, both, low, high, far, below, above,
                 w_mid_t, w_out, grads2, h0_far, h1_far,
                 grads, pbar, a0_far, h0, h1, a0, a1, x, e, x_four, y_two, sems):
    info = Tables(place, source, level, quadrant)
    got = (both, low, high, far, below, above)
    copies = Copies(sems)
    for step in range(CHUNKS):
        for hbm, near in ((h1_far, h1), (h0_far, h0)):
            copies.start(hbm.at[:, span(step)], near.at[:, span(step)])
    pbar[...] = local1[...]
    take_back(info, pbar, got, x_four, y_two)
    for step in range(CHUNKS):
        at = span(step)
        for copy in copies.made[2 * step : 2 * step + 2]:
            copy.wait()
        e_now, a1_now, a0_now = signals(
            cells_of(pbar, step), h0[:, at], h1[:, at], w_mid_t[...], w_out[...]
        )
        x[:, at] = cells_of(f0, step).astype(BF16)
        e[:, at] = e_now
        a1[:, at] = a1_now
        a0[:, at] = a0_now
        copies.start(a0.at[:, at], a0_far.at[:, at])
    put_grads(grads, x, e, h0, h1, a0, a1, grads2)
    for copy in copies.made[2 * CHUNKS :]:
        copy.wait()


def final_kernel(place, source, level, quadrant, post2, both, low, high, far, below, above,
                 out, work, x_four, y_two, z_two):
    info = Tables(place, source, level, quadrant)
    stream(info, post2, (both, low, high, far, below, above), out, work, x_four, y_two, z_two)


def bar_kernel(pbar, w_in_t, a0_far, fbar, a0, sems):
    copies = Copies(sems)
    for step in range(CHUNKS):
        copies.start(a0_far.at[:, span(step)], a0.at[:, span(step)])
    for step in range(CHUNKS):
        copies.made[step].wait()
        put_cells(fbar, step, cells_of(pbar, step) + dot(w_in_t[...], a0[:, span(step)]))


def unpack_kernel(place, mine, other, g_in, g_mid, g_out, whole):
    scale = float(NB * NZ * CELLS) ** -0.5
    core = place[0] & 1
    whole[pl.ds(pl.multiple_of(core * HALF, HALF), HALF), :] = mine[...]
    whole[pl.ds(pl.multiple_of((1 - core) * HALF, HALF), HALF), :] = other[...]
    for j in range(4):
        cols = pl.ds(j * 128, 128)
        g_mid[:, cols] = whole[pl.ds(j * HID, HID), :] * scale
        g_out[:, cols] = whole[pl.ds(OUT_AT + 24 * j, Q), :] * scale
        g_in[:, cols] = whole[pl.ds(IN_AT + 24 * j, Q), :] * scale


BLOCK = (Q, ROWS, 128)
HIDDEN = (HID, CELLS)
THIN = (Q, CELLS)
SENDS = [(2, 2, 2, 8, 128), (128, 128), (2, ROWS, 128)]
FACES = [(2, 2, 8, 128), (2, 16, 128), (2, ROWS, 128)]


def run(kernel, tables, args, outs, scratch, mflops, hbm=()):
    def shape(s):
        return jax.ShapeDtypeStruct(s, F32) if isinstance(s, tuple) else s

    def buffer(s):
        return pltpu.VMEM(s, F32) if isinstance(s, tuple) else s

    def out_spec(s):
        far = not isinstance(s, (tuple, jax.ShapeDtypeStruct))
        return pl.BlockSpec(memory_space=pltpu.HBM if far else pltpu.VMEM)

    args = list(args)
    in_specs = [pl.BlockSpec(memory_space=pltpu.SMEM)] * len(tables)
    for i in range(len(args)):
        if i in hbm:
            args[i] = pltpu.with_memory_space_constraint(args[i], pltpu.HBM)
        in_specs.append(pl.BlockSpec(memory_space=pltpu.HBM if i in hbm else pltpu.VMEM))
    return pl.pallas_call(
        kernel,
        out_shape=[shape(s) for s in outs],
        in_specs=in_specs,
        out_specs=[out_spec(s) for s in outs],
        scratch_shapes=[buffer(s) for s in scratch],
        compiler_params=pltpu.CompilerParams(vmem_limit_bytes=VMEM_LIMIT),
        cost_estimate=pl.CostEstimate(
            flops=mflops * 1000000, bytes_accessed=1 << 20, transcendentals=0
        ),
    )(*tables, *args)


def send(value, target):
    pairs = [
        (b * NZ + z, nb % NB * NZ + nz % NZ)
        for b in range(NB)
        for z in range(NZ)
        for nb, nz in [target(b, z)]
    ]
    return lax.ppermute(value, AXES, pairs)


def exchange(xs, xys, zs):
    x = xs.reshape(64, 128)
    below = send(zs, lambda b, z: (b, z + 1))
    above = send(zs, lambda b, z: (b, z - 1))
    both = send(xys, lambda b, z: (b ^ 1, z))
    far = send(x, lambda b, z: (b - 3 if b % 2 == 0 else b + 3, z))
    pair = jnp.concatenate([x, both[:64]])
    low = send(pair, lambda b, z: (b + 2, z))
    high = send(pair, lambda b, z: (b - 2, z))
    return both, low, high, far, below, above


def total_over_devices(grads, core, beside):
    def other_core(v):
        return send(v, lambda b, z: (b ^ 1, z))

    halves = grads.reshape(2, HALF, 128)
    mine = lax.dynamic_index_in_dim(halves, core, 0, keepdims=False)
    given = lax.dynamic_index_in_dim(halves, 1 - core, 0, keepdims=False)
    arrived, beside = lax.optimization_barrier((other_core(given), beside))
    mine = (mine + arrived).reshape(64, 1, HALF * 2)
    mine = lax.all_to_all(mine, CHIPS, 0, 0, tiled=True).sum(axis=0, keepdims=True)
    mine = jnp.broadcast_to(mine, (64, 1, HALF * 2))
    mine = lax.all_to_all(mine, CHIPS, 0, 0, tiled=True).reshape(HALF, 128)
    return mine, other_core(mine), beside


def shards(populations, w_in, w_mid, w_out, cotangent, face_source, face_level, face_quadrant):
    f0 = populations.reshape(BLOCK)
    cot = cotangent.reshape(BLOCK)
    w_in_t = w_in.T
    w_mid = w_mid[0]
    w_mid_t = w_mid.T
    place = lax.axis_index(BLOCKS).astype(jnp.int32).reshape(1)
    tables = [place, face_source.T, face_level[0], face_quadrant[0]]
    hidden = pltpu.HBM(HIDDEN, BF16)
    thin = jax.ShapeDtypeStruct(THIN, BF16)
    grad = (GROWS, 128)
    near = pltpu.VMEM(HIDDEN, BF16)
    near_thin = pltpu.VMEM(THIN, BF16)
    sems = pltpu.SemaphoreType.DMA

    post1, local2, *sends, h0, h1 = run(
        first_kernel, tables[:1], [*tables[1:], f0, cot, w_in_t, w_mid, w_out],
        [BLOCK, BLOCK, *SENDS, hidden, hidden],
        [pltpu.SMEM((4, NB), jnp.int32), pltpu.SMEM((1, 6), jnp.int32),
         pltpu.SMEM((1, 6), jnp.int32),
         BLOCK, BLOCK, pltpu.VMEM((Q, HID), BF16), pltpu.VMEM((HID, HID), BF16),
         pltpu.VMEM((Q, HID), BF16), near, near, BLOCK, *FACES[1:], sems((8,)),
         sems((2 * CHUNKS,))],
        4000, range(8),
    )
    got = exchange(*sends)
    post2, local1, *sends, x2, e2, h0_2, h1_2, a0_2, a1_2 = run(
        second_kernel, tables, [post1, local2, *got, w_in_t, w_mid, w_mid_t, w_out],
        [BLOCK, BLOCK, *SENDS, thin, thin, hidden, hidden, hidden, hidden],
        [near] * 4 + [BLOCK] * 4 + FACES + [sems((4 * CHUNKS,))], 10000,
    )
    got = exchange(*sends)
    (grads2,) = run(
        grads_kernel, [], [x2, e2, h0_2, h1_2, a0_2, a1_2], [grad],
        [near] * 4 + [sems((4 * CHUNKS,))], 4000, (2, 3, 4, 5),
    )
    grads, pbar1, a0 = run(
        third_kernel, tables, [f0, local1, *got, w_mid_t, w_out, grads2, h0, h1],
        [grad, BLOCK, hidden],
        [near] * 4 + [near_thin] * 2 + [*FACES[:2], sems((3 * CHUNKS,))],
        8000, (11, 12),
    )
    post2, grads = lax.optimization_barrier((post2, grads))
    (final,) = run(final_kernel, tables, [post2, *got], [BLOCK], [BLOCK, *FACES], 500)
    (fbar0,) = run(
        bar_kernel, [], [pbar1, w_in_t, a0], [BLOCK], [near, sems((CHUNKS,))], 500, (2,)
    )
    mine, other, final = total_over_devices(grads, place[0] % 2, final)
    g_in, g_mid, g_out = run(
        unpack_kernel, [place], [mine, other], [(Q, HID), (HID, HID), (Q, HID)], [grad], 10
    )
    whole = (Q, 1, 1, CELLS)
    return final.reshape(whole), fbar0.reshape(whole), g_in.T, g_mid[None], g_out


def solution(mesh):
    cells = P(None, "slab", BLOCKS, None)
    local = P("slab", BLOCKS, None)
    split = Mesh(mesh.devices.reshape(NX, NX, 2, NZ), AXES)
    return jax.shard_map(
        shards,
        mesh=split,
        in_specs=(cells, P(), P(), P(), cells, P(), local, local),
        out_specs=(cells, cells, P(), P(), P()),
        check_vma=False,
    )
```

time: 135 us -> 112 us (0.83)
  blocking collectives: 0 us -> 32.7 us
  starting transfers between devices: 49.2 us -> 28.1 us
  waiting for transfers between devices: 19.7 us -> 2.04 us
  between operations: 16.5 us -> 0.89 us
  local copies, waits for them, and re-layouts: 11.8 us -> 1.32 us
  Pallas kernels: 37.1 us -> 44.8 us
    all_to_all x0 -> x2, blocking collectives: none -> 32.7 us  [the longest x1 16.6 us: total_over_devices(): lax.all_to_all(mine, CHIPS, 0, 0, tiled=True).sum(axis=0, keepdims=True)]
    ppermute x33 -> x14, starting transfers between devices: 49.2 us -> 28.1 us  [send(): return lax.ppermute(value, AXES, pairs)]
    ppermute x33 -> x14, waiting for transfers between devices: 19.7 us -> 2.04 us  [send(): return lax.ppermute(value, AXES, pairs)]
    unnamed x27 -> x19, local copies, waits for them, and re-layouts: 9.63 us -> 0.96 us
    pallas_call x5 -> x7, Pallas kernels: 37.1 us -> 44.8 us  [run(): pl.pallas_call(kernel, out_shape=[shape(s) for s in outs], in_specs=in_sp...]
  transfers between devices with their start and end apart: 33 -> 14, of which waited for: 11 -> 3; matrix products, arithmetic and copies ran while one was open for 1% -> 0% of each run, Pallas kernels for 1% -> 11%
where the time goes in v1:
time: 112 us; the launch traced here: 111 us
  Pallas kernels  44.8 us (40%)
  blocking collectives  32.7 us (29%)
  starting transfers between devices  28.1 us (25%)
  waiting for transfers between devices  2.04 us (2%)
  other arithmetic  1.49 us (1%)
  local copies, waits for them, and re-layouts  1.32 us (1%)
    pallas_call x7, Pallas kernels, run(): pl.pallas_call(kernel, out_shape=[shape(s) for s in outs], in_specs=in_sp...  44.8 us
    ppermute x14, starting transfers between devices, send(): return lax.ppermute(value, AXES, pairs)  28.1 us
    all_to_all x1, blocking collectives, total_over_devices(): lax.all_to_all(mine, CHIPS, 0, 0, tiled=True).sum(axis=0, keepdims=True)  16.6 us
    all_to_all x1, blocking collectives, total_over_devices(): mine = lax.all_to_all(mine, CHIPS, 0, 0, tiled=True).reshape(HALF, 128)  16.1 us
  transfers between devices with their start and end apart: 14, of which 3 were waited for; matrix products, arithmetic and copies ran while one was open for 0% of the time, Pallas kernels for 11%

profile of v1, /device:TPU:1, one launch (start us, length us, event | category | flops | bytes accessed | tf_op | source)
XLA Modules:
  0.0 111.3 jit_solution(9602518863441327484)
XLA Ops:
  0.7 7.3 %shard_map.119 = (f32[19,32,128]{2,1,0:T(8,128)S(1)}, f32[19,32,128]{2,1,0:T(8,128)S(1)}, f32[2,2,2,8,128]{4,3,2,1,0:T(8,128)S(1)}, f32[128,128]{1,0:T(8,128)S(1...) custom-call(s32[1]{0:T(128)} %bitcast.place, s32[4,32]{1,0:T(4,128)} %bitcast.41, ...), custom_call_target="tpu_custom_call" | custom-call | flops 4000000000 | bytes 1048576 | tf_op jit(solution)/shard_map/pallas_call | solution.py:604
  8.0 1.5 %collective-permute-start = (f32[128,128]{1,0:T(8,128)S(1)}, f32[128,128]{1,0:T(8,128)S(1)}, u32[]{:S(2)}, u32[]{:S(2)}) collective-permute-start(f32[128,128]{1,0:T(8,128)S(1)} %get-tuple-element.35), channel_id=1, source_target_pairs={{0,4},{1,5},{2,6},{3,7},{4,0},{5,1},{6,2},{7,3},{8,12},{9,13},{10,... | collective-permute-start | bytes 196616 | tf_op jit(solution)/shard_map/ppermute | solution.py:624
  9.5 0.9 collective-permute-done.both
  10.4 1.4 %collective-permute-start.1 = (f32[128,128]{1,0:T(8,128)S(1)}, f32[128,128]{1,0:T(8,128)S(1)}, u32[]{:S(2)}, u32[]{:S(2)}) collective-permute-start(f32[128,128]{1,0:T(8,128)S(1)} %pad_maximum_fusion), channel_id=1, source_target_pairs={{0,8},{1,9},{2,10},{3,11},{4,12},{5,13},{6,14},{7,15},{8,16},{9,17... | collective-permute-start | bytes 196616 | tf_op jit(solution)/shard_map/ppermute | solution.py:624
  11.9 3.7 %collective-permute-start.2 = (f32[128,128]{1,0:T(8,128)S(1)}, f32[128,128]{1,0:T(8,128)S(1)}, u32[]{:S(2)}, u32[]{:S(2)}) collective-permute-start(f32[128,128]{1,0:T(8,128)S(1)} %pad_maximum_fusion), channel_id=1, source_target_pairs={{0,120},{1,121},{2,122},{3,123},{4,124},{5,125},{6,126},{7,127},{8... | collective-permute-start | bytes 196616 | tf_op jit(solution)/shard_map/ppermute | solution.py:624
  15.6 0.2 collective-permute-start.3
  15.8 1.6 %collective-permute-start.4 = (f32[2,32,128]{2,1,0:T(8,128)S(1)}, f32[2,32,128]{2,1,0:T(8,128)S(1)}, u32[]{:S(2)}, u32[]{:S(2)}) collective-permute-start(f32[2,32,128]{2,1,0:T(8,128)S(1)} %get-tuple-element.37), channel_id=1, source_target_pairs={{0,1},{1,2},{2,3},{3,0},{4,5},{5,6},{6,7},{7,4},{8,9},{9,10},{10,1... | collective-permute-start | bytes 98312 | tf_op jit(solution)/shard_map/ppermute | solution.py:624
  17.4 2.1 %collective-permute-start.5 = (f32[2,32,128]{2,1,0:T(8,128)S(1)}, f32[2,32,128]{2,1,0:T(8,128)S(1)}, u32[]{:S(2)}, u32[]{:S(2)}) collective-permute-start(f32[2,32,128]{2,1,0:T(8,128)S(1)} %get-tuple-element.37), channel_id=1, source_target_pairs={{0,3},{1,0},{2,1},{3,2},{4,7},{5,4},{6,5},{7,6},{8,11},{9,8},{10,9... | collective-permute-start | bytes 98312 | tf_op jit(solution)/shard_map/ppermute | solution.py:624
  19.5 0.2 copy.23
  19.8 0.7 collective-permute-done.3.far
  20.5 0.4 collective-permute-done.4.below
  20.9 12.5 %shard_map.120 = (f32[19,32,128]{2,1,0:T(8,128)S(1)}, f32[19,32,128]{2,1,0:T(8,128)S(1)}, f32[2,2,2,8,128]{4,3,2,1,0:T(8,128)S(1)}, f32[128,128]{1,0:T(8,128)S(1...) custom-call(s32[1]{0:T(128)} %bitcast.place, ...), custom_call_target="tpu_custom_call" | custom-call | flops 10000000000 | bytes 1048576 | tf_op jit(solution)/shard_map/pallas_call | solution.py:604
  33.4 0.7 copy-done.7
  34.1 2.7 %collective-permute-start.6 = (f32[128,128]{1,0:T(8,128)S(1)}, f32[128,128]{1,0:T(8,128)S(1)}, u32[]{:S(2)}, u32[]{:S(2)}) collective-permute-start(f32[128,128]{1,0:T(8,128)S(1)} %get-tuple-element.40), channel_id=1, source_target_pairs={{0,4},{1,5},{2,6},{3,7},{4,0},{5,1},{6,2},{7,3},{8,12},{9,13},{10,... | collective-permute-start | bytes 196616 | tf_op jit(solution)/shard_map/ppermute | solution.py:624
  36.8 1.5 %collective-permute-start.10 = (f32[2,32,128]{2,1,0:T(8,128)S(1)}, f32[2,32,128]{2,1,0:T(8,128)S(1)}, u32[]{:S(2)}, u32[]{:S(2)}) collective-permute-start(f32[2,32,128]{2,1,0:T(8,128)S(1)} %get-tuple-element.42), channel_id=1, source_target_pairs={{0,1},{1,2},{2,3},{3,0},{4,5},{5,6},{6,7},{7,4},{8,9},{9,10},{10,1... | collective-permute-start | bytes 98312 | tf_op jit(solution)/shard_map/ppermute | solution.py:624
  38.3 2.0 %collective-permute-start.11 = (f32[2,32,128]{2,1,0:T(8,128)S(1)}, f32[2,32,128]{2,1,0:T(8,128)S(1)}, u32[]{:S(2)}, u32[]{:S(2)}) collective-permute-start(f32[2,32,128]{2,1,0:T(8,128)S(1)} %get-tuple-element.42), channel_id=1, source_target_pairs={{0,3},{1,0},{2,1},{3,2},{4,7},{5,4},{6,5},{7,6},{8,11},{9,8},{10,9... | collective-permute-start | bytes 98312 | tf_op jit(solution)/shard_map/ppermute | solution.py:624
  40.3 1.1 collective-permute-start.9
  41.4 0.1 collective-permute-start.7
  41.5 4.8 %collective-permute-start.8 = (f32[128,128]{1,0:T(8,128)S(1)}, f32[128,128]{1,0:T(8,128)S(1)}, u32[]{:S(2)}, u32[]{:S(2)}) collective-permute-start(f32[128,128]{1,0:T(8,128)S(1)} %pad_maximum_fusion.1), channel_id=1, source_target_pairs={{0,120},{1,121},{2,122},{3,123},{4,124},{5,125},{6,126},{7,127},{8... | collective-permute-start | bytes 196616 | tf_op jit(solution)/shard_map/ppermute | solution.py:624
  46.2 7.5 %shard_map.121.grads2 = f32[2304,128]{1,0:T(8,128)S(1)} custom-call(bf16[19,4096]{1,0:T(8,128)(2,1)S(1)} %get-tuple-element.43.x, bf16[19,4096]{1,0:T(8,128)(2,1)S(1)} %get-tuple-element.44.e, bf16[512,4096]{1,0:T(8,128)(2,1)} %get-tuple-element.45.h0_far, bf16[512,4096]{1,0:T(8,128)(2,1)} %get-tuple-element.46.h1_far, ...), custom_call_target="tpu_custom_call" | custom-call | flops 4000000000 | bytes 1048576 | tf_op jit(solution)/shard_map/pallas_call | solution.py:604
  53.9 11.3 %shard_map.122 = (f32[2304,128]{1,0:T(8,128)S(1)}, f32[19,32,128]{2,1,0:T(8,128)S(1)}, bf16[512,4096]{1,0:T(8,128)(2,1)}) custom-call(s32[1]{0:T(128)} %bitcast.place, s32[4,32]{1,0:T(4,128)S(1)} %bitcast.43, s32[1,6]{1,0:T(1,128)S(1)} %bitcast.47, s32[1,6]{1,0:T(1,128)S(1)} %bitcast.51, f32[19,32,128]{2,1,0:T(8,128)S(1)} %bitcast.40, ...), custom_call_target="tpu_custom_call" | custom-call | flops 8000000000 | bytes 1048576 | tf_op jit(solution)/shard_map/pallas_call | solution.py:604
  65.2 1.9 %collective-permute-start.12 = (f32[1152,128]{1,0:T(8,128)S(1)}, f32[1152,128]{1,0:T(8,128)}, u32[]{:S(2)}, u32[]{:S(2)}) collective-permute-start(f32[1152,128]{1,0:T(8,128)S(1)} %dynamic-slice_bitcast_fusion), channel_id=1, source_target_pairs={{0,4},{1,5},{2,6},{3,7},{4,0},{5,1},{6,2},{7,3},{8,12},{9,13},{10,... | collective-permute-start | bytes 1769480 | tf_op jit(solution)/shard_map/ppermute | solution.py:624
  67.1 1.7 %shard_map.123 = f32[19,32,128]{2,1,0:T(8,128)} custom-call(s32[1]{0:T(128)} %bitcast.place, s32[4,32]{1,0:T(4,128)S(1)} %bitcast.44, s32[1,6]{1,0:T(1,128)S(1)} %bitcast.48, s32[1,6]{1,0:T(1,128)S(1)} %bitcast.52, f32[19,32,128]{2,1,0:T(8,128)S(1)} %get-tuple-element.53.post2, f32[128,128]{1,0:T(8,128)S(1)} %collective-permute-done.6.both, ...), custom_call_target="tpu_custom_call" | custom-call | flops 500000000 | bytes 1048576 | tf_op jit(solution)/shard_map/pallas_call | solution.py:604
  68.9 0.0 collective-permute-done.12
  68.9 1.1 %bitcast_add_fusion = f32[1152,128]{1,0:T(8,128)S(1)} fusion(f32[1152,128]{1,0:T(8,128)} %collective-permute-done.12, f32[2,1152,128]{2,1,0:T(8,128)S(1)} %bitcast.27, s32[]{:T(128)S(6)} %select_n.16), kind=kLoop, calls=%fused_computation | loop fusion | flops 147456 | bytes 1769476 | tf_op jit(solution)/shard_map/add | solution.py:647
  70.0 16.6 %all_to_all.10 = f32[64,1,2304]{2,1,0:T(1,128)S(1)} all-to-all(f32[64,1,2304]{2,1,0:T(1,128)S(1)} %bitcast.53), channel_id=1, replica_groups=mesh['bx'=4,'by'=4,'core'=2,'slab'=4] {'bx','by','slab'}, dimensions={0} | all-to-all | bytes 1179648 | tf_op jit(solution)/shard_map/all_to_all | solution.py:648
  86.7 0.4 reduce_sum.9
  87.0 0.3 broadcast_in_dim.4
  87.3 16.1 %all_to_all.11 = f32[64,1,2304]{2,1,0:T(1,128)S(1)} all-to-all(f32[64,1,2304]{2,1,0:T(1,128)S(1)} %broadcast_in_dim.4), channel_id=1, replica_groups=mesh['bx'=4,'by'=4,'core'=2,'slab'=4] {'bx','by','slab'}, dimensions={0} | all-to-all | bytes 1179648 | tf_op jit(solution)/shard_map/all_to_all | solution.py:650
  103.4 3.4 %collective-permute-start.13 = (f32[1152,128]{1,0:T(8,128)S(1)}, f32[1152,128]{1,0:T(8,128)S(1)}, u32[]{:S(2)}, u32[]{:S(2)}) collective-permute-start(f32[1152,128]{1,0:T(8,128)S(1)} %bitcast.24), channel_id=1, source_target_pairs={{0,4},{1,5},{2,6},{3,7},{4,0},{5,1},{6,2},{7,3},{8,12},{9,13},{10,... | collective-permute-start | bytes 1769480 | tf_op jit(solution)/shard_map/ppermute | solution.py:624
  106.8 3.2 %shard_map.124 = f32[19,32,128]{2,1,0:T(8,128)} custom-call(f32[19,32,128]{2,1,0:T(8,128)S(1)} %get-tuple-element.55.pbar, bf16[19,512]{1,0:T(8,128)(2,1)S(1)} %bitcast.38, bf16[512,4096]{1,0:T(8,128)(2,1)} %get-tuple-element.56.a0_far), custom_call_target="tpu_custom_call" | custom-call | flops 500000000 | bytes 1048576 | tf_op jit(solution)/shard_map/pallas_call | solution.py:604
  110.1 1.2 %shard_map.125 = (f32[19,512]{1,0:T(8,128)}, f32[512,512]{1,0:T(8,128)}, f32[19,512]{1,0:T(8,128)}) custom-call(s32[1]{0:T(128)} %bitcast.place, f32[1152,128]{1,0:T(8,128)S(1)} %bitcast.25, f32[1152,128]{1,0:T(8,128)S(1)} %collective-permute-done.13.other), custom_call_target="tpu_custom_call" | custom-call | flops 10000000 | bytes 1048576 | tf_op jit(solution)/shard_map/pallas_call | solution.py:604
  (32 shorter events, 0.1 us)
Async XLA Ops:
  0.6 18.9 %copy-start = (bf16[1,512,512]{2,1,0:T(8,128)(2,1)S(1)}, bf16[1,512,512]{2,1,0:T(8,128)(2,1)}, u32[]{:S(2)}) copy-start(bf16[1,512,512]{2,1,0:T(8,128)(2,1)} %param.10) | copy-start | bytes 1572868
  0.7 20.2 %copy-start.1 = (bf16[512,19]{0,1:T(8,128)(2,1)S(1)}, bf16[512,19]{0,1:T(8,128)(2,1)}, u32[]{:S(2)}) copy-start(bf16[512,19]{0,1:T(8,128)(2,1)} %param.9) | copy-start | bytes 58372
  0.7 20.2 %copy-start.3 = (bf16[19,512]{1,0:T(8,128)(2,1)S(1)}, bf16[19,512]{1,0:T(8,128)(2,1)}, u32[]{:S(2)}) copy-start(bf16[19,512]{1,0:T(8,128)(2,1)} %w_out.3) | copy-start | bytes 58372
  0.7 20.2 %copy-start.4 = (s32[32,4]{0,1:T(4,128)S(1)}, s32[32,4]{0,1:T(4,128)}, u32[]{:S(2)}) copy-start(s32[32,4]{0,1:T(4,128)} %param.13) | copy-start | bytes 1540
  0.7 20.2 %copy-start.5 = (s32[1,1,6]{2,1,0:T(1,128)S(1)}, s32[1,1,6]{2,1,0:T(1,128)}, u32[]{:S(2)}) copy-start(s32[1,1,6]{2,1,0:T(1,128)} %param.14) | copy-start | bytes 76
  0.7 20.2 %copy-start.6 = (s32[1,1,6]{2,1,0:T(1,128)S(1)}, s32[1,1,6]{2,1,0:T(1,128)}, u32[]{:S(2)}) copy-start(s32[1,1,6]{2,1,0:T(1,128)} %param.15) | copy-start | bytes 76
  8.0 2.4 %collective-permute-start = (f32[128,128]{1,0:T(8,128)S(1)}, f32[128,128]{1,0:T(8,128)S(1)}, u32[]{:S(2)}, u32[]{:S(2)}) collective-permute-start(f32[128,128]{1,0:T(8,128)S(1)} %get-tuple-element.35), channel_id=1, source_target_pairs={{0,4},{1,5},{2,6},{3,7},{4,0},{5,1},{6,2},{7,3},{8,12},{9,13},{10,... | collective-permute-start | bytes 196616 | tf_op jit(solution)/shard_map/ppermute | solution.py:624
  10.4 10.4 %collective-permute-start.1 = (f32[128,128]{1,0:T(8,128)S(1)}, f32[128,128]{1,0:T(8,128)S(1)}, u32[]{:S(2)}, u32[]{:S(2)}) collective-permute-start(f32[128,128]{1,0:T(8,128)S(1)} %pad_maximum_fusion), channel_id=1, source_target_pairs={{0,8},{1,9},{2,10},{3,11},{4,12},{5,13},{6,14},{7,15},{8,16},{9,17... | collective-permute-start | bytes 196616 | tf_op jit(solution)/shard_map/ppermute | solution.py:624
  11.9 9.0 %collective-permute-start.2 = (f32[128,128]{1,0:T(8,128)S(1)}, f32[128,128]{1,0:T(8,128)S(1)}, u32[]{:S(2)}, u32[]{:S(2)}) collective-permute-start(f32[128,128]{1,0:T(8,128)S(1)} %pad_maximum_fusion), channel_id=1, source_target_pairs={{0,120},{1,121},{2,122},{3,123},{4,124},{5,125},{6,126},{7,127},{8... | collective-permute-start | bytes 196616 | tf_op jit(solution)/shard_map/ppermute | solution.py:624
  15.6 4.8 %collective-permute-start.3 = (f32[64,128]{1,0:T(8,128)S(1)}, f32[64,128]{1,0:T(8,128)S(1)}, u32[]{:S(2)}, u32[]{:S(2)}) collective-permute-start(f32[64,128]{1,0:T(8,128)S(1)} %bitcast.35), channel_id=1, source_target_pairs={{0,116},{1,117},{2,118},{3,119},{4,16},{5,17},{6,18},{7,19},{8,124... | collective-permute-start | bytes 98312 | tf_op jit(solution)/shard_map/ppermute | solution.py:624
  15.8 5.1 %collective-permute-start.4 = (f32[2,32,128]{2,1,0:T(8,128)S(1)}, f32[2,32,128]{2,1,0:T(8,128)S(1)}, u32[]{:S(2)}, u32[]{:S(2)}) collective-permute-start(f32[2,32,128]{2,1,0:T(8,128)S(1)} %get-tuple-element.37), channel_id=1, source_target_pairs={{0,1},{1,2},{2,3},{3,0},{4,5},{5,6},{6,7},{7,4},{8,9},{9,10},{10,1... | collective-permute-start | bytes 98312 | tf_op jit(solution)/shard_map/ppermute | solution.py:624
  17.4 3.4 %collective-permute-start.5 = (f32[2,32,128]{2,1,0:T(8,128)S(1)}, f32[2,32,128]{2,1,0:T(8,128)S(1)}, u32[]{:S(2)}, u32[]{:S(2)}) collective-permute-start(f32[2,32,128]{2,1,0:T(8,128)S(1)} %get-tuple-element.37), channel_id=1, source_target_pairs={{0,3},{1,0},{2,1},{3,2},{4,7},{5,4},{6,5},{7,6},{8,11},{9,8},{10,9... | collective-permute-start | bytes 98312 | tf_op jit(solution)/shard_map/ppermute | solution.py:624
  33.4 0.7 copy-start.7
  34.1 7.3 %collective-permute-start.6 = (f32[128,128]{1,0:T(8,128)S(1)}, f32[128,128]{1,0:T(8,128)S(1)}, u32[]{:S(2)}, u32[]{:S(2)}) collective-permute-start(f32[128,128]{1,0:T(8,128)S(1)} %get-tuple-element.40), channel_id=1, source_target_pairs={{0,4},{1,5},{2,6},{3,7},{4,0},{5,1},{6,2},{7,3},{8,12},{9,13},{10,... | collective-permute-start | bytes 196616 | tf_op jit(solution)/shard_map/ppermute | solution.py:624
  36.8 17.0 %collective-permute-start.10 = (f32[2,32,128]{2,1,0:T(8,128)S(1)}, f32[2,32,128]{2,1,0:T(8,128)S(1)}, u32[]{:S(2)}, u32[]{:S(2)}) collective-permute-start(f32[2,32,128]{2,1,0:T(8,128)S(1)} %get-tuple-element.42), channel_id=1, source_target_pairs={{0,1},{1,2},{2,3},{3,0},{4,5},{5,6},{6,7},{7,4},{8,9},{9,10},{10,1... | collective-permute-start | bytes 98312 | tf_op jit(solution)/shard_map/ppermute | solution.py:624
  38.3 15.5 %collective-permute-start.11 = (f32[2,32,128]{2,1,0:T(8,128)S(1)}, f32[2,32,128]{2,1,0:T(8,128)S(1)}, u32[]{:S(2)}, u32[]{:S(2)}) collective-permute-start(f32[2,32,128]{2,1,0:T(8,128)S(1)} %get-tuple-element.42), channel_id=1, source_target_pairs={{0,3},{1,0},{2,1},{3,2},{4,7},{5,4},{6,5},{7,6},{8,11},{9,8},{10,9... | collective-permute-start | bytes 98312 | tf_op jit(solution)/shard_map/ppermute | solution.py:624
  40.3 13.5 %collective-permute-start.9 = (f32[64,128]{1,0:T(8,128)S(1)}, f32[64,128]{1,0:T(8,128)S(1)}, u32[]{:S(2)}, u32[]{:S(2)}) collective-permute-start(f32[64,128]{1,0:T(8,128)S(1)} %bitcast.32), channel_id=1, source_target_pairs={{0,116},{1,117},{2,118},{3,119},{4,16},{5,17},{6,18},{7,19},{8,124... | collective-permute-start | bytes 98312 | tf_op jit(solution)/shard_map/ppermute | solution.py:624
  41.4 12.4 %collective-permute-start.7 = (f32[128,128]{1,0:T(8,128)S(1)}, f32[128,128]{1,0:T(8,128)S(1)}, u32[]{:S(2)}, u32[]{:S(2)}) collective-permute-start(f32[128,128]{1,0:T(8,128)S(1)} %pad_maximum_fusion.1), channel_id=1, source_target_pairs={{0,8},{1,9},{2,10},{3,11},{4,12},{5,13},{6,14},{7,15},{8,16},{9,17... | collective-permute-start | bytes 196616 | tf_op jit(solution)/shard_map/ppermute | solution.py:624
  41.5 12.4 %collective-permute-start.8 = (f32[128,128]{1,0:T(8,128)S(1)}, f32[128,128]{1,0:T(8,128)S(1)}, u32[]{:S(2)}, u32[]{:S(2)}) collective-permute-start(f32[128,128]{1,0:T(8,128)S(1)} %pad_maximum_fusion.1), channel_id=1, source_target_pairs={{0,120},{1,121},{2,122},{3,123},{4,124},{5,125},{6,126},{7,127},{8... | collective-permute-start | bytes 196616 | tf_op jit(solution)/shard_map/ppermute | solution.py:624
  46.2 7.6 %copy-start.2 = (f32[19,1,1,4096]{3,2,1,0:T(1,128)S(1)}, f32[19,1,1,4096]{3,2,1,0:T(1,128)}, u32[]{:S(2)}) copy-start(f32[19,1,1,4096]{3,2,1,0:T(1,128)} %param.8) | copy-start | bytes 933892
  46.2 7.6 %copy-start.8 = (f32[19,32,128]{2,1,0:T(8,128)S(1)}, f32[19,32,128]{2,1,0:T(8,128)}, u32[]{:S(2)}) copy-start(f32[19,32,128]{2,1,0:T(8,128)} %copy-done.7) | copy-start | bytes 933892
  65.2 3.7 %collective-permute-start.12 = (f32[1152,128]{1,0:T(8,128)S(1)}, f32[1152,128]{1,0:T(8,128)}, u32[]{:S(2)}, u32[]{:S(2)}) collective-permute-start(f32[1152,128]{1,0:T(8,128)S(1)} %dynamic-slice_bitcast_fusion), channel_id=1, source_target_pairs={{0,4},{1,5},{2,6},{3,7},{4,0},{5,1},{6,2},{7,3},{8,12},{9,13},{10,... | collective-permute-start | bytes 1769480 | tf_op jit(solution)/shard_map/ppermute | solution.py:624
  103.4 6.7 %collective-permute-start.13 = (f32[1152,128]{1,0:T(8,128)S(1)}, f32[1152,128]{1,0:T(8,128)S(1)}, u32[]{:S(2)}, u32[]{:S(2)}) collective-permute-start(f32[1152,128]{1,0:T(8,128)S(1)} %bitcast.24), channel_id=1, source_target_pairs={{0,4},{1,5},{2,6},{3,7},{4,0},{5,1},{6,2},{7,3},{8,12},{9,13},{10,... | collective-permute-start | bytes 1769480 | tf_op jit(solution)/shard_map/ppermute | solution.py:624

commit v2 on v1

--- a/solution.py
+++ b/solution.py
@@ -21,7 +21,6 @@
 CHIPS = ("bx", "by", "slab")
 F32 = jnp.float32
 BF16 = jnp.bfloat16
-VMEM_LIMIT = 32 * 1024 * 1024
 GROWS = 2304
 HALF = GROWS // 2
 OUT_AT = 4 * HID
@@ -260,23 +259,35 @@
     return jnp.where(iota(ROWS, 1) & 15 < 8, z_two[0], z_two[1])
 
 
-def choose_x(info, face, both, low, high, far, kind):
+def choose_x(info, face, got, kind):
+    swapped, x_got, z_got, far, passed = got
     d = info.distance(face)
     even = info.block() & 1 == 0
+
+    def at(distance):
+        return jnp.where(even, distance % NB, -distance % NB)
+
     cases = [
-        (jnp.where(even, 1, NB - 1), both, 0),
-        (NB - 2, low, 0),
-        (jnp.where(even, NB - 1, NB - 3), low, 64),
-        (2, high, 0),
-        (jnp.where(even, 3, 1), high, 64),
-        (jnp.where(even, NB - 3, 3), far, 0),
+        (at(1), swapped, 0),
+        (at(-2), x_got, 0),
+        (at(-1), x_got, 64),
+        (at(3), passed, 0),
+        (at(2), passed, 64),
+        (at(-3), far, 0),
     ]
     return lambda f, r: sum_where(
         [
-            (d == spot, ref[pl.ds(at + 8 * (kind * 4 + f * 2 + r), 8), :])
-            for spot, ref, at in cases
+            (d == spot, ref[pl.ds(start + 8 * (kind * 4 + f * 2 + r), 8), :])
+            for spot, ref, start in cases
         ]
     )
+
+
+def choose_z(info, got, kind):
+    direct = got[2][pl.ds(32 * kind, 32), :]
+    passed = got[4][pl.ds(128 + 32 * kind, 32), :]
+    even = info.block() & 1 == 0
+    return jnp.where(even, direct, passed), jnp.where(even, passed, direct)
 
 
 def sum_where(cases):
@@ -286,7 +297,7 @@
     return total
 
 
-def stream_back(info, bar, local, xs, xys, zs, work, y_two, z_two):
+def stream_back(info, bar, local, xs, sends, work, y_two, z_two):
     for q in range(Q):
         v = bar[q]
         if is_edge(q):
@@ -308,9 +319,9 @@
     pack_faces(work, put_x, put_y, put_z)
     gather_x(info, x_four)
     gather_y(info, y_two)
-    zs[1] = gather_z(info, z_two)
-    xys[pl.ds(32, 32), :] = xs[1].reshape(32, 128)
-    xys[pl.ds(96, 32), :] = y_two[...].reshape(32, 128)
+    sends[pl.ds(160, 32), :] = gather_z(info, z_two)
+    sends[pl.ds(32, 32), :] = xs[1].reshape(32, 128)
+    sends[pl.ds(96, 32), :] = y_two[...].reshape(32, 128)
     row, lane = iota(ROWS, 0), iota(ROWS, 1)
     coords = [row >> 1, (row & 1) * 8 + (lane >> 4), lane & 15]
     for q in range(Q):
@@ -328,7 +339,7 @@
         local[q] = v
 
 
-def send_post(post, xs, xys, zs):
+def send_post(post, xs, sends):
     x_four = xs.at[0]
     x_four[...] = jnp.zeros(x_four.shape, F32)
 
@@ -336,27 +347,26 @@
         x_four[f, r, pl.ds(i, 1), :] = v
 
     def put_y(f, v):
-        xys[pl.ds(64 + 16 * f, 16), :] = v
+        sends[pl.ds(64 + 16 * f, 16), :] = v
 
     def put_z(v):
-        zs[0] = v
+        sends[pl.ds(128, 32), :] = v
 
     pack_faces(post, put_x, put_y, put_z)
-    xys[pl.ds(0, 32), :] = xs[0].reshape(32, 128)
+    sends[pl.ds(0, 32), :] = xs[0].reshape(32, 128)
 
 
 def stream(info, post, got, out, work, x_four, y_two, z_two):
-    both, low, high, far, below, above = got
+    swapped = got[0]
     for f in (0, 1):
-        pick = choose_x(info, f ^ 1, both, low, high, far, 0)
+        pick = choose_x(info, f ^ 1, got, 0)
         for r in (0, 1):
             x_four[f, r] = pick(f, r)
     refine_x(info, x_four)
-    y_two[0] = both[pl.ds(64, 16), :]
-    y_two[1] = both[pl.ds(80, 16), :]
+    y_two[0] = swapped[pl.ds(64, 16), :]
+    y_two[1] = swapped[pl.ds(80, 16), :]
     refine_y(info, y_two)
-    z_two[0] = below[0]
-    z_two[1] = above[0]
+    z_two[0], z_two[1] = choose_z(info, got, 0)
     z = refine_z(info, z_two)
     work[...] = post[...]
     unpack_faces(work, lambda f, r, i: x_four[f, r, pl.ds(i, 1), :], y_two, z, False)
@@ -368,14 +378,15 @@
 
 
 def take_back(info, bar, got, x_four, y_two):
-    both, low, high, far, below, above = got
+    swapped = got[0]
     for f in (0, 1):
-        pick = choose_x(info, f, both, low, high, far, 1)
+        pick = choose_x(info, f, got, 1)
         for r in (0, 1):
             x_four[f, r] = pick(f, r)
-    y_two[0] = both[pl.ds(96, 16), :]
-    y_two[1] = both[pl.ds(112, 16), :]
-    z = jnp.where(iota(ROWS, 1) & 15 < 8, above[1], below[1])
+    y_two[0] = swapped[pl.ds(96, 16), :]
+    y_two[1] = swapped[pl.ds(112, 16), :]
+    below, above = choose_z(info, got, 1)
+    z = jnp.where(iota(ROWS, 1) & 15 < 8, above, below)
     unpack_faces(bar, lambda f, r, i: x_four[f, r, pl.ds(i, 1), :], y_two, z, True)
 
 
@@ -449,8 +460,8 @@
 
 
 def first_kernel(place, source_far, level_far, quadrant_far, f0_far, cot_far, w_in_far, w_mid_far,
-                 w_out_far, post, local, xs, xys, zs, h0_far, h1_far,
-                 source, level, quadrant, f0, cot, w_in_t, w_mid, w_out, h0, h1, work, y_two, z_two,
+                 w_out_far, post, local, sends, h0_far, h1_far,
+                 source, level, quadrant, xs, f0, cot, w_in_t, w_mid, w_out, h0, h1, work, y_two, z_two,
                  sems, out_sems):
     info = Tables(place, source, level, quadrant)
     copies = Copies(sems)
@@ -460,7 +471,7 @@
         copies.start(far, near)
     for copy in copies.made[:4]:
         copy.wait()
-    stream_back(info, cot, local, xs, xys, zs, work, y_two, z_two)
+    stream_back(info, cot, local, xs, sends, work, y_two, z_two)
     for copy in copies.made[4:]:
         copy.wait()
     copies = Copies(out_sems)
@@ -471,98 +482,70 @@
         h1[:, span(step)] = b
         copies.start(h1.at[:, span(step)], h1_far.at[:, span(step)])
         put_cells(post, step, out)
-    send_post(post, xs, xys, zs)
+    send_post(post, xs, sends)
     copies.wait()
 
 
-def second_kernel(place, source, level, quadrant, post1, local2, both, low, high, far, below, above,
-                  w_in_t, w_mid, w_mid_t, w_out,
-                  post, local, xs, xys, zs, x, e, h0_far, h1_far, a0_far, a1_far,
-                  h0, h1, a0, a1, f1, pbar, fbar, work, x_four, y_two, z_two, sems):
+def second_kernel(place, source, level, quadrant, post1, local2, swapped, x_got, z_got, far, passed,
+                  w_in_t, w_mid, w_mid_t, w_out, post, local, sends, grads_far,
+                  grads, xs, x, e, h0, h1, a0, a1, f1, pbar, fbar, work, x_four, y_two, z_two, sem):
     info = Tables(place, source, level, quadrant)
-    got = (both, low, high, far, below, above)
+    got = (swapped, x_got, z_got, far, passed)
     stream(info, post1, got, f1, work, x_four, y_two, z_two)
     pbar[...] = local2[...]
     take_back(info, pbar, got, x_four, y_two)
-    copies = Copies(sems)
     for step in range(CHUNKS):
         at = span(step)
         f = cells_of(f1, step)
         h0_now, h1_now, out = forward(f, w_in_t[...], w_mid[...], w_out[...])
         put_cells(post, step, out)
-        x[:, at] = f.astype(BF16)
-        h0[:, at] = h0_now
-        copies.start(h0.at[:, at], h0_far.at[:, at])
-        h1[:, at] = h1_now
-        copies.start(h1.at[:, at], h1_far.at[:, at])
         bar = cells_of(pbar, step)
         e_now, a1_now, a0_now = signals(bar, h0_now, h1_now, w_mid_t[...], w_out[...])
         put_cells(fbar, step, bar + dot(w_in_t[...], a0_now))
+        x[:, at] = f.astype(BF16)
         e[:, at] = e_now
+        h0[:, at] = h0_now
+        h1[:, at] = h1_now
         a1[:, at] = a1_now
-        copies.start(a1.at[:, at], a1_far.at[:, at])
         a0[:, at] = a0_now
-        copies.start(a0.at[:, at], a0_far.at[:, at])
-    send_post(post, xs, xys, zs)
-    stream_back(info, fbar, local, xs, xys, zs, work, y_two, z_two)
+    put_grads(grads, x, e, h0, h1, a0, a1, None)
+    copies = Copies(sem)
+    copies.start(grads, grads_far)
+    send_post(post, xs, sends)
+    stream_back(info, fbar, local, xs, sends, work, y_two, z_two)
     copies.wait()
 
 
-def grads_kernel(x, e, h0_far, h1_far, a0_far, a1_far, grads, h0, h1, a0, a1, sems):
-    copies = Copies(sems)
-    pairs = ((h0_far, h0), (a1_far, a1), (h1_far, h1), (a0_far, a0))
-    for step in range(CHUNKS):
-        for far, near in pairs:
-            copies.start(far.at[:, span(step)], near.at[:, span(step)])
-    for step in range(CHUNKS):
-        for copy in copies.made[4 * step : 4 * step + 4]:
-            copy.wait()
-        at = span(step)
-        put_grads(grads, x.at[:, at], e.at[:, at], h0.at[:, at], h1.at[:, at], a0.at[:, at],
-                  a1.at[:, at], grads if step else None)
-
-
-def third_kernel(place, source, level, quadrant, f0, local1, both, low, high, far, below, above,
-                 w_mid_t, w_out, grads2, h0_far, h1_far,
-                 grads, pbar, a0_far, h0, h1, a0, a1, x, e, x_four, y_two, sems):
+def third_kernel(place, source, level, quadrant, f0, local1, swapped, x_got, z_got, far, passed,
+                 w_in_t, w_mid_t, w_out, grads2_far, h0_far, h1_far,
+                 grads, fbar, pbar, h0, h1, a0, a1, x, e, x_four, y_two, sems):
     info = Tables(place, source, level, quadrant)
-    got = (both, low, high, far, below, above)
     copies = Copies(sems)
     for step in range(CHUNKS):
         for hbm, near in ((h1_far, h1), (h0_far, h0)):
             copies.start(hbm.at[:, span(step)], near.at[:, span(step)])
+    copies.start(grads2_far, grads)
     pbar[...] = local1[...]
-    take_back(info, pbar, got, x_four, y_two)
+    take_back(info, pbar, (swapped, x_got, z_got, far, passed), x_four, y_two)
     for step in range(CHUNKS):
         at = span(step)
         for copy in copies.made[2 * step : 2 * step + 2]:
             copy.wait()
-        e_now, a1_now, a0_now = signals(
-            cells_of(pbar, step), h0[:, at], h1[:, at], w_mid_t[...], w_out[...]
-        )
+        bar = cells_of(pbar, step)
+        e_now, a1_now, a0_now = signals(bar, h0[:, at], h1[:, at], w_mid_t[...], w_out[...])
+        put_cells(fbar, step, bar + dot(w_in_t[...], a0_now))
         x[:, at] = cells_of(f0, step).astype(BF16)
         e[:, at] = e_now
         a1[:, at] = a1_now
         a0[:, at] = a0_now
-        copies.start(a0.at[:, at], a0_far.at[:, at])
-    put_grads(grads, x, e, h0, h1, a0, a1, grads2)
-    for copy in copies.made[2 * CHUNKS :]:
-        copy.wait()
-
-
-def final_kernel(place, source, level, quadrant, post2, both, low, high, far, below, above,
+    copies.made[-1].wait()
+    put_grads(grads, x, e, h0, h1, a0, a1, grads)
+
+
+def final_kernel(place, source, level, quadrant, post2, swapped, x_got, z_got, far, passed,
                  out, work, x_four, y_two, z_two):
     info = Tables(place, source, level, quadrant)
-    stream(info, post2, (both, low, high, far, below, above), out, work, x_four, y_two, z_two)
-
-
-def bar_kernel(pbar, w_in_t, a0_far, fbar, a0, sems):
-    copies = Copies(sems)
-    for step in range(CHUNKS):
-        copies.start(a0_far.at[:, span(step)], a0.at[:, span(step)])
-    for step in range(CHUNKS):
-        copies.made[step].wait()
-        put_cells(fbar, step, cells_of(pbar, step) + dot(w_in_t[...], a0[:, span(step)]))
+    stream(info, post2, (swapped, x_got, z_got, far, passed), out, work, x_four, y_two, z_two)
 
 
 def unpack_kernel(place, mine, other, g_in, g_mid, g_out, whole):
@@ -580,11 +563,12 @@
 BLOCK = (Q, ROWS, 128)
 HIDDEN = (HID, CELLS)
 THIN = (Q, CELLS)
-SENDS = [(2, 2, 2, 8, 128), (128, 128), (2, ROWS, 128)]
+SENDS = (192, 128)
+X_TWO = (2, 2, 2, 8, 128)
 FACES = [(2, 2, 8, 128), (2, 16, 128), (2, ROWS, 128)]
 
 
-def run(kernel, tables, args, outs, scratch, mflops, hbm=()):
+def run(kernel, tables, args, outs, scratch, mflops, megabytes, hbm=()):
     def shape(s):
         return jax.ShapeDtypeStruct(s, F32) if isinstance(s, tuple) else s
 
@@ -607,7 +591,7 @@
         in_specs=in_specs,
         out_specs=[out_spec(s) for s in outs],
         scratch_shapes=[buffer(s) for s in scratch],
-        compiler_params=pltpu.CompilerParams(vmem_limit_bytes=VMEM_LIMIT),
+        compiler_params=pltpu.CompilerParams(vmem_limit_bytes=megabytes << 20),
         cost_estimate=pl.CostEstimate(
             flops=mflops * 1000000, bytes_accessed=1 << 20, transcendentals=0
         ),
@@ -624,16 +608,20 @@
     return lax.ppermute(value, AXES, pairs)
 
 
-def exchange(xs, xys, zs):
-    x = xs.reshape(64, 128)
-    below = send(zs, lambda b, z: (b, z + 1))
-    above = send(zs, lambda b, z: (b, z - 1))
-    both = send(xys, lambda b, z: (b ^ 1, z))
-    far = send(x, lambda b, z: (b - 3 if b % 2 == 0 else b + 3, z))
-    pair = jnp.concatenate([x, both[:64]])
-    low = send(pair, lambda b, z: (b + 2, z))
-    high = send(pair, lambda b, z: (b - 2, z))
-    return both, low, high, far, below, above
+def exchange(sends):
+    swapped = send(sends, lambda b, z: (b ^ 1, z))
+    far = send(sends[:64], lambda b, z: (b - 3 if b % 2 == 0 else b + 3, z))
+    x_got = send(
+        jnp.concatenate([sends[:64], swapped[:64]]),
+        lambda b, z: (b + 2 if b % 2 == 0 else b - 2, z),
+    )
+    z_got = send(
+        jnp.concatenate([sends[128:], swapped[128:]]),
+        lambda b, z: (b, z + 1 if b % 2 == 0 else z - 1),
+    )
+    x_got, z_got, far = lax.optimization_barrier((x_got, z_got, far))
+    passed = send(jnp.concatenate([x_got, z_got[64:]]), lambda b, z: (b ^ 1, z))
+    return swapped, x_got, z_got, far, passed
 
 
 def total_over_devices(grads, core, beside):
@@ -666,41 +654,35 @@
     near_thin = pltpu.VMEM(THIN, BF16)
     sems = pltpu.SemaphoreType.DMA
 
-    post1, local2, *sends, h0, h1 = run(
+    post1, local2, sends, h0, h1 = run(
         first_kernel, tables[:1], [*tables[1:], f0, cot, w_in_t, w_mid, w_out],
-        [BLOCK, BLOCK, *SENDS, hidden, hidden],
+        [BLOCK, BLOCK, SENDS, hidden, hidden],
         [pltpu.SMEM((4, NB), jnp.int32), pltpu.SMEM((1, 6), jnp.int32),
-         pltpu.SMEM((1, 6), jnp.int32),
+         pltpu.SMEM((1, 6), jnp.int32), X_TWO,
          BLOCK, BLOCK, pltpu.VMEM((Q, HID), BF16), pltpu.VMEM((HID, HID), BF16),
          pltpu.VMEM((Q, HID), BF16), near, near, BLOCK, *FACES[1:], sems((8,)),
          sems((2 * CHUNKS,))],
-        4000, range(8),
+        4000, 32, range(8),
     )
-    got = exchange(*sends)
-    post2, local1, *sends, x2, e2, h0_2, h1_2, a0_2, a1_2 = run(
+    got = exchange(sends)
+    post2, local1, sends, grads2 = run(
         second_kernel, tables, [post1, local2, *got, w_in_t, w_mid, w_mid_t, w_out],
-        [BLOCK, BLOCK, *SENDS, thin, thin, hidden, hidden, hidden, hidden],
-        [near] * 4 + [BLOCK] * 4 + FACES + [sems((4 * CHUNKS,))], 10000,
+        [BLOCK, BLOCK, SENDS, pltpu.HBM(grad, F32)],
+        [grad, X_TWO, near_thin, near_thin, *[near] * 4, *[BLOCK] * 4, *FACES, sems((1,))],
+        14000, 32,
     )
-    got = exchange(*sends)
-    (grads2,) = run(
-        grads_kernel, [], [x2, e2, h0_2, h1_2, a0_2, a1_2], [grad],
-        [near] * 4 + [sems((4 * CHUNKS,))], 4000, (2, 3, 4, 5),
-    )
-    grads, pbar1, a0 = run(
-        third_kernel, tables, [f0, local1, *got, w_mid_t, w_out, grads2, h0, h1],
-        [grad, BLOCK, hidden],
-        [near] * 4 + [near_thin] * 2 + [*FACES[:2], sems((3 * CHUNKS,))],
-        8000, (11, 12),
+    got = exchange(sends)
+    grads, fbar0 = run(
+        third_kernel, tables, [f0, local1, *got, w_in_t, w_mid_t, w_out, grads2, h0, h1],
+        [grad, BLOCK],
+        [BLOCK, *[near] * 4, near_thin, near_thin, *FACES[:2], sems((2 * CHUNKS + 1,))],
+        8000, 32, (10, 11, 12),
     )
     post2, grads = lax.optimization_barrier((post2, grads))
-    (final,) = run(final_kernel, tables, [post2, *got], [BLOCK], [BLOCK, *FACES], 500)
-    (fbar0,) = run(
-        bar_kernel, [], [pbar1, w_in_t, a0], [BLOCK], [near, sems((CHUNKS,))], 500, (2,)
-    )
+    (final,) = run(final_kernel, tables, [post2, *got], [BLOCK], [BLOCK, *FACES], 500, 8)
     mine, other, final = total_over_devices(grads, place[0] % 2, final)
     g_in, g_mid, g_out = run(
-        unpack_kernel, [place], [mine, other], [(Q, HID), (HID, HID), (Q, HID)], [grad], 10
+        unpack_kernel, [place], [mine, other], [(Q, HID), (HID, HID), (Q, HID)], [grad], 10, 8
     )
     whole = (Q, 1, 1, CELLS)
     return final.reshape(whole), fbar0.reshape(whole), g_in.T, g_mid[None], g_out

time: 112 us -> 110 us (0.982)
  waiting for transfers between devices: 2.04 us -> 15.9 us
  starting transfers between devices: 28.1 us -> 18 us
  Pallas kernels: 44.8 us -> 37.8 us
  blocking collectives: 32.7 us -> 35.1 us
    ppermute x14 -> x12, waiting for transfers between devices: 2.04 us -> 15.9 us  [send(): return lax.ppermute(value, AXES, pairs)]
    ppermute x14 -> x12, starting transfers between devices: 28.1 us -> 18 us  [send(): return lax.ppermute(value, AXES, pairs)]
    pallas_call x7 -> x5, Pallas kernels: 44.8 us -> 37.8 us  [run(): pl.pallas_call(kernel, out_shape=[shape(s) for s in outs], in_specs=in_sp...]
    all_to_all x1, blocking collectives: 16.6 us -> 19.2 us  [total_over_devices(): lax.all_to_all(mine, CHIPS, 0, 0, tiled=True).sum(axis=0, keepdims=True)]
  transfers between devices with their start and end apart: 14 -> 12, of which waited for: 3 -> 8; matrix products, arithmetic and copies ran while one was open for 0% -> 0% of each run, Pallas kernels for 11% -> 2%
where the time goes in v2:
time: 110 us
  Pallas kernels  37.8 us (34%)
  blocking collectives  35.1 us (32%)
  starting transfers between devices  18 us (16%)
  waiting for transfers between devices  15.9 us (14%)
  other arithmetic  1.52 us (1%)
    pallas_call x5, Pallas kernels, run(): pl.pallas_call(kernel, out_shape=[shape(s) for s in outs], in_specs=in_sp...  37.8 us
    all_to_all x1, blocking collectives, total_over_devices(): lax.all_to_all(mine, CHIPS, 0, 0, tiled=True).sum(axis=0, keepdims=True)  19.2 us
    ppermute x12, starting transfers between devices, send(): return lax.ppermute(value, AXES, pairs)  18 us
    all_to_all x1, blocking collectives, total_over_devices(): mine = lax.all_to_all(mine, CHIPS, 0, 0, tiled=True).reshape(HALF, 128)  15.9 us
    ppermute x12, waiting for transfers between devices, send(): return lax.ppermute(value, AXES, pairs)  15.9 us
  transfers between devices with their start and end apart: 12, of which 8 were waited for; matrix products, arithmetic and copies ran while one was open for 0% of the time, Pallas kernels for 2%

profile of v2, /device:TPU:1, one launch (start us, length us, event | category | flops | bytes accessed | tf_op | source)
XLA Modules:
  0.0 109.7 jit_solution(12095989897809951997)
XLA Ops:
  0.7 7.3 %shard_map.119 = (f32[19,32,128]{2,1,0:T(8,128)S(1)}, f32[19,32,128]{2,1,0:T(8,128)S(1)}, f32[192,128]{1,0:T(8,128)S(1)}, bf16[512,4096]{1,0:T(8,128)(2,1)}, bf16[512,4096]{1,0:T(8,128)(2,1)}) custom-call(s32[1]{0:T(128)} %bitcast.place, s32[4,32]{1,0:T(4,128)} %bitcast.35, s32[1,6]{1,0:T(1,128)} %bitcast.39, s32[1,6]{1,0:T(1,128)} %bitcast.43, ...), custom_call_target="tpu_custom_call" | custom-call | flops 4000000000 | bytes 1048576 | tf_op jit(solution)/shard_map/pallas_call | solution.py:588
  8.0 0.0 copy-start.2
  8.0 0.0 copy-start.3
  8.0 0.0 copy-start.4
  8.1 1.5 %collective-permute-start = (f32[192,128]{1,0:T(8,128)S(1)}, f32[192,128]{1,0:T(8,128)S(1)}, u32[]{:S(2)}, u32[]{:S(2)}) collective-permute-start(f32[192,128]{1,0:T(8,128)S(1)} %get-tuple-element.31), channel_id=1, source_target_pairs={{0,4},{1,5},{2,6},{3,7},{4,0},{5,1},{6,2},{7,3},{8,12},{9,13},{10,... | collective-permute-start | bytes 294920 | tf_op jit(solution)/shard_map/ppermute | solution.py:608
  9.6 0.9 collective-permute-done.swapped
  10.5 5.1 %collective-permute-start.1 = (f32[128,128]{1,0:T(8,128)S(1)}, f32[128,128]{1,0:T(8,128)S(1)}, u32[]{:S(2)}, u32[]{:S(2)}) collective-permute-start(f32[128,128]{1,0:T(8,128)S(1)} %pad_maximum_fusion.2), channel_id=1, source_target_pairs={{0,8},{1,9},{2,10},{3,11},{4,124},{5,125},{6,126},{7,127},{8,16},{... | collective-permute-start | bytes 196616 | tf_op jit(solution)/shard_map/ppermute | solution.py:608
  15.6 3.8 %collective-permute-start.2 = (f32[128,128]{1,0:T(8,128)S(1)}, f32[128,128]{1,0:T(8,128)S(1)}, u32[]{:S(2)}, u32[]{:S(2)}) collective-permute-start(f32[128,128]{1,0:T(8,128)S(1)} %pad_maximum_fusion.3), channel_id=1, source_target_pairs={{0,1},{1,2},{2,3},{3,0},{4,7},{5,4},{6,5},{7,6},{8,9},{9,10},{10,1... | collective-permute-start | bytes 196616 | tf_op jit(solution)/shard_map/ppermute | solution.py:608
  19.4 4.8 %collective-permute-done.3.far = f32[64,128]{1,0:T(8,128)S(1)} collective-permute-done((f32[64,128]{1,0:T(8,128)S(1)}, f32[64,128]{1,0:T(8,128)S(1)}, u32[]{:S(2)}, u32[]{:S(2)}) %collective-permute-start.3) | collective-permute-done | bytes 32800 | tf_op jit(solution)/shard_map/ppermute | solution.py:608
  24.2 0.3 collective-permute-start.4
  24.5 0.2 copy.23
  24.7 1.1 collective-permute-done.4.passed
  25.8 15.3 %shard_map.120 = (f32[19,32,128]{2,1,0:T(8,128)S(1)}, f32[19,32,128]{2,1,0:T(8,128)S(1)}, f32[192,128]{1,0:T(8,128)S(1)}, f32[2304,128]{1,0:T(8,128)}) custom-call(s32[1]{0:T(128)} %bitcast.place, s32[4,32]{1,0:T(4,128)S(1)} %bitcast.36, s32[1,6]{1,0:T(1,128)S(1)} %bitcast.40, s32[1,6]{1,0:T(1,128)S(1)} %bitcast.44, ...), custom_call_target="tpu_custom_call" | custom-call | flops 14000000000 | bytes 1048576 | tf_op jit(solution)/shard_map/pallas_call | solution.py:588
  41.2 0.2 collective-permute-start.5
  41.4 1.1 %collective-permute-done.5.swapped = f32[192,128]{1,0:T(8,128)S(1)} collective-permute-done((f32[192,128]{1,0:T(8,128)S(1)}, f32[192,128]{1,0:T(8,128)S(1)}, u32[]{:S(2)}, u32[]{:S(2)}) %collective-permute-start.5) | collective-permute-done | bytes 98336 | tf_op jit(solution)/shard_map/ppermute | solution.py:608
  42.6 2.6 %collective-permute-start.6 = (f32[128,128]{1,0:T(8,128)S(1)}, f32[128,128]{1,0:T(8,128)S(1)}, u32[]{:S(2)}, u32[]{:S(2)}) collective-permute-start(f32[128,128]{1,0:T(8,128)S(1)} %pad_maximum_fusion.4), channel_id=1, source_target_pairs={{0,8},{1,9},{2,10},{3,11},{4,124},{5,125},{6,126},{7,127},{8,16},{... | collective-permute-start | bytes 196616 | tf_op jit(solution)/shard_map/ppermute | solution.py:608
  45.2 0.1 collective-permute-start.7
  45.3 5.2 %collective-permute-done.8.far = f32[64,128]{1,0:T(8,128)S(1)} collective-permute-done((f32[64,128]{1,0:T(8,128)S(1)}, f32[64,128]{1,0:T(8,128)S(1)}, u32[]{:S(2)}, u32[]{:S(2)}) %collective-permute-start.8) | collective-permute-done | bytes 32800 | tf_op jit(solution)/shard_map/ppermute | solution.py:608
  50.6 0.4 collective-permute-start.9
  51.0 1.0 collective-permute-done.9.passed
  51.9 12.2 %shard_map.121 = (f32[2304,128]{1,0:T(8,128)S(1)}, f32[19,32,128]{2,1,0:T(8,128)}) custom-call(s32[1]{0:T(128)} %bitcast.place, s32[4,32]{1,0:T(4,128)S(1)} %bitcast.37, s32[1,6]{1,0:T(1,128)S(1)} %bitcast.41, s32[1,6]{1,0:T(1,128)S(1)} %bitcast.45, f32[19,32,128]{2,1,0:T(8,128)S(1)} %bitcast.31, f32[19,32,128]{2,1,0:T(8,128)S(1)} %get-tuple-element.36.local1, ...), custom_call_target="tpu_custom_call" | custom-call | flops 8000000000 | bytes 1048576 | tf_op jit(solution)/shard_map/pallas_call | solution.py:588
  64.2 0.4 collective-permute-start.10
  64.6 1.7 %shard_map.122 = f32[19,32,128]{2,1,0:T(8,128)} custom-call(s32[1]{0:T(128)} %bitcast.place, s32[4,32]{1,0:T(4,128)S(1)} %bitcast.38, s32[1,6]{1,0:T(1,128)S(1)} %bitcast.42, s32[1,6]{1,0:T(1,128)S(1)} %bitcast.46, f32[19,32,128]{2,1,0:T(8,128)S(1)} %get-tuple-element.46.post2, f32[192,128]{1,0:T(8,128)S(1)} %collective-permute-done.5.swapped, ...), custom_call_target="tpu_custom_call" | custom-call | flops 500000000 | bytes 1048576 | tf_op jit(solution)/shard_map/pallas_call | solution.py:588
  66.3 0.1 collective-permute-done.10
  66.4 1.1 %bitcast_add_fusion = f32[1152,128]{1,0:T(8,128)S(1)} fusion(f32[1152,128]{1,0:T(8,128)} %collective-permute-done.10, f32[2,1152,128]{2,1,0:T(8,128)S(1)} %bitcast.25, s32[]{:T(128)S(6)} %select_n.16), kind=kLoop, calls=%fused_computation | loop fusion | flops 147456 | bytes 1769476 | tf_op jit(solution)/shard_map/add | solution.py:635
  67.6 19.2 %all_to_all.10 = f32[64,1,2304]{2,1,0:T(1,128)S(1)} all-to-all(f32[64,1,2304]{2,1,0:T(1,128)S(1)} %bitcast.47), channel_id=1, replica_groups=mesh['bx'=4,'by'=4,'core'=2,'slab'=4] {'bx','by','slab'}, dimensions={0} | all-to-all | bytes 1179648 | tf_op jit(solution)/shard_map/all_to_all | solution.py:636
  86.7 0.4 reduce_sum.9
  87.1 0.3 broadcast_in_dim.4
  87.4 15.9 %all_to_all.11 = f32[64,1,2304]{2,1,0:T(1,128)S(1)} all-to-all(f32[64,1,2304]{2,1,0:T(1,128)S(1)} %broadcast_in_dim.4), channel_id=1, replica_groups=mesh['bx'=4,'by'=4,'core'=2,'slab'=4] {'bx','by','slab'}, dimensions={0} | all-to-all | bytes 1179648 | tf_op jit(solution)/shard_map/all_to_all | solution.py:638
  103.3 3.5 %collective-permute-start.11 = (f32[1152,128]{1,0:T(8,128)S(1)}, f32[1152,128]{1,0:T(8,128)S(1)}, u32[]{:S(2)}, u32[]{:S(2)}) collective-permute-start(f32[1152,128]{1,0:T(8,128)S(1)} %bitcast.22), channel_id=1, source_target_pairs={{0,4},{1,5},{2,6},{3,7},{4,0},{5,1},{6,2},{7,3},{8,12},{9,13},{10,... | collective-permute-start | bytes 1769480 | tf_op jit(solution)/shard_map/ppermute | solution.py:608
  106.9 1.6 %collective-permute-done.11.other = f32[1152,128]{1,0:T(8,128)S(1)} collective-permute-done((f32[1152,128]{1,0:T(8,128)S(1)}, f32[1152,128]{1,0:T(8,128)S(1)}, u32[]{:S(2)}, u32[]{:S(2)}) %collective-permute-start.11) | collective-permute-done | bytes 589856 | tf_op jit(solution)/shard_map/ppermute | solution.py:608
  108.5 1.2 %shard_map.123 = (f32[19,512]{1,0:T(8,128)}, f32[512,512]{1,0:T(8,128)}, f32[19,512]{1,0:T(8,128)}) custom-call(s32[1]{0:T(128)} %bitcast.place, f32[1152,128]{1,0:T(8,128)S(1)} %bitcast.23, f32[1152,128]{1,0:T(8,128)S(1)} %collective-permute-done.11.other), custom_call_target="tpu_custom_call" | custom-call | flops 10000000 | bytes 1048576 | tf_op jit(solution)/shard_map/pallas_call | solution.py:588
  (30 shorter events, 0.2 us)
Async XLA Ops:
  0.6 23.9 %copy-start = (bf16[1,512,512]{2,1,0:T(8,128)(2,1)S(1)}, bf16[1,512,512]{2,1,0:T(8,128)(2,1)}, u32[]{:S(2)}) copy-start(bf16[1,512,512]{2,1,0:T(8,128)(2,1)} %param.10) | copy-start | bytes 1572868
  8.0 17.8 %copy-start.2 = (bf16[512,19]{0,1:T(8,128)(2,1)S(1)}, bf16[512,19]{0,1:T(8,128)(2,1)}, u32[]{:S(2)}) copy-start(bf16[512,19]{0,1:T(8,128)(2,1)} %param.9) | copy-start | bytes 58372
  8.0 17.8 %copy-start.3 = (bf16[19,512]{1,0:T(8,128)(2,1)S(1)}, bf16[19,512]{1,0:T(8,128)(2,1)}, u32[]{:S(2)}) copy-start(bf16[19,512]{1,0:T(8,128)(2,1)} %w_out.3) | copy-start | bytes 58372
  8.0 17.8 %copy-start.4 = (s32[32,4]{0,1:T(4,128)S(1)}, s32[32,4]{0,1:T(4,128)}, u32[]{:S(2)}) copy-start(s32[32,4]{0,1:T(4,128)} %param.13) | copy-start | bytes 1540
  8.0 17.8 %copy-start.5 = (s32[1,1,6]{2,1,0:T(1,128)S(1)}, s32[1,1,6]{2,1,0:T(1,128)}, u32[]{:S(2)}) copy-start(s32[1,1,6]{2,1,0:T(1,128)} %param.14) | copy-start | bytes 76
  8.0 17.8 %copy-start.6 = (s32[1,1,6]{2,1,0:T(1,128)S(1)}, s32[1,1,6]{2,1,0:T(1,128)}, u32[]{:S(2)}) copy-start(s32[1,1,6]{2,1,0:T(1,128)} %param.15) | copy-start | bytes 76
  8.1 2.4 %collective-permute-start = (f32[192,128]{1,0:T(8,128)S(1)}, f32[192,128]{1,0:T(8,128)S(1)}, u32[]{:S(2)}, u32[]{:S(2)}) collective-permute-start(f32[192,128]{1,0:T(8,128)S(1)} %get-tuple-element.31), channel_id=1, source_target_pairs={{0,4},{1,5},{2,6},{3,7},{4,0},{5,1},{6,2},{7,3},{8,12},{9,13},{10,... | collective-permute-start | bytes 294920 | tf_op jit(solution)/shard_map/ppermute | solution.py:608
  10.5 13.7 %collective-permute-start.1 = (f32[128,128]{1,0:T(8,128)S(1)}, f32[128,128]{1,0:T(8,128)S(1)}, u32[]{:S(2)}, u32[]{:S(2)}) collective-permute-start(f32[128,128]{1,0:T(8,128)S(1)} %pad_maximum_fusion.2), channel_id=1, source_target_pairs={{0,8},{1,9},{2,10},{3,11},{4,124},{5,125},{6,126},{7,127},{8,16},{... | collective-permute-start | bytes 196616 | tf_op jit(solution)/shard_map/ppermute | solution.py:608
  15.6 8.6 %collective-permute-start.2 = (f32[128,128]{1,0:T(8,128)S(1)}, f32[128,128]{1,0:T(8,128)S(1)}, u32[]{:S(2)}, u32[]{:S(2)}) collective-permute-start(f32[128,128]{1,0:T(8,128)S(1)} %pad_maximum_fusion.3), channel_id=1, source_target_pairs={{0,1},{1,2},{2,3},{3,0},{4,7},{5,4},{6,5},{7,6},{8,9},{9,10},{10,1... | collective-permute-start | bytes 196616 | tf_op jit(solution)/shard_map/ppermute | solution.py:608
  19.4 4.8 %collective-permute-start.3 = (f32[64,128]{1,0:T(8,128)S(1)}, f32[64,128]{1,0:T(8,128)S(1)}, u32[]{:S(2)}, u32[]{:S(2)}) collective-permute-start(f32[64,128]{1,0:T(8,128)S(1)} %get-tuple-element.73), channel_id=1, source_target_pairs={{0,116},{1,117},{2,118},{3,119},{4,16},{5,17},{6,18},{7,19},{8,124... | collective-permute-start | bytes 98312 | tf_op jit(solution)/shard_map/ppermute | solution.py:608
  24.2 1.6 %collective-permute-start.4 = (f32[192,128]{1,0:T(8,128)S(1)}, f32[192,128]{1,0:T(8,128)S(1)}, u32[]{:S(2)}, u32[]{:S(2)}) collective-permute-start(f32[192,128]{1,0:T(8,128)S(1)} %pad_maximum_fusion), channel_id=1, source_target_pairs={{0,4},{1,5},{2,6},{3,7},{4,0},{5,1},{6,2},{7,3},{8,12},{9,13},{10,... | collective-permute-start | bytes 294920 | tf_op jit(solution)/shard_map/ppermute | solution.py:608
  25.8 26.1 %copy-start.1 = (f32[19,1,1,4096]{3,2,1,0:T(1,128)S(1)}, f32[19,1,1,4096]{3,2,1,0:T(1,128)}, u32[]{:S(2)}) copy-start(f32[19,1,1,4096]{3,2,1,0:T(1,128)} %param.8) | copy-start | bytes 933892
  41.2 1.4 %collective-permute-start.5 = (f32[192,128]{1,0:T(8,128)S(1)}, f32[192,128]{1,0:T(8,128)S(1)}, u32[]{:S(2)}, u32[]{:S(2)}) collective-permute-start(f32[192,128]{1,0:T(8,128)S(1)} %get-tuple-element.37), channel_id=1, source_target_pairs={{0,4},{1,5},{2,6},{3,7},{4,0},{5,1},{6,2},{7,3},{8,12},{9,13},{10,... | collective-permute-start | bytes 294920 | tf_op jit(solution)/shard_map/ppermute | solution.py:608
  42.6 8.0 %collective-permute-start.6 = (f32[128,128]{1,0:T(8,128)S(1)}, f32[128,128]{1,0:T(8,128)S(1)}, u32[]{:S(2)}, u32[]{:S(2)}) collective-permute-start(f32[128,128]{1,0:T(8,128)S(1)} %pad_maximum_fusion.4), channel_id=1, source_target_pairs={{0,8},{1,9},{2,10},{3,11},{4,124},{5,125},{6,126},{7,127},{8,16},{... | collective-permute-start | bytes 196616 | tf_op jit(solution)/shard_map/ppermute | solution.py:608
  45.2 5.3 %collective-permute-start.7 = (f32[128,128]{1,0:T(8,128)S(1)}, f32[128,128]{1,0:T(8,128)S(1)}, u32[]{:S(2)}, u32[]{:S(2)}) collective-permute-start(f32[128,128]{1,0:T(8,128)S(1)} %pad_maximum_fusion.5), channel_id=1, source_target_pairs={{0,1},{1,2},{2,3},{3,0},{4,7},{5,4},{6,5},{7,6},{8,9},{9,10},{10,1... | collective-permute-start | bytes 196616 | tf_op jit(solution)/shard_map/ppermute | solution.py:608
  45.3 5.2 %collective-permute-start.8 = (f32[64,128]{1,0:T(8,128)S(1)}, f32[64,128]{1,0:T(8,128)S(1)}, u32[]{:S(2)}, u32[]{:S(2)}) collective-permute-start(f32[64,128]{1,0:T(8,128)S(1)} %get-tuple-element.69), channel_id=1, source_target_pairs={{0,116},{1,117},{2,118},{3,119},{4,16},{5,17},{6,18},{7,19},{8,124... | collective-permute-start | bytes 98312 | tf_op jit(solution)/shard_map/ppermute | solution.py:608
  50.6 1.4 %collective-permute-start.9 = (f32[192,128]{1,0:T(8,128)S(1)}, f32[192,128]{1,0:T(8,128)S(1)}, u32[]{:S(2)}, u32[]{:S(2)}) collective-permute-start(f32[192,128]{1,0:T(8,128)S(1)} %pad_maximum_fusion.1), channel_id=1, source_target_pairs={{0,4},{1,5},{2,6},{3,7},{4,0},{5,1},{6,2},{7,3},{8,12},{9,13},{10,... | collective-permute-start | bytes 294920 | tf_op jit(solution)/shard_map/ppermute | solution.py:608
  64.2 2.2 %collective-permute-start.10 = (f32[1152,128]{1,0:T(8,128)S(1)}, f32[1152,128]{1,0:T(8,128)}, u32[]{:S(2)}, u32[]{:S(2)}) collective-permute-start(f32[1152,128]{1,0:T(8,128)S(1)} %dynamic-slice_bitcast_fusion), channel_id=1, source_target_pairs={{0,4},{1,5},{2,6},{3,7},{4,0},{5,1},{6,2},{7,3},{8,12},{9,13},{10,... | collective-permute-start | bytes 1769480 | tf_op jit(solution)/shard_map/ppermute | solution.py:608
  103.3 5.2 %collective-permute-start.11 = (f32[1152,128]{1,0:T(8,128)S(1)}, f32[1152,128]{1,0:T(8,128)S(1)}, u32[]{:S(2)}, u32[]{:S(2)}) collective-permute-start(f32[1152,128]{1,0:T(8,128)S(1)} %bitcast.22), channel_id=1, source_target_pairs={{0,4},{1,5},{2,6},{3,7},{4,0},{5,1},{6,2},{7,3},{8,12},{9,13},{10,... | collective-permute-start | bytes 1769480 | tf_op jit(solution)/shard_map/ppermute | solution.py:608

commit v3 on v2

--- a/solution.py
+++ b/solution.py
@@ -460,8 +460,8 @@
 
 
 def first_kernel(place, source_far, level_far, quadrant_far, f0_far, cot_far, w_in_far, w_mid_far,
-                 w_out_far, post, local, sends, h0_far, h1_far,
-                 source, level, quadrant, xs, f0, cot, w_in_t, w_mid, w_out, h0, h1, work, y_two, z_two,
+                 w_out_far, post, local, sends, xs, h0_far, h1_far,
+                 source, level, quadrant, f0, cot, w_in_t, w_mid, w_out, h0, h1, work, y_two, z_two,
                  sems, out_sems):
     info = Tables(place, source, level, quadrant)
     copies = Copies(sems)
@@ -487,8 +487,8 @@
 
 
 def second_kernel(place, source, level, quadrant, post1, local2, swapped, x_got, z_got, far, passed,
-                  w_in_t, w_mid, w_mid_t, w_out, post, local, sends, grads_far,
-                  grads, xs, x, e, h0, h1, a0, a1, f1, pbar, fbar, work, x_four, y_two, z_two, sem):
+                  w_in_t, w_mid, w_mid_t, w_out, post, local, sends, xs, grads_far,
+                  grads, x, e, h0, h1, a0, a1, f1, pbar, fbar, work, x_four, y_two, z_two, sem):
     info = Tables(place, source, level, quadrant)
     got = (swapped, x_got, z_got, far, passed)
     stream(info, post1, got, f1, work, x_four, y_two, z_two)
@@ -548,6 +548,11 @@
     stream(info, post2, (swapped, x_got, z_got, far, passed), out, work, x_four, y_two, z_two)
 
 
+def add_kernel(place, grads, arrived, mine):
+    half = pl.ds(pl.multiple_of((place[0] & 1) * HALF, HALF), HALF)
+    mine[...] = grads[half, :] + arrived[...]
+
+
 def unpack_kernel(place, mine, other, g_in, g_mid, g_out, whole):
     scale = float(NB * NZ * CELLS) ** -0.5
     core = place[0] & 1
@@ -608,11 +613,12 @@
     return lax.ppermute(value, AXES, pairs)
 
 
-def exchange(sends):
+def exchange(sends, xs):
+    xs = xs.reshape(64, 128)
     swapped = send(sends, lambda b, z: (b ^ 1, z))
-    far = send(sends[:64], lambda b, z: (b - 3 if b % 2 == 0 else b + 3, z))
+    far = send(xs, lambda b, z: (b - 3 if b % 2 == 0 else b + 3, z))
     x_got = send(
-        jnp.concatenate([sends[:64], swapped[:64]]),
+        jnp.concatenate([xs, swapped[:64]]),
         lambda b, z: (b + 2 if b % 2 == 0 else b - 2, z),
     )
     z_got = send(
@@ -624,19 +630,19 @@
     return swapped, x_got, z_got, far, passed
 
 
-def total_over_devices(grads, core, beside):
+def total_over_devices(grads, place, beside):
     def other_core(v):
         return send(v, lambda b, z: (b ^ 1, z))
 
     halves = grads.reshape(2, HALF, 128)
-    mine = lax.dynamic_index_in_dim(halves, core, 0, keepdims=False)
-    given = lax.dynamic_index_in_dim(halves, 1 - core, 0, keepdims=False)
-    arrived, beside = lax.optimization_barrier((other_core(given), beside))
-    mine = (mine + arrived).reshape(64, 1, HALF * 2)
+    given = lax.dynamic_index_in_dim(halves, 1 - place[0] % 2, 0, keepdims=False)
+    (mine,) = run(add_kernel, [place], [grads, other_core(given)], [(HALF, 128)], [], 10, 8)
+    mine = mine.reshape(64, 1, HALF * 2)
     mine = lax.all_to_all(mine, CHIPS, 0, 0, tiled=True).sum(axis=0, keepdims=True)
     mine = jnp.broadcast_to(mine, (64, 1, HALF * 2))
     mine = lax.all_to_all(mine, CHIPS, 0, 0, tiled=True).reshape(HALF, 128)
-    return mine, other_core(mine), beside
+    other, beside = lax.optimization_barrier((other_core(mine), beside))
+    return mine, other, beside
 
 
 def shards(populations, w_in, w_mid, w_out, cotangent, face_source, face_level, face_quadrant):
@@ -654,24 +660,24 @@
     near_thin = pltpu.VMEM(THIN, BF16)
     sems = pltpu.SemaphoreType.DMA
 
-    post1, local2, sends, h0, h1 = run(
+    post1, local2, *sends, h0, h1 = run(
         first_kernel, tables[:1], [*tables[1:], f0, cot, w_in_t, w_mid, w_out],
-        [BLOCK, BLOCK, SENDS, hidden, hidden],
+        [BLOCK, BLOCK, SENDS, X_TWO, hidden, hidden],
         [pltpu.SMEM((4, NB), jnp.int32), pltpu.SMEM((1, 6), jnp.int32),
-         pltpu.SMEM((1, 6), jnp.int32), X_TWO,
+         pltpu.SMEM((1, 6), jnp.int32),
          BLOCK, BLOCK, pltpu.VMEM((Q, HID), BF16), pltpu.VMEM((HID, HID), BF16),
          pltpu.VMEM((Q, HID), BF16), near, near, BLOCK, *FACES[1:], sems((8,)),
          sems((2 * CHUNKS,))],
         4000, 32, range(8),
     )
-    got = exchange(sends)
-    post2, local1, sends, grads2 = run(
+    got = exchange(*sends)
+    post2, local1, *sends, grads2 = run(
         second_kernel, tables, [post1, local2, *got, w_in_t, w_mid, w_mid_t, w_out],
-        [BLOCK, BLOCK, SENDS, pltpu.HBM(grad, F32)],
-        [grad, X_TWO, near_thin, near_thin, *[near] * 4, *[BLOCK] * 4, *FACES, sems((1,))],
+        [BLOCK, BLOCK, SENDS, X_TWO, pltpu.HBM(grad, F32)],
+        [grad, near_thin, near_thin, *[near] * 4, *[BLOCK] * 4, *FACES, sems((1,))],
         14000, 32,
     )
-    got = exchange(sends)
+    got = exchange(*sends)
     grads, fbar0 = run(
         third_kernel, tables, [f0, local1, *got, w_in_t, w_mid_t, w_out, grads2, h0, h1],
         [grad, BLOCK],
@@ -680,7 +686,7 @@
     )
     post2, grads = lax.optimization_barrier((post2, grads))
     (final,) = run(final_kernel, tables, [post2, *got], [BLOCK], [BLOCK, *FACES], 500, 8)
-    mine, other, final = total_over_devices(grads, place[0] % 2, final)
+    mine, other, final = total_over_devices(grads, place, final)
     g_in, g_mid, g_out = run(
         unpack_kernel, [place], [mine, other], [(Q, HID), (HID, HID), (Q, HID)], [grad], 10, 8
     )

time: 110 us -> 109 us (level)
  other arithmetic: 1.52 us -> 0.39 us
    add x1 -> x0, other arithmetic: 1.13 us -> none  [total_over_devices(): mine = (mine + arrived).reshape(64, 1, HALF * 2)]
    pallas_call x5 -> x6, Pallas kernels: 37.8 us -> 37.8 us  [run(): pl.pallas_call(kernel, out_shape=[shape(s) for s in outs], in_specs=in_sp...]
  transfers between devices with their start and end apart: 12 -> 12, of which waited for: 8 -> 7; matrix products, arithmetic and copies ran while one was open for 0% -> 0% of each run, Pallas kernels for 2% -> 2%
where the time goes in v3:
time: 109 us
  Pallas kernels  37.8 us (35%)
  blocking collectives  35.1 us (32%)
  starting transfers between devices  18 us (17%)
  waiting for transfers between devices  15.8 us (14%)
    pallas_call x6, Pallas kernels, run(): pl.pallas_call(kernel, out_shape=[shape(s) for s in outs], in_specs=in_sp...  37.8 us
    all_to_all x1, blocking collectives, total_over_devices(): lax.all_to_all(mine, CHIPS, 0, 0, tiled=True).sum(axis=0, keepdims=True)  19.2 us
    ppermute x12, starting transfers between devices, send(): return lax.ppermute(value, AXES, pairs)  18 us
    all_to_all x1, blocking collectives, total_over_devices(): mine = lax.all_to_all(mine, CHIPS, 0, 0, tiled=True).reshape(HALF, 128)  15.9 us
    ppermute x12, waiting for transfers between devices, send(): return lax.ppermute(value, AXES, pairs)  15.8 us
  transfers between devices with their start and end apart: 12, of which 7 were waited for; matrix products, arithmetic and copies ran while one was open for 0% of the time, Pallas kernels for 2%

profile of v3, /device:TPU:1, one launch (start us, length us, event | category | flops | bytes accessed | tf_op | source)
XLA Modules:
  0.0 108.6 jit_solution(1442023299854923539)
XLA Ops:
  0.7 7.3 %shard_map.119 = (f32[19,32,128]{2,1,0:T(8,128)S(1)}, f32[19,32,128]{2,1,0:T(8,128)S(1)}, f32[192,128]{1,0:T(8,128)S(1)}, f32[2,2,2,8,128]{4,3,2,1,0:T(8,128)S(1...) custom-call(s32[1]{0:T(128)} %bitcast.place, s32[4,32]{1,0:T(4,128)} %bitcast.39, s32[1,6]{1,0:T(1,128)} %bitcast.43, ...), custom_call_target="tpu_custom_call" | custom-call | flops 4000000000 | bytes 1048576 | tf_op jit(solution)/shard_map/pallas_call | solution.py:593
  7.9 0.0 copy-start.2
  8.0 0.0 copy-start.3
  8.0 0.0 copy-start.4
  8.0 0.0 copy-start.5
  8.0 1.5 %collective-permute-start = (f32[192,128]{1,0:T(8,128)S(1)}, f32[192,128]{1,0:T(8,128)S(1)}, u32[]{:S(2)}, u32[]{:S(2)}) collective-permute-start(f32[192,128]{1,0:T(8,128)S(1)} %get-tuple-element.33), channel_id=1, source_target_pairs={{0,4},{1,5},{2,6},{3,7},{4,0},{5,1},{6,2},{7,3},{8,12},{9,13},{10,... | collective-permute-start | bytes 294920 | tf_op jit(solution)/shard_map/ppermute | solution.py:613
  9.5 0.9 collective-permute-done.swapped
  10.5 5.1 %collective-permute-start.1 = (f32[128,128]{1,0:T(8,128)S(1)}, f32[128,128]{1,0:T(8,128)S(1)}, u32[]{:S(2)}, u32[]{:S(2)}) collective-permute-start(f32[128,128]{1,0:T(8,128)S(1)} %pad_maximum_fusion.2), channel_id=1, source_target_pairs={{0,8},{1,9},{2,10},{3,11},{4,124},{5,125},{6,126},{7,127},{8,16},{... | collective-permute-start | bytes 196616 | tf_op jit(solution)/shard_map/ppermute | solution.py:613
  15.6 3.8 %collective-permute-start.2 = (f32[128,128]{1,0:T(8,128)S(1)}, f32[128,128]{1,0:T(8,128)S(1)}, u32[]{:S(2)}, u32[]{:S(2)}) collective-permute-start(f32[128,128]{1,0:T(8,128)S(1)} %pad_maximum_fusion.3), channel_id=1, source_target_pairs={{0,1},{1,2},{2,3},{3,0},{4,7},{5,4},{6,5},{7,6},{8,9},{9,10},{10,1... | collective-permute-start | bytes 196616 | tf_op jit(solution)/shard_map/ppermute | solution.py:613
  19.3 4.8 %collective-permute-done.3.far = f32[64,128]{1,0:T(8,128)S(1)} collective-permute-done((f32[64,128]{1,0:T(8,128)S(1)}, f32[64,128]{1,0:T(8,128)S(1)}, u32[]{:S(2)}, u32[]{:S(2)}) %collective-permute-start.3) | collective-permute-done | bytes 32800 | tf_op jit(solution)/shard_map/ppermute | solution.py:613
  24.2 0.3 collective-permute-start.4
  24.5 0.2 copy.23
  24.7 1.1 collective-permute-done.4.passed
  25.8 15.3 %shard_map.120 = (f32[19,32,128]{2,1,0:T(8,128)S(1)}, f32[19,32,128]{2,1,0:T(8,128)S(1)}, f32[192,128]{1,0:T(8,128)S(1)}, f32[2,2,2,8,128]{4,3,2,1,0:T(8,128)S(1)}, f32[2304,128]{1,0:T(8,128)}) custom-call(s32[1]{0:T(128)} %bitcast.place, s32[4,32]{1,0:T(4,128)S(1)} %bitcast.40, s32[1,6]{1,0:T(1,128)S(1)} %bitcast.44, s32[1,6]{1,0:T(1,128)S(1)} %bitcast.48, ...), custom_call_target="tpu_custom_call" | custom-call | flops 14000000000 | bytes 1048576 | tf_op jit(solution)/shard_map/pallas_call | solution.py:593
  41.1 0.2 collective-permute-start.5
  41.4 1.2 %collective-permute-done.5.swapped = f32[192,128]{1,0:T(8,128)S(1)} collective-permute-done((f32[192,128]{1,0:T(8,128)S(1)}, f32[192,128]{1,0:T(8,128)S(1)}, u32[]{:S(2)}, u32[]{:S(2)}) %collective-permute-start.5) | collective-permute-done | bytes 98336 | tf_op jit(solution)/shard_map/ppermute | solution.py:613
  42.5 2.6 %collective-permute-start.6 = (f32[128,128]{1,0:T(8,128)S(1)}, f32[128,128]{1,0:T(8,128)S(1)}, u32[]{:S(2)}, u32[]{:S(2)}) collective-permute-start(f32[128,128]{1,0:T(8,128)S(1)} %pad_maximum_fusion.4), channel_id=1, source_target_pairs={{0,8},{1,9},{2,10},{3,11},{4,124},{5,125},{6,126},{7,127},{8,16},{... | collective-permute-start | bytes 196616 | tf_op jit(solution)/shard_map/ppermute | solution.py:613
  45.2 0.1 collective-permute-start.7
  45.3 5.2 %collective-permute-done.8.far = f32[64,128]{1,0:T(8,128)S(1)} collective-permute-done((f32[64,128]{1,0:T(8,128)S(1)}, f32[64,128]{1,0:T(8,128)S(1)}, u32[]{:S(2)}, u32[]{:S(2)}) %collective-permute-start.8) | collective-permute-done | bytes 32800 | tf_op jit(solution)/shard_map/ppermute | solution.py:613
  50.5 0.4 collective-permute-start.9
  50.9 1.0 collective-permute-done.9.passed
  51.9 12.2 %shard_map.121 = (f32[2304,128]{1,0:T(8,128)S(1)}, f32[19,32,128]{2,1,0:T(8,128)}) custom-call(s32[1]{0:T(128)} %bitcast.place, s32[4,32]{1,0:T(4,128)S(1)} %bitcast.41, s32[1,6]{1,0:T(1,128)S(1)} %bitcast.45, s32[1,6]{1,0:T(1,128)S(1)} %bitcast.49, f32[19,32,128]{2,1,0:T(8,128)S(1)} %bitcast.35, f32[19,32,128]{2,1,0:T(8,128)S(1)} %get-tuple-element.39.local1, ...), custom_call_target="tpu_custom_call" | custom-call | flops 8000000000 | bytes 1048576 | tf_op jit(solution)/shard_map/pallas_call | solution.py:593
  64.2 0.4 collective-permute-start.10
  64.6 1.7 %collective-permute-done.10.arrived = f32[1152,128]{1,0:T(8,128)S(1)} collective-permute-done((f32[1152,128]{1,0:T(8,128)S(1)}, f32[1152,128]{1,0:T(8,128)S(1)}, u32[]{:S(2)}, u32[]{:S(2)}) %collective-permute-start.10) | collective-permute-done | bytes 589856 | tf_op jit(solution)/shard_map/ppermute | solution.py:613
  66.3 0.1 shard_map.122
  66.3 19.2 %all_to_all.10 = f32[64,1,2304]{2,1,0:T(1,128)S(1)} all-to-all(f32[64,1,2304]{2,1,0:T(1,128)S(1)} %bitcast.23), channel_id=1, replica_groups=mesh['bx'=4,'by'=4,'core'=2,'slab'=4] {'bx','by','slab'}, dimensions={0} | all-to-all | bytes 1179648 | tf_op jit(solution)/shard_map/all_to_all | solution.py:641
  85.5 0.4 reduce_sum.9
  85.9 0.3 broadcast_in_dim.4
  86.2 15.9 %all_to_all.11 = f32[64,1,2304]{2,1,0:T(1,128)S(1)} all-to-all(f32[64,1,2304]{2,1,0:T(1,128)S(1)} %broadcast_in_dim.4), channel_id=1, replica_groups=mesh['bx'=4,'by'=4,'core'=2,'slab'=4] {'bx','by','slab'}, dimensions={0} | all-to-all | bytes 1179648 | tf_op jit(solution)/shard_map/all_to_all | solution.py:643
  102.1 3.5 %collective-permute-start.11 = (f32[1152,128]{1,0:T(8,128)S(1)}, f32[1152,128]{1,0:T(8,128)S(1)}, u32[]{:S(2)}, u32[]{:S(2)}) collective-permute-start(f32[1152,128]{1,0:T(8,128)S(1)} %bitcast.24), channel_id=1, source_target_pairs={{0,4},{1,5},{2,6},{3,7},{4,0},{5,1},{6,2},{7,3},{8,12},{9,13},{10,... | collective-permute-start | bytes 1769480 | tf_op jit(solution)/shard_map/ppermute | solution.py:613
  105.7 1.7 %shard_map.123 = f32[19,32,128]{2,1,0:T(8,128)} custom-call(s32[1]{0:T(128)} %bitcast.place, s32[4,32]{1,0:T(4,128)S(1)} %bitcast.42, s32[1,6]{1,0:T(1,128)S(1)} %bitcast.46, s32[1,6]{1,0:T(1,128)S(1)} %bitcast.50, f32[19,32,128]{2,1,0:T(8,128)S(1)} %get-tuple-element.50.post2, f32[192,128]{1,0:T(8,128)S(1)} %collective-permute-done.5.swapped, ...), custom_call_target="tpu_custom_call" | custom-call | flops 500000000 | bytes 1048576 | tf_op jit(solution)/shard_map/pallas_call | solution.py:593
  107.4 1.2 %shard_map.124 = (f32[19,512]{1,0:T(8,128)}, f32[512,512]{1,0:T(8,128)}, f32[19,512]{1,0:T(8,128)}) custom-call(s32[1]{0:T(128)} %bitcast.place, f32[1152,128]{1,0:T(8,128)S(1)} %bitcast.25, f32[1152,128]{1,0:T(8,128)S(1)} %collective-permute-done.11.other), custom_call_target="tpu_custom_call" | custom-call | flops 10000000 | bytes 1048576 | tf_op jit(solution)/shard_map/pallas_call | solution.py:593
  (30 shorter events, 0.2 us)
Async XLA Ops:
  0.6 23.8 %copy-start = (bf16[1,512,512]{2,1,0:T(8,128)(2,1)S(1)}, bf16[1,512,512]{2,1,0:T(8,128)(2,1)}, u32[]{:S(2)}) copy-start(bf16[1,512,512]{2,1,0:T(8,128)(2,1)} %param.10) | copy-start | bytes 1572868
  7.9 17.8 %copy-start.2 = (bf16[512,19]{0,1:T(8,128)(2,1)S(1)}, bf16[512,19]{0,1:T(8,128)(2,1)}, u32[]{:S(2)}) copy-start(bf16[512,19]{0,1:T(8,128)(2,1)} %param.9) | copy-start | bytes 58372
  8.0 17.8 %copy-start.3 = (bf16[19,512]{1,0:T(8,128)(2,1)S(1)}, bf16[19,512]{1,0:T(8,128)(2,1)}, u32[]{:S(2)}) copy-start(bf16[19,512]{1,0:T(8,128)(2,1)} %w_out.3) | copy-start | bytes 58372
  8.0 17.8 %copy-start.4 = (s32[32,4]{0,1:T(4,128)S(1)}, s32[32,4]{0,1:T(4,128)}, u32[]{:S(2)}) copy-start(s32[32,4]{0,1:T(4,128)} %param.13) | copy-start | bytes 1540
  8.0 17.8 %copy-start.5 = (s32[1,1,6]{2,1,0:T(1,128)S(1)}, s32[1,1,6]{2,1,0:T(1,128)}, u32[]{:S(2)}) copy-start(s32[1,1,6]{2,1,0:T(1,128)} %param.14) | copy-start | bytes 76
  8.0 17.8 %copy-start.6 = (s32[1,1,6]{2,1,0:T(1,128)S(1)}, s32[1,1,6]{2,1,0:T(1,128)}, u32[]{:S(2)}) copy-start(s32[1,1,6]{2,1,0:T(1,128)} %param.15) | copy-start | bytes 76
  8.0 2.4 %collective-permute-start = (f32[192,128]{1,0:T(8,128)S(1)}, f32[192,128]{1,0:T(8,128)S(1)}, u32[]{:S(2)}, u32[]{:S(2)}) collective-permute-start(f32[192,128]{1,0:T(8,128)S(1)} %get-tuple-element.33), channel_id=1, source_target_pairs={{0,4},{1,5},{2,6},{3,7},{4,0},{5,1},{6,2},{7,3},{8,12},{9,13},{10,... | collective-permute-start | bytes 294920 | tf_op jit(solution)/shard_map/ppermute | solution.py:613
  10.5 13.7 %collective-permute-start.1 = (f32[128,128]{1,0:T(8,128)S(1)}, f32[128,128]{1,0:T(8,128)S(1)}, u32[]{:S(2)}, u32[]{:S(2)}) collective-permute-start(f32[128,128]{1,0:T(8,128)S(1)} %pad_maximum_fusion.2), channel_id=1, source_target_pairs={{0,8},{1,9},{2,10},{3,11},{4,124},{5,125},{6,126},{7,127},{8,16},{... | collective-permute-start | bytes 196616 | tf_op jit(solution)/shard_map/ppermute | solution.py:613
  15.6 8.6 %collective-permute-start.2 = (f32[128,128]{1,0:T(8,128)S(1)}, f32[128,128]{1,0:T(8,128)S(1)}, u32[]{:S(2)}, u32[]{:S(2)}) collective-permute-start(f32[128,128]{1,0:T(8,128)S(1)} %pad_maximum_fusion.3), channel_id=1, source_target_pairs={{0,1},{1,2},{2,3},{3,0},{4,7},{5,4},{6,5},{7,6},{8,9},{9,10},{10,1... | collective-permute-start | bytes 196616 | tf_op jit(solution)/shard_map/ppermute | solution.py:613
  19.3 4.8 %collective-permute-start.3 = (f32[64,128]{1,0:T(8,128)S(1)}, f32[64,128]{1,0:T(8,128)S(1)}, u32[]{:S(2)}, u32[]{:S(2)}) collective-permute-start(f32[64,128]{1,0:T(8,128)S(1)} %bitcast.33), channel_id=1, source_target_pairs={{0,116},{1,117},{2,118},{3,119},{4,16},{5,17},{6,18},{7,19},{8,124... | collective-permute-start | bytes 98312 | tf_op jit(solution)/shard_map/ppermute | solution.py:613
  24.2 1.6 %collective-permute-start.4 = (f32[192,128]{1,0:T(8,128)S(1)}, f32[192,128]{1,0:T(8,128)S(1)}, u32[]{:S(2)}, u32[]{:S(2)}) collective-permute-start(f32[192,128]{1,0:T(8,128)S(1)} %pad_maximum_fusion), channel_id=1, source_target_pairs={{0,4},{1,5},{2,6},{3,7},{4,0},{5,1},{6,2},{7,3},{8,12},{9,13},{10,... | collective-permute-start | bytes 294920 | tf_op jit(solution)/shard_map/ppermute | solution.py:613
  25.8 26.1 %copy-start.1 = (f32[19,1,1,4096]{3,2,1,0:T(1,128)S(1)}, f32[19,1,1,4096]{3,2,1,0:T(1,128)}, u32[]{:S(2)}) copy-start(f32[19,1,1,4096]{3,2,1,0:T(1,128)} %param.8) | copy-start | bytes 933892
  41.1 1.4 %collective-permute-start.5 = (f32[192,128]{1,0:T(8,128)S(1)}, f32[192,128]{1,0:T(8,128)S(1)}, u32[]{:S(2)}, u32[]{:S(2)}) collective-permute-start(f32[192,128]{1,0:T(8,128)S(1)} %get-tuple-element.40), channel_id=1, source_target_pairs={{0,4},{1,5},{2,6},{3,7},{4,0},{5,1},{6,2},{7,3},{8,12},{9,13},{10,... | collective-permute-start | bytes 294920 | tf_op jit(solution)/shard_map/ppermute | solution.py:613
  42.5 8.0 %collective-permute-start.6 = (f32[128,128]{1,0:T(8,128)S(1)}, f32[128,128]{1,0:T(8,128)S(1)}, u32[]{:S(2)}, u32[]{:S(2)}) collective-permute-start(f32[128,128]{1,0:T(8,128)S(1)} %pad_maximum_fusion.4), channel_id=1, source_target_pairs={{0,8},{1,9},{2,10},{3,11},{4,124},{5,125},{6,126},{7,127},{8,16},{... | collective-permute-start | bytes 196616 | tf_op jit(solution)/shard_map/ppermute | solution.py:613
  45.2 5.3 %collective-permute-start.7 = (f32[128,128]{1,0:T(8,128)S(1)}, f32[128,128]{1,0:T(8,128)S(1)}, u32[]{:S(2)}, u32[]{:S(2)}) collective-permute-start(f32[128,128]{1,0:T(8,128)S(1)} %pad_maximum_fusion.5), channel_id=1, source_target_pairs={{0,1},{1,2},{2,3},{3,0},{4,7},{5,4},{6,5},{7,6},{8,9},{9,10},{10,1... | collective-permute-start | bytes 196616 | tf_op jit(solution)/shard_map/ppermute | solution.py:613
  45.3 5.2 %collective-permute-start.8 = (f32[64,128]{1,0:T(8,128)S(1)}, f32[64,128]{1,0:T(8,128)S(1)}, u32[]{:S(2)}, u32[]{:S(2)}) collective-permute-start(f32[64,128]{1,0:T(8,128)S(1)} %bitcast.31), channel_id=1, source_target_pairs={{0,116},{1,117},{2,118},{3,119},{4,16},{5,17},{6,18},{7,19},{8,124... | collective-permute-start | bytes 98312 | tf_op jit(solution)/shard_map/ppermute | solution.py:613
  50.5 1.4 %collective-permute-start.9 = (f32[192,128]{1,0:T(8,128)S(1)}, f32[192,128]{1,0:T(8,128)S(1)}, u32[]{:S(2)}, u32[]{:S(2)}) collective-permute-start(f32[192,128]{1,0:T(8,128)S(1)} %pad_maximum_fusion.1), channel_id=1, source_target_pairs={{0,4},{1,5},{2,6},{3,7},{4,0},{5,1},{6,2},{7,3},{8,12},{9,13},{10,... | collective-permute-start | bytes 294920 | tf_op jit(solution)/shard_map/ppermute | solution.py:613
  64.2 2.1 %collective-permute-start.10 = (f32[1152,128]{1,0:T(8,128)S(1)}, f32[1152,128]{1,0:T(8,128)S(1)}, u32[]{:S(2)}, u32[]{:S(2)}) collective-permute-start(f32[1152,128]{1,0:T(8,128)S(1)} %dynamic-slice_bitcast_fusion), channel_id=1, source_target_pairs={{0,4},{1,5},{2,6},{3,7},{4,0},{5,1},{6,2},{7,3},{8,12},{9,13},{10,... | collective-permute-start | bytes 1769480 | tf_op jit(solution)/shard_map/ppermute | solution.py:613
  102.1 5.3 %collective-permute-start.11 = (f32[1152,128]{1,0:T(8,128)S(1)}, f32[1152,128]{1,0:T(8,128)S(1)}, u32[]{:S(2)}, u32[]{:S(2)}) collective-permute-start(f32[1152,128]{1,0:T(8,128)S(1)} %bitcast.24), channel_id=1, source_target_pairs={{0,4},{1,5},{2,6},{3,7},{4,0},{5,1},{6,2},{7,3},{8,12},{9,13},{10,... | collective-permute-start | bytes 1769480 | tf_op jit(solution)/shard_map/ppermute | solution.py:613

commit v4 on v3

--- a/solution.py
+++ b/solution.py
@@ -614,18 +614,16 @@
 
 
 def exchange(sends, xs):
-    xs = xs.reshape(64, 128)
+    def next_chip(b, z):
+        return (b + 2 if b % 2 == 0 else b - 2, z)
+
     swapped = send(sends, lambda b, z: (b ^ 1, z))
-    far = send(xs, lambda b, z: (b - 3 if b % 2 == 0 else b + 3, z))
-    x_got = send(
-        jnp.concatenate([xs, swapped[:64]]),
-        lambda b, z: (b + 2 if b % 2 == 0 else b - 2, z),
-    )
+    x_got = send(jnp.concatenate([xs.reshape(64, 128), swapped[:64]]), next_chip)
     z_got = send(
         jnp.concatenate([sends[128:], swapped[128:]]),
         lambda b, z: (b, z + 1 if b % 2 == 0 else z - 1),
     )
-    x_got, z_got, far = lax.optimization_barrier((x_got, z_got, far))
+    far = send(x_got[64:], next_chip)
     passed = send(jnp.concatenate([x_got, z_got[64:]]), lambda b, z: (b ^ 1, z))
     return swapped, x_got, z_got, far, passed
 

time: 109 us -> 116 us (1.064)
  starting transfers between devices: 18 us -> 35.1 us
  waiting for transfers between devices: 15.8 us -> 8.28 us
  blocking collectives: 35.1 us -> 32.4 us
    ppermute x12, starting transfers between devices: 18 us -> 35.1 us  [send(): return lax.ppermute(value, AXES, pairs)]
    ppermute x12, waiting for transfers between devices: 15.8 us -> 8.28 us  [send(): return lax.ppermute(value, AXES, pairs)]
    all_to_all x1, blocking collectives: 19.2 us -> 16.4 us  [total_over_devices(): lax.all_to_all(mine, CHIPS, 0, 0, tiled=True).sum(axis=0, keepdims=True)]
  transfers between devices with their start and end apart: 12 -> 12, of which waited for: 7 -> 7; matrix products, arithmetic and copies ran while one was open for 0% -> 0% of each run, Pallas kernels for 2% -> 1%
where the time goes in v4:
time: 116 us; the launch traced here: 115 us
  Pallas kernels  37.8 us (33%)
  starting transfers between devices  35.1 us (30%)
  blocking collectives  32.4 us (28%)
  waiting for transfers between devices  8.28 us (7%)
    pallas_call x6, Pallas kernels, run(): pl.pallas_call(kernel, out_shape=[shape(s) for s in outs], in_specs=in_sp...  37.8 us
    ppermute x12, starting transfers between devices, send(): return lax.ppermute(value, AXES, pairs)  35.1 us
    all_to_all x1, blocking collectives, total_over_devices(): lax.all_to_all(mine, CHIPS, 0, 0, tiled=True).sum(axis=0, keepdims=True)  16.4 us
    all_to_all x1, blocking collectives, total_over_devices(): mine = lax.all_to_all(mine, CHIPS, 0, 0, tiled=True).reshape(HALF, 128)  15.9 us
    ppermute x12, waiting for transfers between devices, send(): return lax.ppermute(value, AXES, pairs)  8.28 us
  transfers between devices with their start and end apart: 12, of which 7 were waited for; matrix products, arithmetic and copies ran while one was open for 0% of the time, Pallas kernels for 1%

profile of v4, /device:TPU:1, one launch (start us, length us, event | category | flops | bytes accessed | tf_op | source)
XLA Modules:
  0.0 115.5 jit_solution(17247428841363286927)
XLA Ops:
  0.7 7.3 %shard_map.119 = (f32[19,32,128]{2,1,0:T(8,128)S(1)}, f32[19,32,128]{2,1,0:T(8,128)S(1)}, f32[192,128]{1,0:T(8,128)S(1)}, f32[2,2,2,8,128]{4,3,2,1,0:T(8,128)S(1...) custom-call(s32[1]{0:T(128)} %bitcast.place, s32[4,32]{1,0:T(4,128)} %bitcast.37, s32[1,6]{1,0:T(1,128)} %bitcast.41, ...), custom_call_target="tpu_custom_call" | custom-call | flops 4000000000 | bytes 1048576 | tf_op jit(solution)/shard_map/pallas_call | solution.py:593
  7.9 0.0 copy-start.2
  8.0 0.0 copy-start.4
  8.0 0.0 copy-start.5
  8.0 1.5 %collective-permute-start = (f32[192,128]{1,0:T(8,128)S(1)}, f32[192,128]{1,0:T(8,128)S(1)}, u32[]{:S(2)}, u32[]{:S(2)}) collective-permute-start(f32[192,128]{1,0:T(8,128)S(1)} %get-tuple-element.27), channel_id=1, source_target_pairs={{0,4},{1,5},{2,6},{3,7},{4,0},{5,1},{6,2},{7,3},{8,12},{9,13},{10,... | collective-permute-start | bytes 294920 | tf_op jit(solution)/shard_map/ppermute | solution.py:613
  9.5 0.9 collective-permute-done.swapped
  10.5 3.9 %collective-permute-start.2 = (f32[128,128]{1,0:T(8,128)S(1)}, f32[128,128]{1,0:T(8,128)S(1)}, u32[]{:S(2)}, u32[]{:S(2)}) collective-permute-start(f32[128,128]{1,0:T(8,128)S(1)} %pad_maximum_fusion.3), channel_id=1, source_target_pairs={{0,1},{1,2},{2,3},{3,0},{4,7},{5,4},{6,5},{7,6},{8,9},{9,10},{10,1... | collective-permute-start | bytes 196616 | tf_op jit(solution)/shard_map/ppermute | solution.py:613
  14.4 4.9 %collective-permute-start.1 = (f32[128,128]{1,0:T(8,128)S(1)}, f32[128,128]{1,0:T(8,128)S(1)}, u32[]{:S(2)}, u32[]{:S(2)}) collective-permute-start(f32[128,128]{1,0:T(8,128)S(1)} %pad_maximum_fusion.2), channel_id=1, source_target_pairs={{0,8},{1,9},{2,10},{3,11},{4,124},{5,125},{6,126},{7,127},{8,16},{... | collective-permute-start | bytes 196616 | tf_op jit(solution)/shard_map/ppermute | solution.py:613
  19.3 1.3 %collective-permute-done.1.x_got = f32[128,128]{1,0:T(8,128)S(1)} collective-permute-done((f32[128,128]{1,0:T(8,128)S(1)}, f32[128,128]{1,0:T(8,128)S(1)}, u32[]{:S(2)}, u32[]{:S(2)}) %collective-permute-start.1) | collective-permute-done | bytes 65568 | tf_op jit(solution)/shard_map/ppermute | solution.py:613
  20.7 5.4 %collective-permute-start.3 = (f32[64,128]{1,0:T(8,128)S(1)}, f32[64,128]{1,0:T(8,128)S(1)}, u32[]{:S(2)}, u32[]{:S(2)}) collective-permute-start(f32[64,128]{1,0:T(8,128)S(1)} %slice.42), channel_id=1, source_target_pairs={{0,8},{1,9},{2,10},{3,11},{4,124},{5,125},{6,126},{7,127},{8,16},{... | collective-permute-start | bytes 98312 | tf_op jit(solution)/shard_map/ppermute | solution.py:613
  26.1 0.2 copy.23
  26.3 0.8 collective-permute-done.3.far
  27.2 15.3 %shard_map.120 = (f32[19,32,128]{2,1,0:T(8,128)S(1)}, f32[19,32,128]{2,1,0:T(8,128)S(1)}, f32[192,128]{1,0:T(8,128)S(1)}, f32[2,2,2,8,128]{4,3,2,1,0:T(8,128)S(1)}, f32[2304,128]{1,0:T(8,128)}) custom-call(s32[1]{0:T(128)} %bitcast.place, s32[4,32]{1,0:T(4,128)S(1)} %bitcast.38, s32[1,6]{1,0:T(1,128)S(1)} %bitcast.42, s32[1,6]{1,0:T(1,128)S(1)} %bitcast.46, ...), custom_call_target="tpu_custom_call" | custom-call | flops 14000000000 | bytes 1048576 | tf_op jit(solution)/shard_map/pallas_call | solution.py:593
  42.5 1.5 %collective-permute-start.5 = (f32[192,128]{1,0:T(8,128)S(1)}, f32[192,128]{1,0:T(8,128)S(1)}, u32[]{:S(2)}, u32[]{:S(2)}) collective-permute-start(f32[192,128]{1,0:T(8,128)S(1)} %get-tuple-element.31), channel_id=1, source_target_pairs={{0,4},{1,5},{2,6},{3,7},{4,0},{5,1},{6,2},{7,3},{8,12},{9,13},{10,... | collective-permute-start | bytes 294920 | tf_op jit(solution)/shard_map/ppermute | solution.py:613
  44.0 0.9 collective-permute-done.5.swapped
  45.0 1.6 %collective-permute-start.7 = (f32[128,128]{1,0:T(8,128)S(1)}, f32[128,128]{1,0:T(8,128)S(1)}, u32[]{:S(2)}, u32[]{:S(2)}) collective-permute-start(f32[128,128]{1,0:T(8,128)S(1)} %pad_maximum_fusion.5), channel_id=1, source_target_pairs={{0,1},{1,2},{2,3},{3,0},{4,7},{5,4},{6,5},{7,6},{8,9},{9,10},{10,1... | collective-permute-start | bytes 196616 | tf_op jit(solution)/shard_map/ppermute | solution.py:613
  46.5 2.9 %collective-permute-start.6 = (f32[128,128]{1,0:T(8,128)S(1)}, f32[128,128]{1,0:T(8,128)S(1)}, u32[]{:S(2)}, u32[]{:S(2)}) collective-permute-start(f32[128,128]{1,0:T(8,128)S(1)} %pad_maximum_fusion.4), channel_id=1, source_target_pairs={{0,8},{1,9},{2,10},{3,11},{4,124},{5,125},{6,126},{7,127},{8,16},{... | collective-permute-start | bytes 196616 | tf_op jit(solution)/shard_map/ppermute | solution.py:613
  49.4 1.3 %collective-permute-done.6.x_got = f32[128,128]{1,0:T(8,128)S(1)} collective-permute-done((f32[128,128]{1,0:T(8,128)S(1)}, f32[128,128]{1,0:T(8,128)S(1)}, u32[]{:S(2)}, u32[]{:S(2)}) %collective-permute-start.6) | collective-permute-done | bytes 65568 | tf_op jit(solution)/shard_map/ppermute | solution.py:613
  50.7 3.8 %collective-permute-start.9 = (f32[192,128]{1,0:T(8,128)S(1)}, f32[192,128]{1,0:T(8,128)S(1)}, u32[]{:S(2)}, u32[]{:S(2)}) collective-permute-start(f32[192,128]{1,0:T(8,128)S(1)} %pad_maximum_fusion.1), channel_id=1, source_target_pairs={{0,4},{1,5},{2,6},{3,7},{4,0},{5,1},{6,2},{7,3},{8,12},{9,13},{10,... | collective-permute-start | bytes 294920 | tf_op jit(solution)/shard_map/ppermute | solution.py:613
  54.5 1.5 %collective-permute-start.8 = (f32[64,128]{1,0:T(8,128)S(1)}, f32[64,128]{1,0:T(8,128)S(1)}, u32[]{:S(2)}, u32[]{:S(2)}) collective-permute-start(f32[64,128]{1,0:T(8,128)S(1)} %slice.46), channel_id=1, source_target_pairs={{0,8},{1,9},{2,10},{3,11},{4,124},{5,125},{6,126},{7,127},{8,16},{... | collective-permute-start | bytes 98312 | tf_op jit(solution)/shard_map/ppermute | solution.py:613
  56.0 1.3 %collective-permute-done.8.far = f32[64,128]{1,0:T(8,128)S(1)} collective-permute-done((f32[64,128]{1,0:T(8,128)S(1)}, f32[64,128]{1,0:T(8,128)S(1)}, u32[]{:S(2)}, u32[]{:S(2)}) %collective-permute-start.8) | collective-permute-done | bytes 32800 | tf_op jit(solution)/shard_map/ppermute | solution.py:613
  57.3 12.2 %shard_map.121 = (f32[2304,128]{1,0:T(8,128)S(1)}, f32[19,32,128]{2,1,0:T(8,128)}) custom-call(s32[1]{0:T(128)} %bitcast.place, s32[4,32]{1,0:T(4,128)S(1)} %bitcast.39, s32[1,6]{1,0:T(1,128)S(1)} %bitcast.43, s32[1,6]{1,0:T(1,128)S(1)} %bitcast.47, f32[19,32,128]{2,1,0:T(8,128)S(1)} %bitcast.33, f32[19,32,128]{2,1,0:T(8,128)S(1)} %get-tuple-element.30.local1, ...), custom_call_target="tpu_custom_call" | custom-call | flops 8000000000 | bytes 1048576 | tf_op jit(solution)/shard_map/pallas_call | solution.py:593
  69.6 4.6 %collective-permute-start.10 = (f32[1152,128]{1,0:T(8,128)S(1)}, f32[1152,128]{1,0:T(8,128)S(1)}, u32[]{:S(2)}, u32[]{:S(2)}) collective-permute-start(f32[1152,128]{1,0:T(8,128)S(1)} %dynamic-slice_bitcast_fusion), channel_id=1, source_target_pairs={{0,4},{1,5},{2,6},{3,7},{4,0},{5,1},{6,2},{7,3},{8,12},{9,13},{10,... | collective-permute-start | bytes 1769480 | tf_op jit(solution)/shard_map/ppermute | solution.py:613
  74.2 1.6 %collective-permute-done.10.arrived = f32[1152,128]{1,0:T(8,128)S(1)} collective-permute-done((f32[1152,128]{1,0:T(8,128)S(1)}, f32[1152,128]{1,0:T(8,128)S(1)}, u32[]{:S(2)}, u32[]{:S(2)}) %collective-permute-start.10) | collective-permute-done | bytes 589856 | tf_op jit(solution)/shard_map/ppermute | solution.py:613
  75.8 0.1 shard_map.122
  75.9 16.4 %all_to_all.10 = f32[64,1,2304]{2,1,0:T(1,128)S(1)} all-to-all(f32[64,1,2304]{2,1,0:T(1,128)S(1)} %bitcast.23), channel_id=1, replica_groups=mesh['bx'=4,'by'=4,'core'=2,'slab'=4] {'bx','by','slab'}, dimensions={0} | all-to-all | bytes 1179648 | tf_op jit(solution)/shard_map/all_to_all | solution.py:639
  92.4 0.4 reduce_sum.9
  92.7 0.3 broadcast_in_dim.4
  93.0 15.9 %all_to_all.11 = f32[64,1,2304]{2,1,0:T(1,128)S(1)} all-to-all(f32[64,1,2304]{2,1,0:T(1,128)S(1)} %broadcast_in_dim.4), channel_id=1, replica_groups=mesh['bx'=4,'by'=4,'core'=2,'slab'=4] {'bx','by','slab'}, dimensions={0} | all-to-all | bytes 1179648 | tf_op jit(solution)/shard_map/all_to_all | solution.py:641
  109.0 3.5 %collective-permute-start.11 = (f32[1152,128]{1,0:T(8,128)S(1)}, f32[1152,128]{1,0:T(8,128)S(1)}, u32[]{:S(2)}, u32[]{:S(2)}) collective-permute-start(f32[1152,128]{1,0:T(8,128)S(1)} %bitcast.24), channel_id=1, source_target_pairs={{0,4},{1,5},{2,6},{3,7},{4,0},{5,1},{6,2},{7,3},{8,12},{9,13},{10,... | collective-permute-start | bytes 1769480 | tf_op jit(solution)/shard_map/ppermute | solution.py:613
  112.5 1.7 %shard_map.123 = f32[19,32,128]{2,1,0:T(8,128)} custom-call(s32[1]{0:T(128)} %bitcast.place, s32[4,32]{1,0:T(4,128)S(1)} %bitcast.40, s32[1,6]{1,0:T(1,128)S(1)} %bitcast.44, s32[1,6]{1,0:T(1,128)S(1)} %bitcast.48, f32[19,32,128]{2,1,0:T(8,128)S(1)} %get-tuple-element.38.post2, f32[192,128]{1,0:T(8,128)S(1)} %collective-permute-done.5.swapped, ...), custom_call_target="tpu_custom_call" | custom-call | flops 500000000 | bytes 1048576 | tf_op jit(solution)/shard_map/pallas_call | solution.py:593
  114.2 1.2 %shard_map.124 = (f32[19,512]{1,0:T(8,128)}, f32[512,512]{1,0:T(8,128)}, f32[19,512]{1,0:T(8,128)}) custom-call(s32[1]{0:T(128)} %bitcast.place, f32[1152,128]{1,0:T(8,128)S(1)} %bitcast.25, f32[1152,128]{1,0:T(8,128)S(1)} %collective-permute-done.11.other), custom_call_target="tpu_custom_call" | custom-call | flops 10000000 | bytes 1048576 | tf_op jit(solution)/shard_map/pallas_call | solution.py:593
  (32 shorter events, 0.2 us)
Async XLA Ops:
  0.6 25.5 %copy-start = (bf16[1,512,512]{2,1,0:T(8,128)(2,1)S(1)}, bf16[1,512,512]{2,1,0:T(8,128)(2,1)}, u32[]{:S(2)}) copy-start(bf16[1,512,512]{2,1,0:T(8,128)(2,1)} %param.10) | copy-start | bytes 1572868
  7.9 19.2 %copy-start.2 = (bf16[512,19]{0,1:T(8,128)(2,1)S(1)}, bf16[512,19]{0,1:T(8,128)(2,1)}, u32[]{:S(2)}) copy-start(bf16[512,19]{0,1:T(8,128)(2,1)} %param.9) | copy-start | bytes 58372
  8.0 19.2 %copy-start.3 = (bf16[19,512]{1,0:T(8,128)(2,1)S(1)}, bf16[19,512]{1,0:T(8,128)(2,1)}, u32[]{:S(2)}) copy-start(bf16[19,512]{1,0:T(8,128)(2,1)} %w_out.3) | copy-start | bytes 58372
  8.0 19.2 %copy-start.4 = (s32[32,4]{0,1:T(4,128)S(1)}, s32[32,4]{0,1:T(4,128)}, u32[]{:S(2)}) copy-start(s32[32,4]{0,1:T(4,128)} %param.13) | copy-start | bytes 1540
  8.0 19.2 %copy-start.5 = (s32[1,1,6]{2,1,0:T(1,128)S(1)}, s32[1,1,6]{2,1,0:T(1,128)}, u32[]{:S(2)}) copy-start(s32[1,1,6]{2,1,0:T(1,128)} %param.14) | copy-start | bytes 76
  8.0 19.2 %copy-start.6 = (s32[1,1,6]{2,1,0:T(1,128)S(1)}, s32[1,1,6]{2,1,0:T(1,128)}, u32[]{:S(2)}) copy-start(s32[1,1,6]{2,1,0:T(1,128)} %param.15) | copy-start | bytes 76
  8.0 2.4 %collective-permute-start = (f32[192,128]{1,0:T(8,128)S(1)}, f32[192,128]{1,0:T(8,128)S(1)}, u32[]{:S(2)}, u32[]{:S(2)}) collective-permute-start(f32[192,128]{1,0:T(8,128)S(1)} %get-tuple-element.27), channel_id=1, source_target_pairs={{0,4},{1,5},{2,6},{3,7},{4,0},{5,1},{6,2},{7,3},{8,12},{9,13},{10,... | collective-permute-start | bytes 294920 | tf_op jit(solution)/shard_map/ppermute | solution.py:613
  10.5 8.8 %collective-permute-start.2 = (f32[128,128]{1,0:T(8,128)S(1)}, f32[128,128]{1,0:T(8,128)S(1)}, u32[]{:S(2)}, u32[]{:S(2)}) collective-permute-start(f32[128,128]{1,0:T(8,128)S(1)} %pad_maximum_fusion.3), channel_id=1, source_target_pairs={{0,1},{1,2},{2,3},{3,0},{4,7},{5,4},{6,5},{7,6},{8,9},{9,10},{10,1... | collective-permute-start | bytes 196616 | tf_op jit(solution)/shard_map/ppermute | solution.py:613
  14.4 6.3 %collective-permute-start.1 = (f32[128,128]{1,0:T(8,128)S(1)}, f32[128,128]{1,0:T(8,128)S(1)}, u32[]{:S(2)}, u32[]{:S(2)}) collective-permute-start(f32[128,128]{1,0:T(8,128)S(1)} %pad_maximum_fusion.2), channel_id=1, source_target_pairs={{0,8},{1,9},{2,10},{3,11},{4,124},{5,125},{6,126},{7,127},{8,16},{... | collective-permute-start | bytes 196616 | tf_op jit(solution)/shard_map/ppermute | solution.py:613
  20.7 6.5 %collective-permute-start.4 = (f32[192,128]{1,0:T(8,128)S(1)}, f32[192,128]{1,0:T(8,128)S(1)}, u32[]{:S(2)}, u32[]{:S(2)}) collective-permute-start(f32[192,128]{1,0:T(8,128)S(1)} %pad_maximum_fusion), channel_id=1, source_target_pairs={{0,4},{1,5},{2,6},{3,7},{4,0},{5,1},{6,2},{7,3},{8,12},{9,13},{10,... | collective-permute-start | bytes 294920 | tf_op jit(solution)/shard_map/ppermute | solution.py:613
  20.7 6.5 %collective-permute-start.3 = (f32[64,128]{1,0:T(8,128)S(1)}, f32[64,128]{1,0:T(8,128)S(1)}, u32[]{:S(2)}, u32[]{:S(2)}) collective-permute-start(f32[64,128]{1,0:T(8,128)S(1)} %slice.42), channel_id=1, source_target_pairs={{0,8},{1,9},{2,10},{3,11},{4,124},{5,125},{6,126},{7,127},{8,16},{... | collective-permute-start | bytes 98312 | tf_op jit(solution)/shard_map/ppermute | solution.py:613
  27.2 30.1 %copy-start.1 = (f32[19,1,1,4096]{3,2,1,0:T(1,128)S(1)}, f32[19,1,1,4096]{3,2,1,0:T(1,128)}, u32[]{:S(2)}) copy-start(f32[19,1,1,4096]{3,2,1,0:T(1,128)} %param.8) | copy-start | bytes 933892
  42.5 2.4 %collective-permute-start.5 = (f32[192,128]{1,0:T(8,128)S(1)}, f32[192,128]{1,0:T(8,128)S(1)}, u32[]{:S(2)}, u32[]{:S(2)}) collective-permute-start(f32[192,128]{1,0:T(8,128)S(1)} %get-tuple-element.31), channel_id=1, source_target_pairs={{0,4},{1,5},{2,6},{3,7},{4,0},{5,1},{6,2},{7,3},{8,12},{9,13},{10,... | collective-permute-start | bytes 294920 | tf_op jit(solution)/shard_map/ppermute | solution.py:613
  45.0 4.4 %collective-permute-start.7 = (f32[128,128]{1,0:T(8,128)S(1)}, f32[128,128]{1,0:T(8,128)S(1)}, u32[]{:S(2)}, u32[]{:S(2)}) collective-permute-start(f32[128,128]{1,0:T(8,128)S(1)} %pad_maximum_fusion.5), channel_id=1, source_target_pairs={{0,1},{1,2},{2,3},{3,0},{4,7},{5,4},{6,5},{7,6},{8,9},{9,10},{10,1... | collective-permute-start | bytes 196616 | tf_op jit(solution)/shard_map/ppermute | solution.py:613
  46.5 4.2 %collective-permute-start.6 = (f32[128,128]{1,0:T(8,128)S(1)}, f32[128,128]{1,0:T(8,128)S(1)}, u32[]{:S(2)}, u32[]{:S(2)}) collective-permute-start(f32[128,128]{1,0:T(8,128)S(1)} %pad_maximum_fusion.4), channel_id=1, source_target_pairs={{0,8},{1,9},{2,10},{3,11},{4,124},{5,125},{6,126},{7,127},{8,16},{... | collective-permute-start | bytes 196616 | tf_op jit(solution)/shard_map/ppermute | solution.py:613
  50.7 6.6 %collective-permute-start.9 = (f32[192,128]{1,0:T(8,128)S(1)}, f32[192,128]{1,0:T(8,128)S(1)}, u32[]{:S(2)}, u32[]{:S(2)}) collective-permute-start(f32[192,128]{1,0:T(8,128)S(1)} %pad_maximum_fusion.1), channel_id=1, source_target_pairs={{0,4},{1,5},{2,6},{3,7},{4,0},{5,1},{6,2},{7,3},{8,12},{9,13},{10,... | collective-permute-start | bytes 294920 | tf_op jit(solution)/shard_map/ppermute | solution.py:613
  54.5 2.8 %collective-permute-start.8 = (f32[64,128]{1,0:T(8,128)S(1)}, f32[64,128]{1,0:T(8,128)S(1)}, u32[]{:S(2)}, u32[]{:S(2)}) collective-permute-start(f32[64,128]{1,0:T(8,128)S(1)} %slice.46), channel_id=1, source_target_pairs={{0,8},{1,9},{2,10},{3,11},{4,124},{5,125},{6,126},{7,127},{8,16},{... | collective-permute-start | bytes 98312 | tf_op jit(solution)/shard_map/ppermute | solution.py:613
  69.6 6.3 %collective-permute-start.10 = (f32[1152,128]{1,0:T(8,128)S(1)}, f32[1152,128]{1,0:T(8,128)S(1)}, u32[]{:S(2)}, u32[]{:S(2)}) collective-permute-start(f32[1152,128]{1,0:T(8,128)S(1)} %dynamic-slice_bitcast_fusion), channel_id=1, source_target_pairs={{0,4},{1,5},{2,6},{3,7},{4,0},{5,1},{6,2},{7,3},{8,12},{9,13},{10,... | collective-permute-start | bytes 1769480 | tf_op jit(solution)/shard_map/ppermute | solution.py:613
  109.0 5.3 %collective-permute-start.11 = (f32[1152,128]{1,0:T(8,128)S(1)}, f32[1152,128]{1,0:T(8,128)S(1)}, u32[]{:S(2)}, u32[]{:S(2)}) collective-permute-start(f32[1152,128]{1,0:T(8,128)S(1)} %bitcast.24), channel_id=1, source_target_pairs={{0,4},{1,5},{2,6},{3,7},{4,0},{5,1},{6,2},{7,3},{8,12},{9,13},{10,... | collective-permute-start | bytes 1769480 | tf_op jit(solution)/shard_map/ppermute | solution.py:613

commit v5 on v3

--- a/solution.py
+++ b/solution.py
@@ -614,11 +614,10 @@
 
 
 def exchange(sends, xs):
-    xs = xs.reshape(64, 128)
     swapped = send(sends, lambda b, z: (b ^ 1, z))
-    far = send(xs, lambda b, z: (b - 3 if b % 2 == 0 else b + 3, z))
+    far = send(sends, lambda b, z: (b - 3 if b % 2 == 0 else b + 3, z))
     x_got = send(
-        jnp.concatenate([xs, swapped[:64]]),
+        jnp.concatenate([xs.reshape(64, 128), swapped[:64]]),
         lambda b, z: (b + 2 if b % 2 == 0 else b - 2, z),
     )
     z_got = send(

time: 109 us -> 108 us (level)
  waiting for transfers between devices: 15.8 us -> 7.25 us
  starting transfers between devices: 18 us -> 26.4 us
    ppermute x12, waiting for transfers between devices: 15.8 us -> 7.25 us  [send(): return lax.ppermute(value, AXES, pairs)]
    ppermute x12, starting transfers between devices: 18 us -> 26.4 us  [send(): return lax.ppermute(value, AXES, pairs)]
  transfers between devices with their start and end apart: 12 -> 12, of which waited for: 7 -> 6; matrix products, arithmetic and copies ran while one was open for 0% -> 0% of each run, Pallas kernels for 2% -> 2%
where the time goes in v5:
time: 108 us
  Pallas kernels  37.8 us (35%)
  blocking collectives  34.3 us (32%)
  starting transfers between devices  26.4 us (24%)
  waiting for transfers between devices  7.25 us (7%)
    pallas_call x6, Pallas kernels, run(): pl.pallas_call(kernel, out_shape=[shape(s) for s in outs], in_specs=in_sp...  37.8 us
    ppermute x12, starting transfers between devices, send(): return lax.ppermute(value, AXES, pairs)  26.4 us
    all_to_all x1, blocking collectives, total_over_devices(): lax.all_to_all(mine, CHIPS, 0, 0, tiled=True).sum(axis=0, keepdims=True)  18.3 us
    all_to_all x1, blocking collectives, total_over_devices(): mine = lax.all_to_all(mine, CHIPS, 0, 0, tiled=True).reshape(HALF, 128)  15.9 us
    ppermute x12, waiting for transfers between devices, send(): return lax.ppermute(value, AXES, pairs)  7.25 us
  transfers between devices with their start and end apart: 12, of which 6 were waited for; matrix products, arithmetic and copies ran while one was open for 0% of the time, Pallas kernels for 2%

profile of v5, /device:TPU:1, one launch (start us, length us, event | category | flops | bytes accessed | tf_op | source)
XLA Modules:
  0.0 107.5 jit_solution(16460007387610224661)
XLA Ops:
  0.7 7.3 %shard_map.119 = (f32[19,32,128]{2,1,0:T(8,128)S(1)}, f32[19,32,128]{2,1,0:T(8,128)S(1)}, f32[192,128]{1,0:T(8,128)S(1)}, f32[2,2,2,8,128]{4,3,2,1,0:T(8,128)S(1...) custom-call(s32[1]{0:T(128)} %bitcast.place, s32[4,32]{1,0:T(4,128)} %bitcast.37, s32[1,6]{1,0:T(1,128)} %bitcast.41, ...), custom_call_target="tpu_custom_call" | custom-call | flops 4000000000 | bytes 1048576 | tf_op jit(solution)/shard_map/pallas_call | solution.py:593
  7.9 0.0 copy-start.2
  8.0 0.0 copy-start.3
  8.0 0.0 copy-start.4
  8.0 0.0 copy-start.5
  8.0 1.5 %collective-permute-start = (f32[192,128]{1,0:T(8,128)S(1)}, f32[192,128]{1,0:T(8,128)S(1)}, u32[]{:S(2)}, u32[]{:S(2)}) collective-permute-start(f32[192,128]{1,0:T(8,128)S(1)} %get-tuple-element.33), channel_id=1, source_target_pairs={{0,4},{1,5},{2,6},{3,7},{4,0},{5,1},{6,2},{7,3},{8,12},{9,13},{10,... | collective-permute-start | bytes 294920 | tf_op jit(solution)/shard_map/ppermute | solution.py:613
  9.5 3.0 %collective-permute-start.3 = (f32[192,128]{1,0:T(8,128)S(1)}, f32[192,128]{1,0:T(8,128)S(1)}, u32[]{:S(2)}, u32[]{:S(2)}) collective-permute-start(f32[192,128]{1,0:T(8,128)S(1)} %get-tuple-element.33), channel_id=1, source_target_pairs={{0,116},{1,117},{2,118},{3,119},{4,16},{5,17},{6,18},{7,19},{8,124... | collective-permute-start | bytes 294920 | tf_op jit(solution)/shard_map/ppermute | solution.py:613
  12.5 3.0 %collective-permute-start.1 = (f32[128,128]{1,0:T(8,128)S(1)}, f32[128,128]{1,0:T(8,128)S(1)}, u32[]{:S(2)}, u32[]{:S(2)}) collective-permute-start(f32[128,128]{1,0:T(8,128)S(1)} %pad_maximum_fusion.2), channel_id=1, source_target_pairs={{0,8},{1,9},{2,10},{3,11},{4,124},{5,125},{6,126},{7,127},{8,16},{... | collective-permute-start | bytes 196616 | tf_op jit(solution)/shard_map/ppermute | solution.py:613
  15.6 3.8 %collective-permute-start.2 = (f32[128,128]{1,0:T(8,128)S(1)}, f32[128,128]{1,0:T(8,128)S(1)}, u32[]{:S(2)}, u32[]{:S(2)}) collective-permute-start(f32[128,128]{1,0:T(8,128)S(1)} %pad_maximum_fusion.3), channel_id=1, source_target_pairs={{0,1},{1,2},{2,3},{3,0},{4,7},{5,4},{6,5},{7,6},{8,9},{9,10},{10,1... | collective-permute-start | bytes 196616 | tf_op jit(solution)/shard_map/ppermute | solution.py:613
  19.3 1.3 %collective-permute-done.2.z_got = f32[128,128]{1,0:T(8,128)S(1)} collective-permute-done((f32[128,128]{1,0:T(8,128)S(1)}, f32[128,128]{1,0:T(8,128)S(1)}, u32[]{:S(2)}, u32[]{:S(2)}) %collective-permute-start.2) | collective-permute-done | bytes 65568 | tf_op jit(solution)/shard_map/ppermute | solution.py:613
  20.7 2.4 %collective-permute-start.4 = (f32[192,128]{1,0:T(8,128)S(1)}, f32[192,128]{1,0:T(8,128)S(1)}, u32[]{:S(2)}, u32[]{:S(2)}) collective-permute-start(f32[192,128]{1,0:T(8,128)S(1)} %pad_maximum_fusion), channel_id=1, source_target_pairs={{0,4},{1,5},{2,6},{3,7},{4,0},{5,1},{6,2},{7,3},{8,12},{9,13},{10,... | collective-permute-start | bytes 294920 | tf_op jit(solution)/shard_map/ppermute | solution.py:613
  23.1 0.2 copy.23
  23.3 0.7 collective-permute-done.4.passed
  24.0 15.3 %shard_map.120 = (f32[19,32,128]{2,1,0:T(8,128)S(1)}, f32[19,32,128]{2,1,0:T(8,128)S(1)}, f32[192,128]{1,0:T(8,128)S(1)}, f32[2,2,2,8,128]{4,3,2,1,0:T(8,128)S(1)}, f32[2304,128]{1,0:T(8,128)}) custom-call(s32[1]{0:T(128)} %bitcast.place, s32[4,32]{1,0:T(4,128)S(1)} %bitcast.38, s32[1,6]{1,0:T(1,128)S(1)} %bitcast.42, s32[1,6]{1,0:T(1,128)S(1)} %bitcast.46, ...), custom_call_target="tpu_custom_call" | custom-call | flops 14000000000 | bytes 1048576 | tf_op jit(solution)/shard_map/pallas_call | solution.py:593
  39.4 0.4 collective-permute-start.5
  39.8 0.9 collective-permute-done.5.swapped
  40.8 4.1 %collective-permute-start.6 = (f32[128,128]{1,0:T(8,128)S(1)}, f32[128,128]{1,0:T(8,128)S(1)}, u32[]{:S(2)}, u32[]{:S(2)}) collective-permute-start(f32[128,128]{1,0:T(8,128)S(1)} %pad_maximum_fusion.4), channel_id=1, source_target_pairs={{0,8},{1,9},{2,10},{3,11},{4,124},{5,125},{6,126},{7,127},{8,16},{... | collective-permute-start | bytes 196616 | tf_op jit(solution)/shard_map/ppermute | solution.py:613
  44.8 1.7 %collective-permute-start.7 = (f32[128,128]{1,0:T(8,128)S(1)}, f32[128,128]{1,0:T(8,128)S(1)}, u32[]{:S(2)}, u32[]{:S(2)}) collective-permute-start(f32[128,128]{1,0:T(8,128)S(1)} %pad_maximum_fusion.5), channel_id=1, source_target_pairs={{0,1},{1,2},{2,3},{3,0},{4,7},{5,4},{6,5},{7,6},{8,9},{9,10},{10,1... | collective-permute-start | bytes 196616 | tf_op jit(solution)/shard_map/ppermute | solution.py:613
  46.6 1.7 %collective-permute-done.7.z_got = f32[128,128]{1,0:T(8,128)S(1)} collective-permute-done((f32[128,128]{1,0:T(8,128)S(1)}, f32[128,128]{1,0:T(8,128)S(1)}, u32[]{:S(2)}, u32[]{:S(2)}) %collective-permute-start.7) | collective-permute-done | bytes 65568 | tf_op jit(solution)/shard_map/ppermute | solution.py:613
  48.3 2.5 %collective-permute-start.9 = (f32[192,128]{1,0:T(8,128)S(1)}, f32[192,128]{1,0:T(8,128)S(1)}, u32[]{:S(2)}, u32[]{:S(2)}) collective-permute-start(f32[192,128]{1,0:T(8,128)S(1)} %pad_maximum_fusion.1), channel_id=1, source_target_pairs={{0,4},{1,5},{2,6},{3,7},{4,0},{5,1},{6,2},{7,3},{8,12},{9,13},{10,... | collective-permute-start | bytes 294920 | tf_op jit(solution)/shard_map/ppermute | solution.py:613
  50.7 0.9 collective-permute-done.9.passed
  51.7 12.2 %shard_map.121 = (f32[2304,128]{1,0:T(8,128)S(1)}, f32[19,32,128]{2,1,0:T(8,128)}) custom-call(s32[1]{0:T(128)} %bitcast.place, s32[4,32]{1,0:T(4,128)S(1)} %bitcast.39, s32[1,6]{1,0:T(1,128)S(1)} %bitcast.43, s32[1,6]{1,0:T(1,128)S(1)} %bitcast.47, f32[19,32,128]{2,1,0:T(8,128)S(1)} %bitcast.33, f32[19,32,128]{2,1,0:T(8,128)S(1)} %get-tuple-element.39.local1, ...), custom_call_target="tpu_custom_call" | custom-call | flops 8000000000 | bytes 1048576 | tf_op jit(solution)/shard_map/pallas_call | solution.py:593
  63.9 0.4 collective-permute-start.10
  64.4 1.6 %collective-permute-done.10.arrived = f32[1152,128]{1,0:T(8,128)S(1)} collective-permute-done((f32[1152,128]{1,0:T(8,128)S(1)}, f32[1152,128]{1,0:T(8,128)S(1)}, u32[]{:S(2)}, u32[]{:S(2)}) %collective-permute-start.10) | collective-permute-done | bytes 589856 | tf_op jit(solution)/shard_map/ppermute | solution.py:613
  66.0 0.1 shard_map.122
  66.1 18.3 %all_to_all.10 = f32[64,1,2304]{2,1,0:T(1,128)S(1)} all-to-all(f32[64,1,2304]{2,1,0:T(1,128)S(1)} %bitcast.23), channel_id=1, replica_groups=mesh['bx'=4,'by'=4,'core'=2,'slab'=4] {'bx','by','slab'}, dimensions={0} | all-to-all | bytes 1179648 | tf_op jit(solution)/shard_map/all_to_all | solution.py:640
  84.5 0.4 reduce_sum.9
  84.8 0.3 broadcast_in_dim.4
  85.1 15.9 %all_to_all.11 = f32[64,1,2304]{2,1,0:T(1,128)S(1)} all-to-all(f32[64,1,2304]{2,1,0:T(1,128)S(1)} %broadcast_in_dim.4), channel_id=1, replica_groups=mesh['bx'=4,'by'=4,'core'=2,'slab'=4] {'bx','by','slab'}, dimensions={0} | all-to-all | bytes 1179648 | tf_op jit(solution)/shard_map/all_to_all | solution.py:642
  101.1 3.5 %collective-permute-start.11 = (f32[1152,128]{1,0:T(8,128)S(1)}, f32[1152,128]{1,0:T(8,128)S(1)}, u32[]{:S(2)}, u32[]{:S(2)}) collective-permute-start(f32[1152,128]{1,0:T(8,128)S(1)} %bitcast.24), channel_id=1, source_target_pairs={{0,4},{1,5},{2,6},{3,7},{4,0},{5,1},{6,2},{7,3},{8,12},{9,13},{10,... | collective-permute-start | bytes 1769480 | tf_op jit(solution)/shard_map/ppermute | solution.py:613
  104.6 1.7 %shard_map.123 = f32[19,32,128]{2,1,0:T(8,128)} custom-call(s32[1]{0:T(128)} %bitcast.place, s32[4,32]{1,0:T(4,128)S(1)} %bitcast.40, s32[1,6]{1,0:T(1,128)S(1)} %bitcast.44, s32[1,6]{1,0:T(1,128)S(1)} %bitcast.48, f32[19,32,128]{2,1,0:T(8,128)S(1)} %get-tuple-element.50.post2, f32[192,128]{1,0:T(8,128)S(1)} %collective-permute-done.5.swapped, ...), custom_call_target="tpu_custom_call" | custom-call | flops 500000000 | bytes 1048576 | tf_op jit(solution)/shard_map/pallas_call | solution.py:593
  106.3 1.2 %shard_map.124 = (f32[19,512]{1,0:T(8,128)}, f32[512,512]{1,0:T(8,128)}, f32[19,512]{1,0:T(8,128)}) custom-call(s32[1]{0:T(128)} %bitcast.place, f32[1152,128]{1,0:T(8,128)S(1)} %bitcast.25, f32[1152,128]{1,0:T(8,128)S(1)} %collective-permute-done.11.other), custom_call_target="tpu_custom_call" | custom-call | flops 10000000 | bytes 1048576 | tf_op jit(solution)/shard_map/pallas_call | solution.py:593
  (30 shorter events, 0.2 us)
Async XLA Ops:
  0.6 22.4 %copy-start = (bf16[1,512,512]{2,1,0:T(8,128)(2,1)S(1)}, bf16[1,512,512]{2,1,0:T(8,128)(2,1)}, u32[]{:S(2)}) copy-start(bf16[1,512,512]{2,1,0:T(8,128)(2,1)} %param.10) | copy-start | bytes 1572868
  7.9 16.1 %copy-start.2 = (bf16[512,19]{0,1:T(8,128)(2,1)S(1)}, bf16[512,19]{0,1:T(8,128)(2,1)}, u32[]{:S(2)}) copy-start(bf16[512,19]{0,1:T(8,128)(2,1)} %param.9) | copy-start | bytes 58372
  8.0 16.1 %copy-start.3 = (bf16[19,512]{1,0:T(8,128)(2,1)S(1)}, bf16[19,512]{1,0:T(8,128)(2,1)}, u32[]{:S(2)}) copy-start(bf16[19,512]{1,0:T(8,128)(2,1)} %w_out.3) | copy-start | bytes 58372
  8.0 16.0 %copy-start.4 = (s32[32,4]{0,1:T(4,128)S(1)}, s32[32,4]{0,1:T(4,128)}, u32[]{:S(2)}) copy-start(s32[32,4]{0,1:T(4,128)} %param.13) | copy-start | bytes 1540
  8.0 16.0 %copy-start.5 = (s32[1,1,6]{2,1,0:T(1,128)S(1)}, s32[1,1,6]{2,1,0:T(1,128)}, u32[]{:S(2)}) copy-start(s32[1,1,6]{2,1,0:T(1,128)} %param.14) | copy-start | bytes 76
  8.0 16.0 %copy-start.6 = (s32[1,1,6]{2,1,0:T(1,128)S(1)}, s32[1,1,6]{2,1,0:T(1,128)}, u32[]{:S(2)}) copy-start(s32[1,1,6]{2,1,0:T(1,128)} %param.15) | copy-start | bytes 76
  8.0 4.5 %collective-permute-start = (f32[192,128]{1,0:T(8,128)S(1)}, f32[192,128]{1,0:T(8,128)S(1)}, u32[]{:S(2)}, u32[]{:S(2)}) collective-permute-start(f32[192,128]{1,0:T(8,128)S(1)} %get-tuple-element.33), channel_id=1, source_target_pairs={{0,4},{1,5},{2,6},{3,7},{4,0},{5,1},{6,2},{7,3},{8,12},{9,13},{10,... | collective-permute-start | bytes 294920 | tf_op jit(solution)/shard_map/ppermute | solution.py:613
  9.5 9.8 %collective-permute-start.3 = (f32[192,128]{1,0:T(8,128)S(1)}, f32[192,128]{1,0:T(8,128)S(1)}, u32[]{:S(2)}, u32[]{:S(2)}) collective-permute-start(f32[192,128]{1,0:T(8,128)S(1)} %get-tuple-element.33), channel_id=1, source_target_pairs={{0,116},{1,117},{2,118},{3,119},{4,16},{5,17},{6,18},{7,19},{8,124... | collective-permute-start | bytes 294920 | tf_op jit(solution)/shard_map/ppermute | solution.py:613
  12.5 6.8 %collective-permute-start.1 = (f32[128,128]{1,0:T(8,128)S(1)}, f32[128,128]{1,0:T(8,128)S(1)}, u32[]{:S(2)}, u32[]{:S(2)}) collective-permute-start(f32[128,128]{1,0:T(8,128)S(1)} %pad_maximum_fusion.2), channel_id=1, source_target_pairs={{0,8},{1,9},{2,10},{3,11},{4,124},{5,125},{6,126},{7,127},{8,16},{... | collective-permute-start | bytes 196616 | tf_op jit(solution)/shard_map/ppermute | solution.py:613
  15.6 5.1 %collective-permute-start.2 = (f32[128,128]{1,0:T(8,128)S(1)}, f32[128,128]{1,0:T(8,128)S(1)}, u32[]{:S(2)}, u32[]{:S(2)}) collective-permute-start(f32[128,128]{1,0:T(8,128)S(1)} %pad_maximum_fusion.3), channel_id=1, source_target_pairs={{0,1},{1,2},{2,3},{3,0},{4,7},{5,4},{6,5},{7,6},{8,9},{9,10},{10,1... | collective-permute-start | bytes 196616 | tf_op jit(solution)/shard_map/ppermute | solution.py:613
  20.7 3.3 %collective-permute-start.4 = (f32[192,128]{1,0:T(8,128)S(1)}, f32[192,128]{1,0:T(8,128)S(1)}, u32[]{:S(2)}, u32[]{:S(2)}) collective-permute-start(f32[192,128]{1,0:T(8,128)S(1)} %pad_maximum_fusion), channel_id=1, source_target_pairs={{0,4},{1,5},{2,6},{3,7},{4,0},{5,1},{6,2},{7,3},{8,12},{9,13},{10,... | collective-permute-start | bytes 294920 | tf_op jit(solution)/shard_map/ppermute | solution.py:613
  24.0 27.6 %copy-start.1 = (f32[19,1,1,4096]{3,2,1,0:T(1,128)S(1)}, f32[19,1,1,4096]{3,2,1,0:T(1,128)}, u32[]{:S(2)}) copy-start(f32[19,1,1,4096]{3,2,1,0:T(1,128)} %param.8) | copy-start | bytes 933892
  39.4 1.4 %collective-permute-start.5 = (f32[192,128]{1,0:T(8,128)S(1)}, f32[192,128]{1,0:T(8,128)S(1)}, u32[]{:S(2)}, u32[]{:S(2)}) collective-permute-start(f32[192,128]{1,0:T(8,128)S(1)} %get-tuple-element.40), channel_id=1, source_target_pairs={{0,4},{1,5},{2,6},{3,7},{4,0},{5,1},{6,2},{7,3},{8,12},{9,13},{10,... | collective-permute-start | bytes 294920 | tf_op jit(solution)/shard_map/ppermute | solution.py:613
  39.8 6.8 %collective-permute-start.8 = (f32[192,128]{1,0:T(8,128)S(1)}, f32[192,128]{1,0:T(8,128)S(1)}, u32[]{:S(2)}, u32[]{:S(2)}) collective-permute-start(f32[192,128]{1,0:T(8,128)S(1)} %get-tuple-element.40), channel_id=1, source_target_pairs={{0,116},{1,117},{2,118},{3,119},{4,16},{5,17},{6,18},{7,19},{8,124... | collective-permute-start | bytes 294920 | tf_op jit(solution)/shard_map/ppermute | solution.py:613
  40.8 5.8 %collective-permute-start.6 = (f32[128,128]{1,0:T(8,128)S(1)}, f32[128,128]{1,0:T(8,128)S(1)}, u32[]{:S(2)}, u32[]{:S(2)}) collective-permute-start(f32[128,128]{1,0:T(8,128)S(1)} %pad_maximum_fusion.4), channel_id=1, source_target_pairs={{0,8},{1,9},{2,10},{3,11},{4,124},{5,125},{6,126},{7,127},{8,16},{... | collective-permute-start | bytes 196616 | tf_op jit(solution)/shard_map/ppermute | solution.py:613
  44.8 3.4 %collective-permute-start.7 = (f32[128,128]{1,0:T(8,128)S(1)}, f32[128,128]{1,0:T(8,128)S(1)}, u32[]{:S(2)}, u32[]{:S(2)}) collective-permute-start(f32[128,128]{1,0:T(8,128)S(1)} %pad_maximum_fusion.5), channel_id=1, source_target_pairs={{0,1},{1,2},{2,3},{3,0},{4,7},{5,4},{6,5},{7,6},{8,9},{9,10},{10,1... | collective-permute-start | bytes 196616 | tf_op jit(solution)/shard_map/ppermute | solution.py:613
  48.3 3.4 %collective-permute-start.9 = (f32[192,128]{1,0:T(8,128)S(1)}, f32[192,128]{1,0:T(8,128)S(1)}, u32[]{:S(2)}, u32[]{:S(2)}) collective-permute-start(f32[192,128]{1,0:T(8,128)S(1)} %pad_maximum_fusion.1), channel_id=1, source_target_pairs={{0,4},{1,5},{2,6},{3,7},{4,0},{5,1},{6,2},{7,3},{8,12},{9,13},{10,... | collective-permute-start | bytes 294920 | tf_op jit(solution)/shard_map/ppermute | solution.py:613
  63.9 2.1 %collective-permute-start.10 = (f32[1152,128]{1,0:T(8,128)S(1)}, f32[1152,128]{1,0:T(8,128)S(1)}, u32[]{:S(2)}, u32[]{:S(2)}) collective-permute-start(f32[1152,128]{1,0:T(8,128)S(1)} %dynamic-slice_bitcast_fusion), channel_id=1, source_target_pairs={{0,4},{1,5},{2,6},{3,7},{4,0},{5,1},{6,2},{7,3},{8,12},{9,13},{10,... | collective-permute-start | bytes 1769480 | tf_op jit(solution)/shard_map/ppermute | solution.py:613
  101.1 5.3 %collective-permute-start.11 = (f32[1152,128]{1,0:T(8,128)S(1)}, f32[1152,128]{1,0:T(8,128)S(1)}, u32[]{:S(2)}, u32[]{:S(2)}) collective-permute-start(f32[1152,128]{1,0:T(8,128)S(1)} %bitcast.24), channel_id=1, source_target_pairs={{0,4},{1,5},{2,6},{3,7},{4,0},{5,1},{6,2},{7,3},{8,12},{9,13},{10,... | collective-permute-start | bytes 1769480 | tf_op jit(solution)/shard_map/ppermute | solution.py:613

commit v6 on v2

--- a/solution.py
+++ b/solution.py
@@ -23,6 +23,9 @@
 BF16 = jnp.bfloat16
 GROWS = 2304
 HALF = GROWS // 2
+Y_AT = 48
+Z_AT = Y_AT + 64
+FAR_ROWS = 104
 OUT_AT = 4 * HID
 IN_AT = OUT_AT + 4 * 24
 
@@ -270,22 +273,22 @@
     cases = [
         (at(1), swapped, 0),
         (at(-2), x_got, 0),
-        (at(-1), x_got, 64),
+        (at(-1), x_got, Y_AT),
         (at(3), passed, 0),
-        (at(2), passed, 64),
+        (at(2), passed, Y_AT),
         (at(-3), far, 0),
     ]
     return lambda f, r: sum_where(
         [
-            (d == spot, ref[pl.ds(start + 8 * (kind * 4 + f * 2 + r), 8), :])
+            (d == spot, ref[pl.ds(start + 5 * (kind * 4 + f * 2 + r), 8), :])
             for spot, ref, start in cases
         ]
     )
 
 
-def choose_z(info, got, kind):
-    direct = got[2][pl.ds(32 * kind, 32), :]
-    passed = got[4][pl.ds(128 + 32 * kind, 32), :]
+def choose_z(info, got):
+    direct = got[2][pl.ds(0, 32), :]
+    passed = got[4][pl.ds(2 * Y_AT, 32), :]
     even = info.block() & 1 == 0
     return jnp.where(even, direct, passed), jnp.where(even, passed, direct)
 
@@ -297,7 +300,22 @@
     return total
 
 
-def stream_back(info, bar, local, xs, sends, work, y_two, z_two):
+def put_x_rows(sends, xs, kind):
+    for f in (0, 1):
+        for r in (0, 1):
+            sends[pl.ds(5 * (kind * 4 + f * 2 + r), 5), :] = xs[kind, f, r, pl.ds(0, 5), :]
+
+
+def put_z_rows(info, sends, z_keep):
+    low = iota(ROWS, 1) & 15 < 8
+    up = jnp.where(low, z_keep[0], z_keep[1])
+    down = jnp.where(low, z_keep[1], z_keep[0])
+    even = info.block() & 1 == 0
+    sends[pl.ds(Z_AT, 32), :] = jnp.where(even, up, down)
+    sends[pl.ds(Z_AT + 32, 32), :] = jnp.where(even, down, up)
+
+
+def stream_back(info, bar, local, xs, sends, z_keep, work, y_two, z_two):
     for q in range(Q):
         v = bar[q]
         if is_edge(q):
@@ -319,9 +337,9 @@
     pack_faces(work, put_x, put_y, put_z)
     gather_x(info, x_four)
     gather_y(info, y_two)
-    sends[pl.ds(160, 32), :] = gather_z(info, z_two)
-    sends[pl.ds(32, 32), :] = xs[1].reshape(32, 128)
-    sends[pl.ds(96, 32), :] = y_two[...].reshape(32, 128)
+    z_keep[1] = gather_z(info, z_two)
+    put_x_rows(sends, xs, 1)
+    sends[pl.ds(Y_AT + 32, 32), :] = y_two[...].reshape(32, 128)
     row, lane = iota(ROWS, 0), iota(ROWS, 1)
     coords = [row >> 1, (row & 1) * 8 + (lane >> 4), lane & 15]
     for q in range(Q):
@@ -339,7 +357,7 @@
         local[q] = v
 
 
-def send_post(post, xs, sends):
+def send_post(post, xs, sends, z_keep):
     x_four = xs.at[0]
     x_four[...] = jnp.zeros(x_four.shape, F32)
 
@@ -347,13 +365,13 @@
         x_four[f, r, pl.ds(i, 1), :] = v
 
     def put_y(f, v):
-        sends[pl.ds(64 + 16 * f, 16), :] = v
+        sends[pl.ds(Y_AT + 16 * f, 16), :] = v
 
     def put_z(v):
-        sends[pl.ds(128, 32), :] = v
+        z_keep[0] = v
 
     pack_faces(post, put_x, put_y, put_z)
-    sends[pl.ds(0, 32), :] = xs[0].reshape(32, 128)
+    put_x_rows(sends, xs, 0)
 
 
 def stream(info, post, got, out, work, x_four, y_two, z_two):
@@ -363,10 +381,10 @@
         for r in (0, 1):
             x_four[f, r] = pick(f, r)
     refine_x(info, x_four)
-    y_two[0] = swapped[pl.ds(64, 16), :]
-    y_two[1] = swapped[pl.ds(80, 16), :]
+    y_two[0] = swapped[pl.ds(Y_AT, 16), :]
+    y_two[1] = swapped[pl.ds(Y_AT + 16, 16), :]
     refine_y(info, y_two)
-    z_two[0], z_two[1] = choose_z(info, got, 0)
+    z_two[0], z_two[1] = choose_z(info, got)
     z = refine_z(info, z_two)
     work[...] = post[...]
     unpack_faces(work, lambda f, r, i: x_four[f, r, pl.ds(i, 1), :], y_two, z, False)
@@ -383,9 +401,9 @@
         pick = choose_x(info, f, got, 1)
         for r in (0, 1):
             x_four[f, r] = pick(f, r)
-    y_two[0] = swapped[pl.ds(96, 16), :]
-    y_two[1] = swapped[pl.ds(112, 16), :]
-    below, above = choose_z(info, got, 1)
+    y_two[0] = swapped[pl.ds(Y_AT + 32, 16), :]
+    y_two[1] = swapped[pl.ds(Y_AT + 48, 16), :]
+    below, above = choose_z(info, got)
     z = jnp.where(iota(ROWS, 1) & 15 < 8, above, below)
     unpack_faces(bar, lambda f, r, i: x_four[f, r, pl.ds(i, 1), :], y_two, z, True)
 
@@ -462,7 +480,7 @@
 def first_kernel(place, source_far, level_far, quadrant_far, f0_far, cot_far, w_in_far, w_mid_far,
                  w_out_far, post, local, sends, h0_far, h1_far,
                  source, level, quadrant, xs, f0, cot, w_in_t, w_mid, w_out, h0, h1, work, y_two, z_two,
-                 sems, out_sems):
+                 z_keep, sems, out_sems):
     info = Tables(place, source, level, quadrant)
     copies = Copies(sems)
     for far, near in ((cot_far, cot), (source_far, source), (level_far, level),
@@ -471,7 +489,7 @@
         copies.start(far, near)
     for copy in copies.made[:4]:
         copy.wait()
-    stream_back(info, cot, local, xs, sends, work, y_two, z_two)
+    stream_back(info, cot, local, xs, sends, z_keep, work, y_two, z_two)
     for copy in copies.made[4:]:
         copy.wait()
     copies = Copies(out_sems)
@@ -482,13 +500,14 @@
         h1[:, span(step)] = b
         copies.start(h1.at[:, span(step)], h1_far.at[:, span(step)])
         put_cells(post, step, out)
-    send_post(post, xs, sends)
+    send_post(post, xs, sends, z_keep)
+    put_z_rows(info, sends, z_keep)
     copies.wait()
 
 
 def second_kernel(place, source, level, quadrant, post1, local2, swapped, x_got, z_got, far, passed,
                   w_in_t, w_mid, w_mid_t, w_out, post, local, sends, grads_far,
-                  grads, xs, x, e, h0, h1, a0, a1, f1, pbar, fbar, work, x_four, y_two, z_two, sem):
+                  grads, xs, x, e, h0, h1, a0, a1, f1, pbar, fbar, work, x_four, y_two, z_two, z_keep, sem):
     info = Tables(place, source, level, quadrant)
     got = (swapped, x_got, z_got, far, passed)
     stream(info, post1, got, f1, work, x_four, y_two, z_two)
@@ -511,8 +530,9 @@
     put_grads(grads, x, e, h0, h1, a0, a1, None)
     copies = Copies(sem)
     copies.start(grads, grads_far)
-    send_post(post, xs, sends)
-    stream_back(info, fbar, local, xs, sends, work, y_two, z_two)
+    send_post(post, xs, sends, z_keep)
+    stream_back(info, fbar, local, xs, sends, z_keep, work, y_two, z_two)
+    put_z_rows(info, sends, z_keep)
     copies.wait()
 
 
@@ -548,6 +568,11 @@
     stream(info, post2, (swapped, x_got, z_got, far, passed), out, work, x_four, y_two, z_two)
 
 
+def add_kernel(place, grads, arrived, mine):
+    half = pl.ds(pl.multiple_of((place[0] & 1) * HALF, HALF), HALF)
+    mine[...] = grads[half, :] + arrived[...]
+
+
 def unpack_kernel(place, mine, other, g_in, g_mid, g_out, whole):
     scale = float(NB * NZ * CELLS) ** -0.5
     core = place[0] & 1
@@ -563,7 +588,7 @@
 BLOCK = (Q, ROWS, 128)
 HIDDEN = (HID, CELLS)
 THIN = (Q, CELLS)
-SENDS = (192, 128)
+SENDS = (Z_AT + 64, 128)
 X_TWO = (2, 2, 2, 8, 128)
 FACES = [(2, 2, 8, 128), (2, 16, 128), (2, ROWS, 128)]
 
@@ -610,33 +635,33 @@
 
 def exchange(sends):
     swapped = send(sends, lambda b, z: (b ^ 1, z))
-    far = send(sends[:64], lambda b, z: (b - 3 if b % 2 == 0 else b + 3, z))
+    far = send(sends[:FAR_ROWS], lambda b, z: (b - 3 if b % 2 == 0 else b + 3, z))
     x_got = send(
-        jnp.concatenate([sends[:64], swapped[:64]]),
+        jnp.concatenate([sends[:Y_AT], swapped[:Y_AT]]),
         lambda b, z: (b + 2 if b % 2 == 0 else b - 2, z),
     )
     z_got = send(
-        jnp.concatenate([sends[128:], swapped[128:]]),
+        jnp.concatenate([sends[Z_AT : Z_AT + 32], swapped[Z_AT + 32 :]]),
         lambda b, z: (b, z + 1 if b % 2 == 0 else z - 1),
     )
     x_got, z_got, far = lax.optimization_barrier((x_got, z_got, far))
-    passed = send(jnp.concatenate([x_got, z_got[64:]]), lambda b, z: (b ^ 1, z))
+    passed = send(jnp.concatenate([x_got, z_got[32:]]), lambda b, z: (b ^ 1, z))
     return swapped, x_got, z_got, far, passed
 
 
-def total_over_devices(grads, core, beside):
+def total_over_devices(grads, place, beside):
     def other_core(v):
         return send(v, lambda b, z: (b ^ 1, z))
 
     halves = grads.reshape(2, HALF, 128)
-    mine = lax.dynamic_index_in_dim(halves, core, 0, keepdims=False)
-    given = lax.dynamic_index_in_dim(halves, 1 - core, 0, keepdims=False)
-    arrived, beside = lax.optimization_barrier((other_core(given), beside))
-    mine = (mine + arrived).reshape(64, 1, HALF * 2)
+    given = lax.dynamic_index_in_dim(halves, 1 - place[0] % 2, 0, keepdims=False)
+    (mine,) = run(add_kernel, [place], [grads, other_core(given)], [(HALF, 128)], [], 10, 8)
+    mine = mine.reshape(64, 1, HALF * 2)
     mine = lax.all_to_all(mine, CHIPS, 0, 0, tiled=True).sum(axis=0, keepdims=True)
     mine = jnp.broadcast_to(mine, (64, 1, HALF * 2))
     mine = lax.all_to_all(mine, CHIPS, 0, 0, tiled=True).reshape(HALF, 128)
-    return mine, other_core(mine), beside
+    other, beside = lax.optimization_barrier((other_core(mine), beside))
+    return mine, other, beside
 
 
 def shards(populations, w_in, w_mid, w_out, cotangent, face_source, face_level, face_quadrant):
@@ -660,7 +685,7 @@
         [pltpu.SMEM((4, NB), jnp.int32), pltpu.SMEM((1, 6), jnp.int32),
          pltpu.SMEM((1, 6), jnp.int32), X_TWO,
          BLOCK, BLOCK, pltpu.VMEM((Q, HID), BF16), pltpu.VMEM((HID, HID), BF16),
-         pltpu.VMEM((Q, HID), BF16), near, near, BLOCK, *FACES[1:], sems((8,)),
+         pltpu.VMEM((Q, HID), BF16), near, near, BLOCK, *FACES[1:], FACES[2], sems((8,)),
          sems((2 * CHUNKS,))],
         4000, 32, range(8),
     )
@@ -668,7 +693,7 @@
     post2, local1, sends, grads2 = run(
         second_kernel, tables, [post1, local2, *got, w_in_t, w_mid, w_mid_t, w_out],
         [BLOCK, BLOCK, SENDS, pltpu.HBM(grad, F32)],
-        [grad, X_TWO, near_thin, near_thin, *[near] * 4, *[BLOCK] * 4, *FACES, sems((1,))],
+        [grad, X_TWO, near_thin, near_thin, *[near] * 4, *[BLOCK] * 4, *FACES, FACES[2], sems((1,))],
         14000, 32,
     )
     got = exchange(sends)
@@ -680,7 +705,7 @@
     )
     post2, grads = lax.optimization_barrier((post2, grads))
     (final,) = run(final_kernel, tables, [post2, *got], [BLOCK], [BLOCK, *FACES], 500, 8)
-    mine, other, final = total_over_devices(grads, place[0] % 2, final)
+    mine, other, final = total_over_devices(grads, place, final)
     g_in, g_mid, g_out = run(
         unpack_kernel, [place], [mine, other], [(Q, HID), (HID, HID), (Q, HID)], [grad], 10, 8
     )

time: 110 us -> 107 us (0.973)
  waiting for transfers between devices: 15.9 us -> 6.41 us
  starting transfers between devices: 18 us -> 26.2 us
  other arithmetic: 1.52 us -> 0.42 us
    ppermute x12, waiting for transfers between devices: 15.9 us -> 6.41 us  [send(): return lax.ppermute(value, AXES, pairs)]
    ppermute x12, starting transfers between devices: 18 us -> 26.2 us  [send(): return lax.ppermute(value, AXES, pairs)]
    add x1 -> x0, other arithmetic: 1.13 us -> none  [total_over_devices(): mine = (mine + arrived).reshape(64, 1, HALF * 2)]
    pallas_call x5 -> x6, Pallas kernels: 37.8 us -> 37.9 us  [run(): pl.pallas_call(kernel, out_shape=[shape(s) for s in outs], in_specs=in_sp...]
  transfers between devices with their start and end apart: 12 -> 12, of which waited for: 8 -> 6; matrix products, arithmetic and copies ran while one was open for 0% -> 0% of each run, Pallas kernels for 2% -> 2%
where the time goes in v6:
time: 107 us
  Pallas kernels  37.9 us (35%)
  blocking collectives  34.3 us (32%)
  starting transfers between devices  26.2 us (24%)
  waiting for transfers between devices  6.41 us (6%)
    pallas_call x6, Pallas kernels, run(): pl.pallas_call(kernel, out_shape=[shape(s) for s in outs], in_specs=in_sp...  37.9 us
    ppermute x12, starting transfers between devices, send(): return lax.ppermute(value, AXES, pairs)  26.2 us
    all_to_all x1, blocking collectives, total_over_devices(): lax.all_to_all(mine, CHIPS, 0, 0, tiled=True).sum(axis=0, keepdims=True)  18.4 us
    all_to_all x1, blocking collectives, total_over_devices(): mine = lax.all_to_all(mine, CHIPS, 0, 0, tiled=True).reshape(HALF, 128)  15.9 us
    ppermute x12, waiting for transfers between devices, send(): return lax.ppermute(value, AXES, pairs)  6.41 us
  transfers between devices with their start and end apart: 12, of which 6 were waited for; matrix products, arithmetic and copies ran while one was open for 0% of the time, Pallas kernels for 2%

profile of v6, /device:TPU:1, one launch (start us, length us, event | category | flops | bytes accessed | tf_op | source)
XLA Modules:
  0.0 106.8 jit_solution(9252080390598859052)
XLA Ops:
  0.7 7.3 %shard_map.119 = (f32[19,32,128]{2,1,0:T(8,128)S(1)}, f32[19,32,128]{2,1,0:T(8,128)S(1)}, f32[176,128]{1,0:T(8,128)S(1)}, bf16[512,4096]{1,0:T(8,128)(2,1)}, bf16[512,4096]{1,0:T(8,128)(2,1)}) custom-call(s32[1]{0:T(128)} %bitcast.place, s32[4,32]{1,0:T(4,128)} %bitcast.33, s32[1,6]{1,0:T(1,128)} %bitcast.37, s32[1,6]{1,0:T(1,128)} %bitcast.41, ...), custom_call_target="tpu_custom_call" | custom-call | flops 4000000000 | bytes 1048576 | tf_op jit(solution)/shard_map/pallas_call | solution.py:613
  8.0 0.0 copy-start.2
  8.0 0.0 copy-start.5
  8.0 0.0 copy-start.6
  8.0 1.5 %collective-permute-start = (f32[176,128]{1,0:T(8,128)S(1)}, f32[176,128]{1,0:T(8,128)S(1)}, u32[]{:S(2)}, u32[]{:S(2)}) collective-permute-start(f32[176,128]{1,0:T(8,128)S(1)} %get-tuple-element.31), channel_id=1, source_target_pairs={{0,4},{1,5},{2,6},{3,7},{4,0},{5,1},{6,2},{7,3},{8,12},{9,13},{10,... | collective-permute-start | bytes 270344 | tf_op jit(solution)/shard_map/ppermute | solution.py:633
  9.6 3.0 %collective-permute-start.3 = (f32[104,128]{1,0:T(8,128)S(1)}, f32[104,128]{1,0:T(8,128)S(1)}, u32[]{:S(2)}, u32[]{:S(2)}) collective-permute-start(f32[104,128]{1,0:T(8,128)S(1)} %slice.40), channel_id=1, source_target_pairs={{0,116},{1,117},{2,118},{3,119},{4,16},{5,17},{6,18},{7,19},{8,124... | collective-permute-start | bytes 159752 | tf_op jit(solution)/shard_map/ppermute | solution.py:633
  12.6 3.0 %collective-permute-start.1 = (f32[96,128]{1,0:T(8,128)S(1)}, f32[96,128]{1,0:T(8,128)S(1)}, u32[]{:S(2)}, u32[]{:S(2)}) collective-permute-start(f32[96,128]{1,0:T(8,128)S(1)} %pad_maximum_fusion.2), channel_id=1, source_target_pairs={{0,8},{1,9},{2,10},{3,11},{4,124},{5,125},{6,126},{7,127},{8,16},{... | collective-permute-start | bytes 147464 | tf_op jit(solution)/shard_map/ppermute | solution.py:633
  15.6 3.8 %collective-permute-start.2 = (f32[64,128]{1,0:T(8,128)S(1)}, f32[64,128]{1,0:T(8,128)S(1)}, u32[]{:S(2)}, u32[]{:S(2)}) collective-permute-start(f32[64,128]{1,0:T(8,128)S(1)} %pad_maximum_fusion.4), channel_id=1, source_target_pairs={{0,1},{1,2},{2,3},{3,0},{4,7},{5,4},{6,5},{7,6},{8,9},{9,10},{10,1... | collective-permute-start | bytes 98312 | tf_op jit(solution)/shard_map/ppermute | solution.py:633
  19.3 1.0 collective-permute-done.2.z_got
  20.4 2.6 %collective-permute-start.4 = (f32[128,128]{1,0:T(8,128)S(1)}, f32[128,128]{1,0:T(8,128)S(1)}, u32[]{:S(2)}, u32[]{:S(2)}) collective-permute-start(f32[128,128]{1,0:T(8,128)S(1)} %pad_maximum_fusion), channel_id=1, source_target_pairs={{0,4},{1,5},{2,6},{3,7},{4,0},{5,1},{6,2},{7,3},{8,12},{9,13},{10,... | collective-permute-start | bytes 196616 | tf_op jit(solution)/shard_map/ppermute | solution.py:633
  22.9 0.2 copy.23
  23.1 0.7 collective-permute-done.4.passed
  23.9 15.4 %shard_map.120 = (f32[19,32,128]{2,1,0:T(8,128)S(1)}, f32[19,32,128]{2,1,0:T(8,128)S(1)}, f32[176,128]{1,0:T(8,128)S(1)}, f32[2304,128]{1,0:T(8,128)}) custom-call(s32[1]{0:T(128)} %bitcast.place, s32[4,32]{1,0:T(4,128)S(1)} %bitcast.34, s32[1,6]{1,0:T(1,128)S(1)} %bitcast.38, s32[1,6]{1,0:T(1,128)S(1)} %bitcast.42, ...), custom_call_target="tpu_custom_call" | custom-call | flops 14000000000 | bytes 1048576 | tf_op jit(solution)/shard_map/pallas_call | solution.py:613
  39.3 0.4 collective-permute-start.5
  39.7 0.1 collective-permute-start.8
  39.8 0.8 collective-permute-done.5.swapped
  40.6 3.7 %collective-permute-start.6 = (f32[96,128]{1,0:T(8,128)S(1)}, f32[96,128]{1,0:T(8,128)S(1)}, u32[]{:S(2)}, u32[]{:S(2)}) collective-permute-start(f32[96,128]{1,0:T(8,128)S(1)} %pad_maximum_fusion.3), channel_id=1, source_target_pairs={{0,8},{1,9},{2,10},{3,11},{4,124},{5,125},{6,126},{7,127},{8,16},{... | collective-permute-start | bytes 147464 | tf_op jit(solution)/shard_map/ppermute | solution.py:633
  44.3 1.7 %collective-permute-start.7 = (f32[64,128]{1,0:T(8,128)S(1)}, f32[64,128]{1,0:T(8,128)S(1)}, u32[]{:S(2)}, u32[]{:S(2)}) collective-permute-start(f32[64,128]{1,0:T(8,128)S(1)} %pad_maximum_fusion.5), channel_id=1, source_target_pairs={{0,1},{1,2},{2,3},{3,0},{4,7},{5,4},{6,5},{7,6},{8,9},{9,10},{10,1... | collective-permute-start | bytes 98312 | tf_op jit(solution)/shard_map/ppermute | solution.py:633
  46.1 1.3 %collective-permute-done.7.z_got = f32[64,128]{1,0:T(8,128)S(1)} collective-permute-done((f32[64,128]{1,0:T(8,128)S(1)}, f32[64,128]{1,0:T(8,128)S(1)}, u32[]{:S(2)}, u32[]{:S(2)}) %collective-permute-start.7) | collective-permute-done | bytes 32800 | tf_op jit(solution)/shard_map/ppermute | solution.py:633
  47.4 2.6 %collective-permute-start.9 = (f32[128,128]{1,0:T(8,128)S(1)}, f32[128,128]{1,0:T(8,128)S(1)}, u32[]{:S(2)}, u32[]{:S(2)}) collective-permute-start(f32[128,128]{1,0:T(8,128)S(1)} %pad_maximum_fusion.1), channel_id=1, source_target_pairs={{0,4},{1,5},{2,6},{3,7},{4,0},{5,1},{6,2},{7,3},{8,12},{9,13},{10,... | collective-permute-start | bytes 196616 | tf_op jit(solution)/shard_map/ppermute | solution.py:633
  50.0 0.9 collective-permute-done.9.passed
  50.9 12.2 %shard_map.121 = (f32[2304,128]{1,0:T(8,128)S(1)}, f32[19,32,128]{2,1,0:T(8,128)}) custom-call(s32[1]{0:T(128)} %bitcast.place, s32[4,32]{1,0:T(4,128)S(1)} %bitcast.35, s32[1,6]{1,0:T(1,128)S(1)} %bitcast.39, s32[1,6]{1,0:T(1,128)S(1)} %bitcast.43, f32[19,32,128]{2,1,0:T(8,128)S(1)} %bitcast.29, f32[19,32,128]{2,1,0:T(8,128)S(1)} %get-tuple-element.36.local1, ...), custom_call_target="tpu_custom_call" | custom-call | flops 8000000000 | bytes 1048576 | tf_op jit(solution)/shard_map/pallas_call | solution.py:613
  63.1 0.4 collective-permute-start.10
  63.6 1.6 %collective-permute-done.10.arrived = f32[1152,128]{1,0:T(8,128)S(1)} collective-permute-done((f32[1152,128]{1,0:T(8,128)S(1)}, f32[1152,128]{1,0:T(8,128)S(1)}, u32[]{:S(2)}, u32[]{:S(2)}) %collective-permute-start.10) | collective-permute-done | bytes 589856 | tf_op jit(solution)/shard_map/ppermute | solution.py:633
  65.2 0.1 shard_map.122
  65.3 18.4 %all_to_all.10 = f32[64,1,2304]{2,1,0:T(1,128)S(1)} all-to-all(f32[64,1,2304]{2,1,0:T(1,128)S(1)} %bitcast.21), channel_id=1, replica_groups=mesh['bx'=4,'by'=4,'core'=2,'slab'=4] {'bx','by','slab'}, dimensions={0} | all-to-all | bytes 1179648 | tf_op jit(solution)/shard_map/all_to_all | solution.py:660
  83.7 0.4 reduce_sum.9
  84.1 0.3 broadcast_in_dim.4
  84.4 15.9 %all_to_all.11 = f32[64,1,2304]{2,1,0:T(1,128)S(1)} all-to-all(f32[64,1,2304]{2,1,0:T(1,128)S(1)} %broadcast_in_dim.4), channel_id=1, replica_groups=mesh['bx'=4,'by'=4,'core'=2,'slab'=4] {'bx','by','slab'}, dimensions={0} | all-to-all | bytes 1179648 | tf_op jit(solution)/shard_map/all_to_all | solution.py:662
  100.3 3.5 %collective-permute-start.11 = (f32[1152,128]{1,0:T(8,128)S(1)}, f32[1152,128]{1,0:T(8,128)S(1)}, u32[]{:S(2)}, u32[]{:S(2)}) collective-permute-start(f32[1152,128]{1,0:T(8,128)S(1)} %bitcast.22), channel_id=1, source_target_pairs={{0,4},{1,5},{2,6},{3,7},{4,0},{5,1},{6,2},{7,3},{8,12},{9,13},{10,... | collective-permute-start | bytes 1769480 | tf_op jit(solution)/shard_map/ppermute | solution.py:633
  103.9 1.7 %shard_map.123 = f32[19,32,128]{2,1,0:T(8,128)} custom-call(s32[1]{0:T(128)} %bitcast.place, s32[4,32]{1,0:T(4,128)S(1)} %bitcast.36, s32[1,6]{1,0:T(1,128)S(1)} %bitcast.40, s32[1,6]{1,0:T(1,128)S(1)} %bitcast.44, f32[19,32,128]{2,1,0:T(8,128)S(1)} %get-tuple-element.46.post2, f32[176,128]{1,0:T(8,128)S(1)} %collective-permute-done.5.swapped, ...), custom_call_target="tpu_custom_call" | custom-call | flops 500000000 | bytes 1048576 | tf_op jit(solution)/shard_map/pallas_call | solution.py:613
  105.6 1.2 %shard_map.124 = (f32[19,512]{1,0:T(8,128)}, f32[512,512]{1,0:T(8,128)}, f32[19,512]{1,0:T(8,128)}) custom-call(s32[1]{0:T(128)} %bitcast.place, f32[1152,128]{1,0:T(8,128)S(1)} %bitcast.23, f32[1152,128]{1,0:T(8,128)S(1)} %collective-permute-done.11.other), custom_call_target="tpu_custom_call" | custom-call | flops 10000000 | bytes 1048576 | tf_op jit(solution)/shard_map/pallas_call | solution.py:613
  (36 shorter events, 0.2 us)
Async XLA Ops:
  0.6 22.3 %copy-start = (bf16[1,512,512]{2,1,0:T(8,128)(2,1)S(1)}, bf16[1,512,512]{2,1,0:T(8,128)(2,1)}, u32[]{:S(2)}) copy-start(bf16[1,512,512]{2,1,0:T(8,128)(2,1)} %param.10) | copy-start | bytes 1572868
  8.0 15.8 %copy-start.2 = (bf16[512,19]{0,1:T(8,128)(2,1)S(1)}, bf16[512,19]{0,1:T(8,128)(2,1)}, u32[]{:S(2)}) copy-start(bf16[512,19]{0,1:T(8,128)(2,1)} %param.9) | copy-start | bytes 58372
  8.0 15.8 %copy-start.3 = (bf16[19,512]{1,0:T(8,128)(2,1)S(1)}, bf16[19,512]{1,0:T(8,128)(2,1)}, u32[]{:S(2)}) copy-start(bf16[19,512]{1,0:T(8,128)(2,1)} %w_out.3) | copy-start | bytes 58372
  8.0 15.8 %copy-start.4 = (s32[32,4]{0,1:T(4,128)S(1)}, s32[32,4]{0,1:T(4,128)}, u32[]{:S(2)}) copy-start(s32[32,4]{0,1:T(4,128)} %param.13) | copy-start | bytes 1540
  8.0 15.8 %copy-start.5 = (s32[1,1,6]{2,1,0:T(1,128)S(1)}, s32[1,1,6]{2,1,0:T(1,128)}, u32[]{:S(2)}) copy-start(s32[1,1,6]{2,1,0:T(1,128)} %param.14) | copy-start | bytes 76
  8.0 15.8 %copy-start.6 = (s32[1,1,6]{2,1,0:T(1,128)S(1)}, s32[1,1,6]{2,1,0:T(1,128)}, u32[]{:S(2)}) copy-start(s32[1,1,6]{2,1,0:T(1,128)} %param.15) | copy-start | bytes 76
  8.0 4.5 %collective-permute-start = (f32[176,128]{1,0:T(8,128)S(1)}, f32[176,128]{1,0:T(8,128)S(1)}, u32[]{:S(2)}, u32[]{:S(2)}) collective-permute-start(f32[176,128]{1,0:T(8,128)S(1)} %get-tuple-element.31), channel_id=1, source_target_pairs={{0,4},{1,5},{2,6},{3,7},{4,0},{5,1},{6,2},{7,3},{8,12},{9,13},{10,... | collective-permute-start | bytes 270344 | tf_op jit(solution)/shard_map/ppermute | solution.py:633
  9.6 9.8 %collective-permute-start.3 = (f32[104,128]{1,0:T(8,128)S(1)}, f32[104,128]{1,0:T(8,128)S(1)}, u32[]{:S(2)}, u32[]{:S(2)}) collective-permute-start(f32[104,128]{1,0:T(8,128)S(1)} %slice.40), channel_id=1, source_target_pairs={{0,116},{1,117},{2,118},{3,119},{4,16},{5,17},{6,18},{7,19},{8,124... | collective-permute-start | bytes 159752 | tf_op jit(solution)/shard_map/ppermute | solution.py:633
  12.6 7.8 %collective-permute-start.1 = (f32[96,128]{1,0:T(8,128)S(1)}, f32[96,128]{1,0:T(8,128)S(1)}, u32[]{:S(2)}, u32[]{:S(2)}) collective-permute-start(f32[96,128]{1,0:T(8,128)S(1)} %pad_maximum_fusion.2), channel_id=1, source_target_pairs={{0,8},{1,9},{2,10},{3,11},{4,124},{5,125},{6,126},{7,127},{8,16},{... | collective-permute-start | bytes 147464 | tf_op jit(solution)/shard_map/ppermute | solution.py:633
  15.6 4.8 %collective-permute-start.2 = (f32[64,128]{1,0:T(8,128)S(1)}, f32[64,128]{1,0:T(8,128)S(1)}, u32[]{:S(2)}, u32[]{:S(2)}) collective-permute-start(f32[64,128]{1,0:T(8,128)S(1)} %pad_maximum_fusion.4), channel_id=1, source_target_pairs={{0,1},{1,2},{2,3},{3,0},{4,7},{5,4},{6,5},{7,6},{8,9},{9,10},{10,1... | collective-permute-start | bytes 98312 | tf_op jit(solution)/shard_map/ppermute | solution.py:633
  20.4 3.5 %collective-permute-start.4 = (f32[128,128]{1,0:T(8,128)S(1)}, f32[128,128]{1,0:T(8,128)S(1)}, u32[]{:S(2)}, u32[]{:S(2)}) collective-permute-start(f32[128,128]{1,0:T(8,128)S(1)} %pad_maximum_fusion), channel_id=1, source_target_pairs={{0,4},{1,5},{2,6},{3,7},{4,0},{5,1},{6,2},{7,3},{8,12},{9,13},{10,... | collective-permute-start | bytes 196616 | tf_op jit(solution)/shard_map/ppermute | solution.py:633
  23.9 27.0 %copy-start.1 = (f32[19,1,1,4096]{3,2,1,0:T(1,128)S(1)}, f32[19,1,1,4096]{3,2,1,0:T(1,128)}, u32[]{:S(2)}) copy-start(f32[19,1,1,4096]{3,2,1,0:T(1,128)} %param.8) | copy-start | bytes 933892
  39.3 1.4 %collective-permute-start.5 = (f32[176,128]{1,0:T(8,128)S(1)}, f32[176,128]{1,0:T(8,128)S(1)}, u32[]{:S(2)}, u32[]{:S(2)}) collective-permute-start(f32[176,128]{1,0:T(8,128)S(1)} %get-tuple-element.37), channel_id=1, source_target_pairs={{0,4},{1,5},{2,6},{3,7},{4,0},{5,1},{6,2},{7,3},{8,12},{9,13},{10,... | collective-permute-start | bytes 270344 | tf_op jit(solution)/shard_map/ppermute | solution.py:633
  39.7 6.4 %collective-permute-start.8 = (f32[104,128]{1,0:T(8,128)S(1)}, f32[104,128]{1,0:T(8,128)S(1)}, u32[]{:S(2)}, u32[]{:S(2)}) collective-permute-start(f32[104,128]{1,0:T(8,128)S(1)} %slice.46), channel_id=1, source_target_pairs={{0,116},{1,117},{2,118},{3,119},{4,16},{5,17},{6,18},{7,19},{8,124... | collective-permute-start | bytes 159752 | tf_op jit(solution)/shard_map/ppermute | solution.py:633
  40.6 6.7 %collective-permute-start.6 = (f32[96,128]{1,0:T(8,128)S(1)}, f32[96,128]{1,0:T(8,128)S(1)}, u32[]{:S(2)}, u32[]{:S(2)}) collective-permute-start(f32[96,128]{1,0:T(8,128)S(1)} %pad_maximum_fusion.3), channel_id=1, source_target_pairs={{0,8},{1,9},{2,10},{3,11},{4,124},{5,125},{6,126},{7,127},{8,16},{... | collective-permute-start | bytes 147464 | tf_op jit(solution)/shard_map/ppermute | solution.py:633
  44.3 3.1 %collective-permute-start.7 = (f32[64,128]{1,0:T(8,128)S(1)}, f32[64,128]{1,0:T(8,128)S(1)}, u32[]{:S(2)}, u32[]{:S(2)}) collective-permute-start(f32[64,128]{1,0:T(8,128)S(1)} %pad_maximum_fusion.5), channel_id=1, source_target_pairs={{0,1},{1,2},{2,3},{3,0},{4,7},{5,4},{6,5},{7,6},{8,9},{9,10},{10,1... | collective-permute-start | bytes 98312 | tf_op jit(solution)/shard_map/ppermute | solution.py:633
  47.4 3.5 %collective-permute-start.9 = (f32[128,128]{1,0:T(8,128)S(1)}, f32[128,128]{1,0:T(8,128)S(1)}, u32[]{:S(2)}, u32[]{:S(2)}) collective-permute-start(f32[128,128]{1,0:T(8,128)S(1)} %pad_maximum_fusion.1), channel_id=1, source_target_pairs={{0,4},{1,5},{2,6},{3,7},{4,0},{5,1},{6,2},{7,3},{8,12},{9,13},{10,... | collective-permute-start | bytes 196616 | tf_op jit(solution)/shard_map/ppermute | solution.py:633
  63.1 2.1 %collective-permute-start.10 = (f32[1152,128]{1,0:T(8,128)S(1)}, f32[1152,128]{1,0:T(8,128)S(1)}, u32[]{:S(2)}, u32[]{:S(2)}) collective-permute-start(f32[1152,128]{1,0:T(8,128)S(1)} %dynamic-slice_bitcast_fusion), channel_id=1, source_target_pairs={{0,4},{1,5},{2,6},{3,7},{4,0},{5,1},{6,2},{7,3},{8,12},{9,13},{10,... | collective-permute-start | bytes 1769480 | tf_op jit(solution)/shard_map/ppermute | solution.py:633
  100.3 5.3 %collective-permute-start.11 = (f32[1152,128]{1,0:T(8,128)S(1)}, f32[1152,128]{1,0:T(8,128)S(1)}, u32[]{:S(2)}, u32[]{:S(2)}) collective-permute-start(f32[1152,128]{1,0:T(8,128)S(1)} %bitcast.22), channel_id=1, source_target_pairs={{0,4},{1,5},{2,6},{3,7},{4,0},{5,1},{6,2},{7,3},{8,12},{9,13},{10,... | collective-permute-start | bytes 1769480 | tf_op jit(solution)/shard_map/ppermute | solution.py:633

commit v7 on v6

--- a/solution.py
+++ b/solution.py
@@ -495,10 +495,10 @@
     copies = Copies(out_sems)
     for step in range(CHUNKS):
         a, b, out = forward(cells_of(f0, step), w_in_t[...], w_mid[...], w_out[...])
-        h0[:, span(step)] = a
-        copies.start(h0.at[:, span(step)], h0_far.at[:, span(step)])
-        h1[:, span(step)] = b
-        copies.start(h1.at[:, span(step)], h1_far.at[:, span(step)])
+        h0[step] = a
+        copies.start(h0.at[step], h0_far.at[step])
+        h1[step] = b
+        copies.start(h1.at[step], h1_far.at[step])
         put_cells(post, step, out)
     send_post(post, xs, sends, z_keep)
     put_z_rows(info, sends, z_keep)
@@ -543,7 +543,7 @@
     copies = Copies(sems)
     for step in range(CHUNKS):
         for hbm, near in ((h1_far, h1), (h0_far, h0)):
-            copies.start(hbm.at[:, span(step)], near.at[:, span(step)])
+            copies.start(hbm.at[step], near.at[:, span(step)])
     copies.start(grads2_far, grads)
     pbar[...] = local1[...]
     take_back(info, pbar, (swapped, x_got, z_got, far, passed), x_four, y_two)
@@ -672,7 +672,8 @@
     w_mid_t = w_mid.T
     place = lax.axis_index(BLOCKS).astype(jnp.int32).reshape(1)
     tables = [place, face_source.T, face_level[0], face_quadrant[0]]
-    hidden = pltpu.HBM(HIDDEN, BF16)
+    hidden = pltpu.HBM((CHUNKS, HID, CHUNK), BF16)
+    by_chunk = pltpu.VMEM((CHUNKS, HID, CHUNK), BF16)
     thin = jax.ShapeDtypeStruct(THIN, BF16)
     grad = (GROWS, 128)
     near = pltpu.VMEM(HIDDEN, BF16)
@@ -685,7 +686,7 @@
         [pltpu.SMEM((4, NB), jnp.int32), pltpu.SMEM((1, 6), jnp.int32),
          pltpu.SMEM((1, 6), jnp.int32), X_TWO,
          BLOCK, BLOCK, pltpu.VMEM((Q, HID), BF16), pltpu.VMEM((HID, HID), BF16),
-         pltpu.VMEM((Q, HID), BF16), near, near, BLOCK, *FACES[1:], FACES[2], sems((8,)),
+         pltpu.VMEM((Q, HID), BF16), by_chunk, by_chunk, BLOCK, *FACES[1:], FACES[2], sems((8,)),
          sems((2 * CHUNKS,))],
         4000, 32, range(8),
     )

time: 107 us -> 107 us (level)
  no operation moved by 1% of the time
where the time goes in v7:
time: 107 us; the launch traced here: 106 us
  Pallas kernels  37.6 us (35%)
  blocking collectives  34.3 us (32%)
  starting transfers between devices  26.2 us (24%)
  waiting for transfers between devices  6.41 us (6%)
    pallas_call x6, Pallas kernels, run(): pl.pallas_call(kernel, out_shape=[shape(s) for s in outs], in_specs=in_sp...  37.6 us
    ppermute x12, starting transfers between devices, send(): return lax.ppermute(value, AXES, pairs)  26.2 us
    all_to_all x1, blocking collectives, total_over_devices(): lax.all_to_all(mine, CHIPS, 0, 0, tiled=True).sum(axis=0, keepdims=True)  18.4 us
    all_to_all x1, blocking collectives, total_over_devices(): mine = lax.all_to_all(mine, CHIPS, 0, 0, tiled=True).reshape(HALF, 128)  15.9 us
    ppermute x12, waiting for transfers between devices, send(): return lax.ppermute(value, AXES, pairs)  6.41 us
  transfers between devices with their start and end apart: 12, of which 6 were waited for; matrix products, arithmetic and copies ran while one was open for 0% of the time, Pallas kernels for 2%

profile of v7, /device:TPU:1, one launch (start us, length us, event | category | flops | bytes accessed | tf_op | source)
XLA Modules:
  0.0 106.4 jit_solution(1309925629655582762)
XLA Ops:
  0.7 7.0 %shard_map.119 = (f32[19,32,128]{2,1,0:T(8,128)S(1)}, f32[19,32,128]{2,1,0:T(8,128)S(1)}, f32[176,128]{1,0:T(8,128)S(1)}, bf16[4,512,1024]{2,1,0:T(8,128)(2,1)}, bf16[4,512,1024]{2,1,0:T(8,128)(2,1)}) custom-call(s32[1]{0:T(128)} %bitcast.place, s32[4,32]{1,0:T(4,128)} %bitcast.33, s32[1,6]{1,0:T(1,128)} %bitcast.37, s32[1,6]{1,0:T(1,128)} %bitcast.41, ...), custom_call_target="tpu_custom_call" | custom-call | flops 4000000000 | bytes 1048576 | tf_op jit(solution)/shard_map/pallas_call | solution.py:613
  7.6 0.0 copy-start.4
  7.7 0.0 copy-start.5
  7.7 1.5 %collective-permute-start = (f32[176,128]{1,0:T(8,128)S(1)}, f32[176,128]{1,0:T(8,128)S(1)}, u32[]{:S(2)}, u32[]{:S(2)}) collective-permute-start(f32[176,128]{1,0:T(8,128)S(1)} %get-tuple-element.31), channel_id=1, source_target_pairs={{0,4},{1,5},{2,6},{3,7},{4,0},{5,1},{6,2},{7,3},{8,12},{9,13},{10,... | collective-permute-start | bytes 270344 | tf_op jit(solution)/shard_map/ppermute | solution.py:633
  9.2 3.0 %collective-permute-start.3 = (f32[104,128]{1,0:T(8,128)S(1)}, f32[104,128]{1,0:T(8,128)S(1)}, u32[]{:S(2)}, u32[]{:S(2)}) collective-permute-start(f32[104,128]{1,0:T(8,128)S(1)} %slice.40), channel_id=1, source_target_pairs={{0,116},{1,117},{2,118},{3,119},{4,16},{5,17},{6,18},{7,19},{8,124... | collective-permute-start | bytes 159752 | tf_op jit(solution)/shard_map/ppermute | solution.py:633
  12.2 3.0 %collective-permute-start.1 = (f32[96,128]{1,0:T(8,128)S(1)}, f32[96,128]{1,0:T(8,128)S(1)}, u32[]{:S(2)}, u32[]{:S(2)}) collective-permute-start(f32[96,128]{1,0:T(8,128)S(1)} %pad_maximum_fusion.2), channel_id=1, source_target_pairs={{0,8},{1,9},{2,10},{3,11},{4,124},{5,125},{6,126},{7,127},{8,16},{... | collective-permute-start | bytes 147464 | tf_op jit(solution)/shard_map/ppermute | solution.py:633
  15.2 3.8 %collective-permute-start.2 = (f32[64,128]{1,0:T(8,128)S(1)}, f32[64,128]{1,0:T(8,128)S(1)}, u32[]{:S(2)}, u32[]{:S(2)}) collective-permute-start(f32[64,128]{1,0:T(8,128)S(1)} %pad_maximum_fusion.4), channel_id=1, source_target_pairs={{0,1},{1,2},{2,3},{3,0},{4,7},{5,4},{6,5},{7,6},{8,9},{9,10},{10,1... | collective-permute-start | bytes 98312 | tf_op jit(solution)/shard_map/ppermute | solution.py:633
  19.0 1.0 collective-permute-done.2.z_got
  20.0 2.6 %collective-permute-start.4 = (f32[128,128]{1,0:T(8,128)S(1)}, f32[128,128]{1,0:T(8,128)S(1)}, u32[]{:S(2)}, u32[]{:S(2)}) collective-permute-start(f32[128,128]{1,0:T(8,128)S(1)} %pad_maximum_fusion), channel_id=1, source_target_pairs={{0,4},{1,5},{2,6},{3,7},{4,0},{5,1},{6,2},{7,3},{8,12},{9,13},{10,... | collective-permute-start | bytes 196616 | tf_op jit(solution)/shard_map/ppermute | solution.py:633
  22.6 0.2 copy.23
  22.8 0.7 collective-permute-done.4.passed
  23.5 0.0 copy-start.1
  23.5 15.4 %shard_map.120 = (f32[19,32,128]{2,1,0:T(8,128)S(1)}, f32[19,32,128]{2,1,0:T(8,128)S(1)}, f32[176,128]{1,0:T(8,128)S(1)}, f32[2304,128]{1,0:T(8,128)}) custom-call(s32[1]{0:T(128)} %bitcast.place, s32[4,32]{1,0:T(4,128)S(1)} %bitcast.34, s32[1,6]{1,0:T(1,128)S(1)} %bitcast.38, s32[1,6]{1,0:T(1,128)S(1)} %bitcast.42, ...), custom_call_target="tpu_custom_call" | custom-call | flops 14000000000 | bytes 1048576 | tf_op jit(solution)/shard_map/pallas_call | solution.py:613
  38.9 0.4 collective-permute-start.5
  39.3 0.1 collective-permute-start.8
  39.4 0.8 collective-permute-done.5.swapped
  40.3 3.7 %collective-permute-start.6 = (f32[96,128]{1,0:T(8,128)S(1)}, f32[96,128]{1,0:T(8,128)S(1)}, u32[]{:S(2)}, u32[]{:S(2)}) collective-permute-start(f32[96,128]{1,0:T(8,128)S(1)} %pad_maximum_fusion.3), channel_id=1, source_target_pairs={{0,8},{1,9},{2,10},{3,11},{4,124},{5,125},{6,126},{7,127},{8,16},{... | collective-permute-start | bytes 147464 | tf_op jit(solution)/shard_map/ppermute | solution.py:633
  43.9 1.7 %collective-permute-start.7 = (f32[64,128]{1,0:T(8,128)S(1)}, f32[64,128]{1,0:T(8,128)S(1)}, u32[]{:S(2)}, u32[]{:S(2)}) collective-permute-start(f32[64,128]{1,0:T(8,128)S(1)} %pad_maximum_fusion.5), channel_id=1, source_target_pairs={{0,1},{1,2},{2,3},{3,0},{4,7},{5,4},{6,5},{7,6},{8,9},{9,10},{10,1... | collective-permute-start | bytes 98312 | tf_op jit(solution)/shard_map/ppermute | solution.py:633
  45.7 1.3 %collective-permute-done.7.z_got = f32[64,128]{1,0:T(8,128)S(1)} collective-permute-done((f32[64,128]{1,0:T(8,128)S(1)}, f32[64,128]{1,0:T(8,128)S(1)}, u32[]{:S(2)}, u32[]{:S(2)}) %collective-permute-start.7) | collective-permute-done | bytes 32800 | tf_op jit(solution)/shard_map/ppermute | solution.py:633
  47.0 2.6 %collective-permute-start.9 = (f32[128,128]{1,0:T(8,128)S(1)}, f32[128,128]{1,0:T(8,128)S(1)}, u32[]{:S(2)}, u32[]{:S(2)}) collective-permute-start(f32[128,128]{1,0:T(8,128)S(1)} %pad_maximum_fusion.1), channel_id=1, source_target_pairs={{0,4},{1,5},{2,6},{3,7},{4,0},{5,1},{6,2},{7,3},{8,12},{9,13},{10,... | collective-permute-start | bytes 196616 | tf_op jit(solution)/shard_map/ppermute | solution.py:633
  49.6 0.9 collective-permute-done.9.passed
  50.5 12.2 %shard_map.121 = (f32[2304,128]{1,0:T(8,128)S(1)}, f32[19,32,128]{2,1,0:T(8,128)}) custom-call(s32[1]{0:T(128)} %bitcast.place, s32[4,32]{1,0:T(4,128)S(1)} %bitcast.35, s32[1,6]{1,0:T(1,128)S(1)} %bitcast.39, s32[1,6]{1,0:T(1,128)S(1)} %bitcast.43, f32[19,32,128]{2,1,0:T(8,128)S(1)} %bitcast.29, f32[19,32,128]{2,1,0:T(8,128)S(1)} %get-tuple-element.36.local1, ...), custom_call_target="tpu_custom_call" | custom-call | flops 8000000000 | bytes 1048576 | tf_op jit(solution)/shard_map/pallas_call | solution.py:613
  62.8 0.4 collective-permute-start.10
  63.2 1.6 %collective-permute-done.10.arrived = f32[1152,128]{1,0:T(8,128)S(1)} collective-permute-done((f32[1152,128]{1,0:T(8,128)S(1)}, f32[1152,128]{1,0:T(8,128)S(1)}, u32[]{:S(2)}, u32[]{:S(2)}) %collective-permute-start.10) | collective-permute-done | bytes 589856 | tf_op jit(solution)/shard_map/ppermute | solution.py:633
  64.9 0.1 shard_map.122
  64.9 18.4 %all_to_all.10 = f32[64,1,2304]{2,1,0:T(1,128)S(1)} all-to-all(f32[64,1,2304]{2,1,0:T(1,128)S(1)} %bitcast.21), channel_id=1, replica_groups=mesh['bx'=4,'by'=4,'core'=2,'slab'=4] {'bx','by','slab'}, dimensions={0} | all-to-all | bytes 1179648 | tf_op jit(solution)/shard_map/all_to_all | solution.py:660
  83.3 0.4 reduce_sum.9
  83.7 0.3 broadcast_in_dim.4
  84.0 15.9 %all_to_all.11 = f32[64,1,2304]{2,1,0:T(1,128)S(1)} all-to-all(f32[64,1,2304]{2,1,0:T(1,128)S(1)} %broadcast_in_dim.4), channel_id=1, replica_groups=mesh['bx'=4,'by'=4,'core'=2,'slab'=4] {'bx','by','slab'}, dimensions={0} | all-to-all | bytes 1179648 | tf_op jit(solution)/shard_map/all_to_all | solution.py:662
  99.9 3.5 %collective-permute-start.11 = (f32[1152,128]{1,0:T(8,128)S(1)}, f32[1152,128]{1,0:T(8,128)S(1)}, u32[]{:S(2)}, u32[]{:S(2)}) collective-permute-start(f32[1152,128]{1,0:T(8,128)S(1)} %bitcast.22), channel_id=1, source_target_pairs={{0,4},{1,5},{2,6},{3,7},{4,0},{5,1},{6,2},{7,3},{8,12},{9,13},{10,... | collective-permute-start | bytes 1769480 | tf_op jit(solution)/shard_map/ppermute | solution.py:633
  103.5 1.7 %shard_map.123 = f32[19,32,128]{2,1,0:T(8,128)} custom-call(s32[1]{0:T(128)} %bitcast.place, s32[4,32]{1,0:T(4,128)S(1)} %bitcast.36, s32[1,6]{1,0:T(1,128)S(1)} %bitcast.40, s32[1,6]{1,0:T(1,128)S(1)} %bitcast.44, f32[19,32,128]{2,1,0:T(8,128)S(1)} %get-tuple-element.46.post2, f32[176,128]{1,0:T(8,128)S(1)} %collective-permute-done.5.swapped, ...), custom_call_target="tpu_custom_call" | custom-call | flops 500000000 | bytes 1048576 | tf_op jit(solution)/shard_map/pallas_call | solution.py:613
  105.2 1.2 %shard_map.124 = (f32[19,512]{1,0:T(8,128)}, f32[512,512]{1,0:T(8,128)}, f32[19,512]{1,0:T(8,128)}) custom-call(s32[1]{0:T(128)} %bitcast.place, f32[1152,128]{1,0:T(8,128)S(1)} %bitcast.23, f32[1152,128]{1,0:T(8,128)S(1)} %collective-permute-done.11.other), custom_call_target="tpu_custom_call" | custom-call | flops 10000000 | bytes 1048576 | tf_op jit(solution)/shard_map/pallas_call | solution.py:613
  (36 shorter events, 0.2 us)
Async XLA Ops:
  0.6 21.9 %copy-start = (bf16[1,512,512]{2,1,0:T(8,128)(2,1)S(1)}, bf16[1,512,512]{2,1,0:T(8,128)(2,1)}, u32[]{:S(2)}) copy-start(bf16[1,512,512]{2,1,0:T(8,128)(2,1)} %param.10) | copy-start | bytes 1572868
  7.6 15.8 %copy-start.2 = (bf16[512,19]{0,1:T(8,128)(2,1)S(1)}, bf16[512,19]{0,1:T(8,128)(2,1)}, u32[]{:S(2)}) copy-start(bf16[512,19]{0,1:T(8,128)(2,1)} %param.9) | copy-start | bytes 58372
  7.6 15.8 %copy-start.3 = (bf16[19,512]{1,0:T(8,128)(2,1)S(1)}, bf16[19,512]{1,0:T(8,128)(2,1)}, u32[]{:S(2)}) copy-start(bf16[19,512]{1,0:T(8,128)(2,1)} %w_out.3) | copy-start | bytes 58372
  7.6 15.8 %copy-start.4 = (s32[32,4]{0,1:T(4,128)S(1)}, s32[32,4]{0,1:T(4,128)}, u32[]{:S(2)}) copy-start(s32[32,4]{0,1:T(4,128)} %param.13) | copy-start | bytes 1540
  7.7 15.8 %copy-start.5 = (s32[1,1,6]{2,1,0:T(1,128)S(1)}, s32[1,1,6]{2,1,0:T(1,128)}, u32[]{:S(2)}) copy-start(s32[1,1,6]{2,1,0:T(1,128)} %param.14) | copy-start | bytes 76
  7.7 15.8 %copy-start.6 = (s32[1,1,6]{2,1,0:T(1,128)S(1)}, s32[1,1,6]{2,1,0:T(1,128)}, u32[]{:S(2)}) copy-start(s32[1,1,6]{2,1,0:T(1,128)} %param.15) | copy-start | bytes 76
  7.7 4.5 %collective-permute-start = (f32[176,128]{1,0:T(8,128)S(1)}, f32[176,128]{1,0:T(8,128)S(1)}, u32[]{:S(2)}, u32[]{:S(2)}) collective-permute-start(f32[176,128]{1,0:T(8,128)S(1)} %get-tuple-element.31), channel_id=1, source_target_pairs={{0,4},{1,5},{2,6},{3,7},{4,0},{5,1},{6,2},{7,3},{8,12},{9,13},{10,... | collective-permute-start | bytes 270344 | tf_op jit(solution)/shard_map/ppermute | solution.py:633
  9.2 9.8 %collective-permute-start.3 = (f32[104,128]{1,0:T(8,128)S(1)}, f32[104,128]{1,0:T(8,128)S(1)}, u32[]{:S(2)}, u32[]{:S(2)}) collective-permute-start(f32[104,128]{1,0:T(8,128)S(1)} %slice.40), channel_id=1, source_target_pairs={{0,116},{1,117},{2,118},{3,119},{4,16},{5,17},{6,18},{7,19},{8,124... | collective-permute-start | bytes 159752 | tf_op jit(solution)/shard_map/ppermute | solution.py:633
  12.2 7.8 %collective-permute-start.1 = (f32[96,128]{1,0:T(8,128)S(1)}, f32[96,128]{1,0:T(8,128)S(1)}, u32[]{:S(2)}, u32[]{:S(2)}) collective-permute-start(f32[96,128]{1,0:T(8,128)S(1)} %pad_maximum_fusion.2), channel_id=1, source_target_pairs={{0,8},{1,9},{2,10},{3,11},{4,124},{5,125},{6,126},{7,127},{8,16},{... | collective-permute-start | bytes 147464 | tf_op jit(solution)/shard_map/ppermute | solution.py:633
  15.2 4.8 %collective-permute-start.2 = (f32[64,128]{1,0:T(8,128)S(1)}, f32[64,128]{1,0:T(8,128)S(1)}, u32[]{:S(2)}, u32[]{:S(2)}) collective-permute-start(f32[64,128]{1,0:T(8,128)S(1)} %pad_maximum_fusion.4), channel_id=1, source_target_pairs={{0,1},{1,2},{2,3},{3,0},{4,7},{5,4},{6,5},{7,6},{8,9},{9,10},{10,1... | collective-permute-start | bytes 98312 | tf_op jit(solution)/shard_map/ppermute | solution.py:633
  20.0 3.5 %collective-permute-start.4 = (f32[128,128]{1,0:T(8,128)S(1)}, f32[128,128]{1,0:T(8,128)S(1)}, u32[]{:S(2)}, u32[]{:S(2)}) collective-permute-start(f32[128,128]{1,0:T(8,128)S(1)} %pad_maximum_fusion), channel_id=1, source_target_pairs={{0,4},{1,5},{2,6},{3,7},{4,0},{5,1},{6,2},{7,3},{8,12},{9,13},{10,... | collective-permute-start | bytes 196616 | tf_op jit(solution)/shard_map/ppermute | solution.py:633
  23.5 27.0 %copy-start.1 = (f32[19,1,1,4096]{3,2,1,0:T(1,128)S(1)}, f32[19,1,1,4096]{3,2,1,0:T(1,128)}, u32[]{:S(2)}) copy-start(f32[19,1,1,4096]{3,2,1,0:T(1,128)} %param.8) | copy-start | bytes 933892
  38.9 1.4 %collective-permute-start.5 = (f32[176,128]{1,0:T(8,128)S(1)}, f32[176,128]{1,0:T(8,128)S(1)}, u32[]{:S(2)}, u32[]{:S(2)}) collective-permute-start(f32[176,128]{1,0:T(8,128)S(1)} %get-tuple-element.37), channel_id=1, source_target_pairs={{0,4},{1,5},{2,6},{3,7},{4,0},{5,1},{6,2},{7,3},{8,12},{9,13},{10,... | collective-permute-start | bytes 270344 | tf_op jit(solution)/shard_map/ppermute | solution.py:633
  39.3 6.4 %collective-permute-start.8 = (f32[104,128]{1,0:T(8,128)S(1)}, f32[104,128]{1,0:T(8,128)S(1)}, u32[]{:S(2)}, u32[]{:S(2)}) collective-permute-start(f32[104,128]{1,0:T(8,128)S(1)} %slice.46), channel_id=1, source_target_pairs={{0,116},{1,117},{2,118},{3,119},{4,16},{5,17},{6,18},{7,19},{8,124... | collective-permute-start | bytes 159752 | tf_op jit(solution)/shard_map/ppermute | solution.py:633
  40.3 6.7 %collective-permute-start.6 = (f32[96,128]{1,0:T(8,128)S(1)}, f32[96,128]{1,0:T(8,128)S(1)}, u32[]{:S(2)}, u32[]{:S(2)}) collective-permute-start(f32[96,128]{1,0:T(8,128)S(1)} %pad_maximum_fusion.3), channel_id=1, source_target_pairs={{0,8},{1,9},{2,10},{3,11},{4,124},{5,125},{6,126},{7,127},{8,16},{... | collective-permute-start | bytes 147464 | tf_op jit(solution)/shard_map/ppermute | solution.py:633
  43.9 3.1 %collective-permute-start.7 = (f32[64,128]{1,0:T(8,128)S(1)}, f32[64,128]{1,0:T(8,128)S(1)}, u32[]{:S(2)}, u32[]{:S(2)}) collective-permute-start(f32[64,128]{1,0:T(8,128)S(1)} %pad_maximum_fusion.5), channel_id=1, source_target_pairs={{0,1},{1,2},{2,3},{3,0},{4,7},{5,4},{6,5},{7,6},{8,9},{9,10},{10,1... | collective-permute-start | bytes 98312 | tf_op jit(solution)/shard_map/ppermute | solution.py:633
  47.0 3.5 %collective-permute-start.9 = (f32[128,128]{1,0:T(8,128)S(1)}, f32[128,128]{1,0:T(8,128)S(1)}, u32[]{:S(2)}, u32[]{:S(2)}) collective-permute-start(f32[128,128]{1,0:T(8,128)S(1)} %pad_maximum_fusion.1), channel_id=1, source_target_pairs={{0,4},{1,5},{2,6},{3,7},{4,0},{5,1},{6,2},{7,3},{8,12},{9,13},{10,... | collective-permute-start | bytes 196616 | tf_op jit(solution)/shard_map/ppermute | solution.py:633
  62.8 2.1 %collective-permute-start.10 = (f32[1152,128]{1,0:T(8,128)S(1)}, f32[1152,128]{1,0:T(8,128)S(1)}, u32[]{:S(2)}, u32[]{:S(2)}) collective-permute-start(f32[1152,128]{1,0:T(8,128)S(1)} %dynamic-slice_bitcast_fusion), channel_id=1, source_target_pairs={{0,4},{1,5},{2,6},{3,7},{4,0},{5,1},{6,2},{7,3},{8,12},{9,13},{10,... | collective-permute-start | bytes 1769480 | tf_op jit(solution)/shard_map/ppermute | solution.py:633
  99.9 5.3 %collective-permute-start.11 = (f32[1152,128]{1,0:T(8,128)S(1)}, f32[1152,128]{1,0:T(8,128)S(1)}, u32[]{:S(2)}, u32[]{:S(2)}) collective-permute-start(f32[1152,128]{1,0:T(8,128)S(1)} %bitcast.22), channel_id=1, source_target_pairs={{0,4},{1,5},{2,6},{3,7},{4,0},{5,1},{6,2},{7,3},{8,12},{9,13},{10,... | collective-permute-start | bytes 1769480 | tf_op jit(solution)/shard_map/ppermute | solution.py:633
